TPU v7x, 32 devices: a whole 2x2x4 slice. The times are simulated.
32 devices in a mesh: gx: 4 (over z), gy: 8 (over y, x, core).
Axes of the slice: x: 2, y: 2, z: 4, core: 2. Of those that a mesh axis runs over, the one named last changes fastest.
Arguments:
- feats: bfloat16 [96, 4, 128, 512], P(None, 'gx', 'gy'), may hold values from -6 to 6
- cotangent: bfloat16 [96, 4, 128, 512], P(None, 'gx', 'gy'), may hold values from -6 to 6
- weight: bfloat16 [96, 2592], replicated, may hold values from -0.125 to 0.125
- cell_slot: int32 [4, 288], P('gx', 'gy'), may hold values from 0 to 16, as said below
- neighbours: int32 [4, 128, 8], P('gx', 'gy'), may hold values from 0 to 44, as said below
- counts: int32 [4, 8], P('gx', 'gy'), may hold values from 2 to 16, as said below
Outputs:
- output: bfloat16 [96, 4, 128, 512], P(None, 'gx', 'gy')
- grad_feats: bfloat16 [96, 4, 128, 512], P(None, 'gx', 'gy')
- grad_weight: float32 [96, 2592], replicated
Inputs may be any that keep to these rules, and one draw needn't show every extreme that they name: `cell_slot`: on each device the live slots are 0 to counts-1, each sits at exactly one tile position, in increasing order of position a*6+b; empty positions hold 16; some device has all 16 slots live. neighbours[i, j, s, k] is the source-table index of the live brick at the city position one step in direction k from slot s, or 45 - 1 (the zero brick) where no live brick is there or s is not live. Neighbours in the same tile are given by their slot; the others by their halo entry. `counts`: devices differ in load; the busiest holds 16 live bricks.
All inputs are finite; a program needn't handle non-finite values.
Results may differ from a plain program's by a relative error of at most 0.0022.
The roundings to bfloat16 on the way count: a program that leaves them out, or rounds other values in their place, can miss the bound.
Values may be sent and summed in bfloat16 or wider, within the bound.
No kernel may reach another device: no remote copies, remote signals or barrier semaphores. Data moves between devices by JAX's collectives and lax.ppermute only.
A program may use at most 128 MiB of HBM per device.

v0:
```python
import functools
import math

import jax
import jax.numpy as jnp
from jax import lax
from jax.experimental import pallas as pl
from jax.experimental.pallas import tpu as pltpu
from jax.sharding import PartitionSpec as P

BF = jnp.bfloat16
F32 = jnp.float32
VMEM = pl.BlockSpec(memory_space=pltpu.VMEM)
SMEM = pl.BlockSpec(memory_space=pltpu.SMEM)
LANES = 128
HALF = 64
ROWS = 2048


def passed_along(block, axis, distance):
    devices = range(lax.axis_size(axis))
    route = [((i - distance) % len(devices), i) for i in devices]
    return lax.ppermute(block, axis, route)


def from_behind(block, axis, distance):
    devices = range(lax.axis_size(axis))
    route = [(i - distance, i) for i in devices if i - distance in devices]
    return lax.ppermute(block, axis, route)


def lane_ids(channels):
    return lax.broadcasted_iota(jnp.int32, (channels, LANES), 1)


def turn(value, amount):
    return pltpu.roll(value, amount, 1)


def nothing(value):
    return jnp.zeros_like(value)


def load_pairs(source, staging, target):
    channels, slots, _ = source.shape
    low = lane_ids(channels) < HALF
    for tile in range(4):
        piece = source[:, :, tile * LANES : (tile + 1) * LANES].astype(F32)
        staging[tile] = piece.reshape(channels * slots, LANES)

    def body(pair, carry):
        for tile in range(4):
            first = staging[tile, pl.ds(2 * pair, channels, stride=slots), :].astype(BF)
            second = staging[tile, pl.ds(2 * pair + 1, channels, stride=slots), :].astype(BF)
            target[pair, 2 * tile] = jnp.where(low, first, turn(second, HALF))
            target[pair, 2 * tile + 1] = jnp.where(low, turn(first, HALF), second)
        return carry

    lax.fori_loop(0, slots // 2, body, 0)


def edge_rows(cells, field, low_out, high_out, slots, side):
    channels = field.shape[2]
    low = lane_ids(channels) < HALF
    for out, line, layer in ((low_out, 0, 0), (high_out, side - 1, 7)):
        for tile in range(side // 2):
            parts = []
            for part in range(2):
                slot = cells[line * side + 2 * tile + part]
                row = field[jnp.minimum(slot, slots - 1) // 2, layer]
                row = turn(row, (part + slot) % 2 * HALF)
                parts.append(jnp.where(slot < slots, row, nothing(row)))
            out[tile] = jnp.where(low, parts[0], parts[1])


def prepare_kernel(cells, feats, pairs, low_out, high_out, staging, *, side):
    load_pairs(feats, staging, pairs)
    edge_rows(cells, pairs, low_out, high_out, feats.shape[1], side)


def regroup_kernel(source, pairs, staging):
    load_pairs(source, staging, pairs)


def column_kernel(cells, field, below, above, low_out, high_out, *, side):
    channels = field.shape[2]
    slots = 2 * field.shape[0]
    lanes = lane_ids(channels)
    for out, line, place in ((low_out, 0, 0), (high_out, side - 1, 56)):
        corner = line % 2 * HALF + place
        for quarter in range(4):
            total = jnp.zeros((channels, LANES), BF)
            for half in range(2):
                layer = quarter + 4 * half
                for u in range(1, side + 1):
                    slot = cells[(u - 1) * side + line]
                    row = field[jnp.minimum(slot, slots - 1) // 2, layer]
                    goal = half * HALF + u * 8
                    row = turn(row, (goal - place + LANES - slot % 2 * HALF) % LANES)
                    row = jnp.where(slot < slots, row, nothing(row))
                    total = jnp.where(lanes // 8 == goal // 8, row, total)
                if layer == 7:
                    goal = half * HALF
                    row = turn(below[line // 2], (goal - corner) % LANES)
                    total = jnp.where(lanes // 8 == goal // 8, row, total)
                if layer == 0:
                    goal = half * HALF + (side + 1) * 8
                    row = turn(above[line // 2], (goal - corner) % LANES)
                    total = jnp.where(lanes // 8 == goal // 8, row, total)
            out[quarter] = total


def fill_table(table, field, below_x, above_x, below_y, above_y):
    pairs, _, channels, _ = field.shape
    low = lane_ids(channels) < HALF

    def body(pair, carry):
        table[pair] = field[pair]
        return carry

    lax.fori_loop(0, pairs, body, 0)
    for quarter in range(4):
        below, above = below_y[quarter], above_y[quarter]
        table[pairs, quarter] = jnp.where(low, below, turn(above, HALF))
        table[pairs, quarter + 4] = jnp.where(low, turn(below, HALF), above)
    tiles = below_x.shape[0]
    for tile in range(tiles):
        table[pairs + 1 + tile, 7] = below_x[tile]
        table[pairs + 1 + tile, 0] = above_x[tile]
    table[pairs + 1 + tiles] = jnp.zeros(table.shape[1:], BF)


def locate(index, pairs, side, column):
    slots = 2 * pairs
    tiles = side // 2
    wide = side + 2
    place = 0 if column is None else column * 8
    own = index < slots
    row = index < slots + 2 * side
    below = index < slots + side
    ordinal = jnp.where(own, index, index - slots - jnp.where(below, 0, side))
    base = jnp.where(own, 0, pairs + 1)
    tile_row = base + ordinal // 2
    lane_row = ordinal % 2 * HALF + place
    last = index >= slots + 2 * side + 2 * wide
    u = index - slots - 2 * side
    lane_column = jnp.where(u < wide, u * 8, HALF + (u - wide) * 8)
    tile = jnp.where(row, tile_row, jnp.where(last, pairs + 1 + tiles, pairs))
    lane = jnp.where(row, lane_row, jnp.where(last, 0, lane_column))
    return tile, lane


def build_columns(group, links, table, columns, pairs, side):
    channels = table.shape[2]
    lanes = lane_ids(channels)
    low = lanes < HALF
    y_first = lanes % HALF < 8
    y_last = lanes % HALF >= 56
    z_first = lanes % 8 == 0
    z_last = lanes % 8 == 7
    spots = {}
    for h in range(2):
        for part in range(2):
            slot = group * 4 + 2 * h + part
            for k, (dx, dy) in enumerate(
                ((-1, -1), (-1, 0), (-1, 1), (0, -1), (0, 1), (1, -1), (1, 0), (1, 1))
            ):
                column = {-1: 7, 0: None, 1: 0}[dy]
                goal = part * HALF + (56 if dy == 1 else 0)
                tile, lane = locate(links[slot * 8 + k], pairs, side, column)
                spots[h, part, dx, dy] = tile, (goal + LANES - lane) % LANES

    def fetch(layer, h, dx, dy):
        rows = []
        for part in range(2):
            tile, amount = spots[h, part, dx, dy]
            rows.append(turn(table[tile, layer], amount))
        return jnp.where(low, rows[0], rows[1])

    def layer_of(xp, layer, dx):
        for h in range(2):
            if dx == 0:
                middle = table[group * 2 + h, layer]
            else:
                middle = fetch(layer, h, dx, 0)
            before = jnp.where(y_first, fetch(layer, h, dx, -1), turn(middle, 8))
            after = jnp.where(y_last, fetch(layer, h, dx, 1), turn(middle, LANES - 8))
            at = pl.multiple_of(xp * 2 * LANES + h * LANES, LANES)
            for b, value in enumerate((before, middle, after)):
                lower = jnp.where(z_first, nothing(value), turn(value, 1))
                upper = jnp.where(z_last, nothing(value), turn(value, LANES - 1))
                for c, shifted in enumerate((lower, value, upper)):
                    start = (b * 3 + c) * channels
                    columns[start : start + channels, pl.ds(at, LANES)] = shifted

    layer_of(0, 7, -1)

    def body(xp, carry):
        layer_of(xp, xp - 1, 0)
        return carry

    lax.fori_loop(1, 9, body, 0)
    layer_of(9, 0, 1)


def product(left, right, contract):
    return lax.dot_general(left, right, (contract, ((), ())), preferred_element_type=F32)


def convolve_group(matrix, columns, carry_ref, finish):
    channels = matrix.shape[0] // 3
    width = 2 * LANES
    for step in range(5):
        part = product(
            matrix[...], columns[:, step * 2 * width : (step + 1) * 2 * width], ((1,), (0,))
        )
        first, second, third = (part[a * channels : (a + 1) * channels] for a in range(3))
        if step > 0:
            left = carry_ref[:, :width] + third[:, :width]
            right = carry_ref[:, width:] + (second[:, :width] + third[:, width:])
            finish(step - 1, left, right)
        if step < 4:
            carry_ref[:, :width] = first[:, :width] + second[:, width:]
            carry_ref[:, width:] = first[:, width:]


def store_slots(staging, t, pair, slots, even, odd):
    channels = even.shape[0]
    low = lane_ids(channels) < HALF
    first = jnp.where(low, even, turn(odd, HALF))
    second = jnp.where(low, turn(even, HALF), odd)
    staging[t, pl.ds(2 * pair, channels, stride=slots), :] = first.astype(F32)
    staging[t, pl.ds(2 * pair + 1, channels, stride=slots), :] = second.astype(F32)


def write_out(staging, out):
    channels, slots, _ = out.shape
    for tile in range(4):
        out[:, :, tile * LANES : (tile + 1) * LANES] = (
            staging[tile].reshape(channels, slots, LANES).astype(BF)
        )


def forward_kernel(
    cells, links, counts, field, below_x, above_x, below_y, above_y, upstream, matrix,
    out, grad, terms, low_out, high_out,
    table, columns, shifted, carry_ref, total, staging, *, side,
):
    pairs, _, channels, _ = field.shape
    slots = 2 * pairs
    fill_table(table, field, below_x, above_x, below_y, above_y)
    total[...] = jnp.zeros(total.shape, F32)
    shifted[...] = jnp.zeros(shifted.shape, BF)
    upper = (lane_ids(channels) >= HALF).astype(jnp.int32)

    def body(group, carry):
        build_columns(group, links, table, columns, pairs, side)

        def finish(t, left, right):
            for h in range(2):
                pair = group * 2 + h
                live = 2 * pair + upper < counts[0]
                results = []
                for odd, hidden in ((0, left), (1, right)):
                    x = 2 * t + odd
                    hidden = hidden[:, h * LANES : (h + 1) * LANES]
                    gate = jax.nn.sigmoid(hidden)
                    inputs = field[pair, x].astype(F32)
                    gradient = upstream[pair, x].astype(F32)
                    result = jnp.where(live, inputs + hidden * gate, 0.0)
                    results.append(result.astype(BF))
                    gradient = gradient * gate * (1.0 + hidden * (1.0 - gate))
                    gradient = jnp.where(live, gradient, 0.0).astype(BF)
                    grad[pair, x] = gradient
                    for a in range(3):
                        at = (x + a) * 2 * LANES + h * LANES
                        shifted[a * channels : (a + 1) * channels, at : at + LANES] = gradient
                store_slots(staging, t, pair, slots, *results)

        convolve_group(matrix, columns, carry_ref, finish)
        total[...] += product(shifted[...], columns[...], ((1,), (1,)))
        return carry

    lax.fori_loop(0, pairs // 2, body, 0)
    height, width = total.shape
    terms[...] = jnp.zeros(terms.shape, F32)
    for tile in range(-(-width // LANES)):
        end = min(width, (tile + 1) * LANES)
        terms[tile * height : (tile + 1) * height, : end - tile * LANES] = total[
            :, tile * LANES : end
        ]
    edge_rows(cells, grad, low_out, high_out, slots, side)
    write_out(staging, out)


def backward_kernel(
    links, counts, field, below_x, above_x, below_y, above_y, upstream, matrix,
    out, table, columns, carry_ref, staging, *, side,
):
    pairs, _, channels, _ = field.shape
    slots = 2 * pairs
    fill_table(table, field, below_x, above_x, below_y, above_y)
    upper = (lane_ids(channels) >= HALF).astype(jnp.int32)

    def body(group, carry):
        build_columns(group, links, table, columns, pairs, side)

        def finish(t, left, right):
            for h in range(2):
                pair = group * 2 + h
                live = 2 * pair + upper < counts[0]
                results = []
                for odd, back in ((0, left), (1, right)):
                    gradient = upstream[pair, 2 * t + odd].astype(F32)
                    gradient = gradient + back[:, h * LANES : (h + 1) * LANES]
                    results.append(jnp.where(live, gradient, 0.0).astype(BF))
                store_slots(staging, t, pair, slots, *results)

        convolve_group(matrix, columns, carry_ref, finish)
        return carry

    lax.fori_loop(0, pairs // 2, body, 0)
    write_out(staging, out)


def unpack_kernel(source, out, *, height, width):
    channels = out.shape[0]
    tiles = -(-width // LANES)
    blocks = []
    for a in range(height // channels):
        for tile in range(tiles):
            start = tile * height + a * channels
            piece = source[start : start + channels, :].astype(F32)
            blocks.append(piece[:, : min(LANES, width - tile * LANES)])
    out[...] = jnp.concatenate(blocks, axis=1)


def call(kernel, out_shape, n_smem, n_vmem, scratch=(), flops=0, moved=4 << 20):
    single = not isinstance(out_shape, (list, tuple))
    return pl.pallas_call(
        kernel,
        out_shape=out_shape,
        in_specs=[SMEM] * n_smem + [VMEM] * n_vmem,
        out_specs=VMEM if single else [VMEM] * len(out_shape),
        scratch_shapes=list(scratch),
        compiler_params=pltpu.CompilerParams(vmem_limit_bytes=56 << 20),
        cost_estimate=pl.CostEstimate(flops=flops, bytes_accessed=moved, transcendentals=0),
    )


def summed(terms, scale):
    axes = ("gx", "gy")
    devices = lax.axis_size("gx") * lax.axis_size("gy")
    me = lax.axis_index("gx") * lax.axis_size("gy") + lax.axis_index("gy")
    bits = [1 << b for b in range(devices.bit_length() - 1)]

    def swapped(block, bit):
        return lax.ppermute(block, axes, [(i, i ^ bit) for i in range(devices)])

    block = terms
    for bit in bits:
        half = block.shape[0] // 2
        mine = me // bit % 2
        kept = lax.dynamic_slice_in_dim(block, mine * half, half, 0)
        sent = lax.dynamic_slice_in_dim(block, (1 - mine) * half, half, 0)
        block = kept + swapped(sent, bit)
    block = (block * scale).astype(BF)
    for bit in bits[::-1]:
        other = swapped(block, bit)
        mine = me // bit % 2
        block = jnp.where(
            mine == 0,
            jnp.concatenate([block, other], axis=0),
            jnp.concatenate([other, block], axis=0),
        )
    return block


def per_device(feats, cotangent, weight, cell_slot, neighbours, counts):
    channels, _, slots, voxels = feats.shape
    side = math.isqrt(cell_slot.shape[1])
    pairs = slots // 2
    cells = cell_slot.reshape(side * side)
    links = neighbours.reshape(slots * 8)
    count = counts.reshape(1)
    native = jax.ShapeDtypeStruct((channels, slots, voxels), BF)
    field = jax.ShapeDtypeStruct((pairs, 8, channels, LANES), BF)
    rows = jax.ShapeDtypeStruct((side // 2, channels, LANES), BF)
    column = jax.ShapeDtypeStruct((4, channels, LANES), BF)
    staging = pltpu.VMEM((4, channels * slots, LANES), F32)
    table = pltpu.VMEM((pairs + 2 + side // 2, 8, channels, LANES), BF)
    columns = pltpu.VMEM((9 * channels, 20 * LANES), BF)
    carry_ref = pltpu.VMEM((channels, 4 * LANES), F32)
    flops = 2 * 27 * channels * channels * slots * voxels

    prepared, low_edge, high_edge = call(
        functools.partial(prepare_kernel, side=side), [field, rows, rows], 1, 1, [staging]
    )(cells, feats.reshape(channels, slots, voxels))
    below_x = passed_along(high_edge, "gx", 1)
    above_x = passed_along(low_edge, "gx", -1)
    upstream = call(regroup_kernel, field, 0, 1, [staging])(
        cotangent.reshape(channels, slots, voxels)
    )
    make_columns = call(functools.partial(column_kernel, side=side), [column, column], 1, 3)
    low_column, high_column = make_columns(cells, prepared, below_x, above_x)
    below_y = from_behind(high_column, "gy", 1)
    above_y = from_behind(low_column, "gy", -1)

    taps = weight.reshape(channels, 3, 9 * channels)
    matrix = taps.transpose(1, 0, 2).reshape(3 * channels, 9 * channels)
    flipped = weight.reshape(channels, 27, channels)[:, ::-1, :].reshape(channels, 3, 9, channels)
    flipped = flipped.transpose(1, 3, 2, 0).reshape(3 * channels, 9 * channels)

    output, grad, terms, low_edge, high_edge = call(
        functools.partial(forward_kernel, side=side),
        [native, field, jax.ShapeDtypeStruct((ROWS, LANES), F32), rows, rows],
        3,
        7,
        [
            table,
            columns,
            pltpu.VMEM((3 * channels, 20 * LANES), BF),
            carry_ref,
            pltpu.VMEM((3 * channels, 9 * channels), F32),
            staging,
        ],
        2 * flops,
    )(cells, links, count, prepared, below_x, above_x, below_y, above_y, upstream, matrix)

    below_x = passed_along(high_edge, "gx", 1)
    above_x = passed_along(low_edge, "gx", -1)
    low_column, high_column = make_columns(cells, grad, below_x, above_x)
    below_y = from_behind(high_column, "gy", 1)
    above_y = from_behind(low_column, "gy", -1)
    grad_feats = call(
        functools.partial(backward_kernel, side=side),
        native,
        2,
        7,
        [table, columns, carry_ref, staging],
        flops,
    )(links, count, grad, below_x, above_x, below_y, above_y, upstream, flipped)

    device_total = lax.axis_size("gx") * lax.axis_size("gy")
    scale = 1.0 / math.sqrt(voxels * slots * device_total)
    grad_weight = call(
        functools.partial(unpack_kernel, height=3 * channels, width=9 * channels),
        jax.ShapeDtypeStruct((channels, 27 * channels), F32),
        0,
        1,
    )(summed(terms, scale))
    return (output.reshape(feats.shape), grad_feats.reshape(feats.shape), grad_weight)


def solution(mesh):
    placed = (
        P(None, "gx", "gy", None),
        P(None, "gx", "gy", None),
        P(),
        P("gx", "gy"),
        P("gx", "gy", None),
        P("gx", "gy"),
    )
    return jax.shard_map(
        per_device,
        mesh=mesh,
        in_specs=placed,
        out_specs=(P(None, "gx", "gy", None), P(None, "gx", "gy", None), P()),
        check_vma=False,
    )
```

profile of v0, /device:TPU:1, one launch (start us, length us, event | category | flops | bytes accessed | tf_op | source)
XLA Modules:
  0.0 160.7 jit_solution(3018428657376233206)
XLA Ops:
  0.6 0.0 copy-start.5
  0.6 4.5 %shard_map.85 = (bf16[8,8,96,128]{3,2,1,0:T(8,128)(2,1)}, bf16[3,96,128]{2,1,0:T(8,128)(2,1)}, bf16[3,96,128]{2,1,0:T(8,128)(2,1)}) custom-call(s32[36]{0:T(128)} %bitcast.24, bf16[96,16,512]{2,1,0:T(8,128)(2,1)} %bitcast.21), custom_call_target="tpu_custom_call" | custom-call | bytes 4194304 | tf_op jit(solution)/shard_map/pallas_call | solution.py:396
  5.2 2.1 %collective-permute-start = (bf16[3,96,128]{2,1,0:T(8,128)(2,1)}, bf16[3,96,128]{2,1,0:T(8,128)(2,1)S(1)}, u32[]{:S(2)}, u32[]{:S(2)}) collective-permute-start(bf16[3,96,128]{2,1,0:T(8,128)(2,1)} %get-tuple-element.16), channel_id=1, source_target_pairs={{24,0},{0,8},{8,16},{16,24},{25,1},{1,9},{9,17},{17,25},{26,2},{2,... | collective-permute-start | bytes 221192 | tf_op jit(solution)/shard_map/ppermute | solution.py:23
  7.3 2.0 %collective-permute-start.1 = (bf16[3,96,128]{2,1,0:T(8,128)(2,1)}, bf16[3,96,128]{2,1,0:T(8,128)(2,1)S(1)}, u32[]{:S(2)}, u32[]{:S(2)}) collective-permute-start(bf16[3,96,128]{2,1,0:T(8,128)(2,1)} %get-tuple-element.17), channel_id=1, source_target_pairs={{8,0},{16,8},{24,16},{0,24},{9,1},{17,9},{25,17},{1,25},{10,2},{18... | collective-permute-start | bytes 221192 | tf_op jit(solution)/shard_map/ppermute | solution.py:23
  9.3 2.1 %collective-permute-done.below.below_x = bf16[3,96,128]{2,1,0:T(8,128)(2,1)S(1)} collective-permute-done((bf16[3,96,128]{2,1,0:T(8,128)(2,1)}, bf16[3,96,128]{2,1,0:T(8,128)(2,1)S(1)}, u32[]{:S(2)}, u32[]{:S(2)}) %collective-permute-start) | collective-permute-done | bytes 73760 | tf_op jit(solution)/shard_map/ppermute | solution.py:23
  11.4 1.3 collective-permute-done.1.above.above_x
  12.7 0.0 copy-done.1
  12.7 0.6 copy-done.2
  13.3 3.0 %shard_map.86 = (bf16[4,96,128]{2,1,0:T(8,128)(2,1)}, bf16[4,96,128]{2,1,0:T(8,128)(2,1)}) custom-call(s32[36]{0:T(128)} %bitcast.25, bf16[8,8,96,128]{3,2,1,0:T(8,128)(2,1)} %get-tuple-element.15.field, bf16[3,96,128]{2,1,0:T(8,128)(2,1)} %copy-done.1, bf16[3,96,128]{2,1,0:T(8,128)(2,1)} %copy-done.2), custom_call_target="tpu_custom_call" | custom-call | bytes 4194304 | tf_op jit(solution)/shard_map/pallas_call | solution.py:405
  16.3 4.1 %collective-permute-start.2 = (bf16[4,96,128]{2,1,0:T(8,128)(2,1)}, bf16[4,96,128]{2,1,0:T(8,128)(2,1)S(1)}, u32[]{:S(2)}, u32[]{:S(2)}) collective-permute-start(bf16[4,96,128]{2,1,0:T(8,128)(2,1)} %get-tuple-element.18), channel_id=1, source_target_pairs={{0,1},{1,2},{2,3},{3,4},{4,5},{5,6},{6,7},{8,9},{9,10},{10,11},{11... | collective-permute-start | bytes 294920 | tf_op jit(solution)/shard_map/ppermute | solution.py:29
  20.4 1.9 %collective-permute-start.3 = (bf16[4,96,128]{2,1,0:T(8,128)(2,1)}, bf16[4,96,128]{2,1,0:T(8,128)(2,1)S(1)}, u32[]{:S(2)}, u32[]{:S(2)}) collective-permute-start(bf16[4,96,128]{2,1,0:T(8,128)(2,1)} %get-tuple-element.19), channel_id=1, source_target_pairs={{1,0},{2,1},{3,2},{4,3},{5,4},{6,5},{7,6},{9,8},{10,9},{11,10},{12... | collective-permute-start | bytes 294920 | tf_op jit(solution)/shard_map/ppermute | solution.py:29
  22.4 0.0 copy-done.5
  22.4 0.1 copy.13
  22.4 0.7 reshape.43.links
  23.8 0.0 copy-start
  23.8 4.5 %shard_map.87.upstream = bf16[8,8,96,128]{3,2,1,0:T(8,128)(2,1)} custom-call(bf16[96,16,512]{2,1,0:T(8,128)(2,1)} %bitcast.22), custom_call_target="tpu_custom_call" | custom-call | bytes 4194304 | tf_op jit(solution)/shard_map/pallas_call | solution.py:401
  28.3 0.4 reshape.47
  28.7 0.8 copy.14
  29.5 0.0 collective-permute-done.2.below_y
  29.5 0.0 collective-permute-done.3.above_y
  29.6 0.6 copy-done.6
  30.2 0.0 copy-done.7
  30.2 41.6 %shard_map.88 = (bf16[96,16,512]{2,1,0:T(8,128)(2,1)}, bf16[8,8,96,128]{3,2,1,0:T(8,128)(2,1)}, f32[2048,128]{1,0:T(8,128)}, bf16[3,96,128]{2,1,0:T(8,128)(2,1)}, bf16[3,96,128]{2,1,0:T(8,128)(2,1)}) custom-call(s32[36]{0:T(128)} %bitcast.26, s32[128]{0:T(128)} %reshape.43.links, s32[1]{0:T(128)} %bitcast.16.counts, ...), custom_call_target="tpu_custom_call" | custom-call | flops 8153726976 | bytes 4194304 | tf_op jit(solution)/shard_map/pallas_call | solution.py:414
  71.8 1.1 constant_dynamic-slice_fusion.4
  72.9 0.1 collective-permute-start.8
  73.0 1.9 %collective-permute-done.8 = f32[1024,128]{1,0:T(8,128)S(1)} collective-permute-done((f32[1024,128]{1,0:T(8,128)S(1)}, f32[1024,128]{1,0:T(8,128)S(1)}, u32[]{:S(2)}, u32[]{:S(2)}) %collective-permute-start.8) | collective-permute-done | bytes 524320 | tf_op jit(solution)/shard_map/ppermute | solution.py:358
  74.8 1.1 dynamic-slice_add_fusion
  76.0 1.5 collective-permute-start.9
  77.5 6.3 %collective-permute-done.9 = f32[512,128]{1,0:T(8,128)S(1)} collective-permute-done((f32[512,128]{1,0:T(8,128)S(1)}, f32[512,128]{1,0:T(8,128)S(1)}, u32[]{:S(2)}, u32[]{:S(2)}) %collective-permute-start.9) | collective-permute-done | bytes 262176 | tf_op jit(solution)/shard_map/ppermute | solution.py:358
  83.9 2.2 %collective-permute-start.10 = (f32[256,128]{1,0:T(8,128)S(1)}, f32[256,128]{1,0:T(8,128)S(1)}, u32[]{:S(2)}, u32[]{:S(2)}) collective-permute-start(f32[256,128]{1,0:T(8,128)S(1)} %constant_dynamic-slice_fusion.2), channel_id=1, source_target_pairs={{0,4},{1,5},{2,6},{3,7},{4,0},{5,1},{6,2},{7,3},{8,12},{9,13},{10,... | collective-permute-start | bytes 393224 | tf_op jit(solution)/shard_map/ppermute | solution.py:358
  86.1 2.4 %collective-permute-done.10 = f32[256,128]{1,0:T(8,128)S(1)} collective-permute-done((f32[256,128]{1,0:T(8,128)S(1)}, f32[256,128]{1,0:T(8,128)S(1)}, u32[]{:S(2)}, u32[]{:S(2)}) %collective-permute-start.10) | collective-permute-done | bytes 131104 | tf_op jit(solution)/shard_map/ppermute | solution.py:358
  88.5 0.9 collective-permute-start.11
  89.4 2.3 %collective-permute-done.11 = f32[128,128]{1,0:T(8,128)S(1)} collective-permute-done((f32[128,128]{1,0:T(8,128)S(1)}, f32[128,128]{1,0:T(8,128)S(1)}, u32[]{:S(2)}, u32[]{:S(2)}) %collective-permute-start.11) | collective-permute-done | bytes 65568 | tf_op jit(solution)/shard_map/ppermute | solution.py:358
  91.7 1.7 %collective-permute-start.12 = (f32[64,128]{1,0:T(8,128)S(1)}, f32[64,128]{1,0:T(8,128)S(1)}, u32[]{:S(2)}, u32[]{:S(2)}) collective-permute-start(f32[64,128]{1,0:T(8,128)S(1)} %constant_dynamic-slice_fusion), channel_id=1, source_target_pairs={{0,16},{1,17},{2,18},{3,19},{4,20},{5,21},{6,22},{7,23},{8,24},{9,... | collective-permute-start | bytes 98312 | tf_op jit(solution)/shard_map/ppermute | solution.py:358
  93.4 2.0 %collective-permute-done.12 = f32[64,128]{1,0:T(8,128)S(1)} collective-permute-done((f32[64,128]{1,0:T(8,128)S(1)}, f32[64,128]{1,0:T(8,128)S(1)}, u32[]{:S(2)}, u32[]{:S(2)}) %collective-permute-start.12) | collective-permute-done | bytes 32800 | tf_op jit(solution)/shard_map/ppermute | solution.py:358
  95.5 1.7 %collective-permute-start.13 = (bf16[64,128]{1,0:T(8,128)(2,1)S(1)}, bf16[64,128]{1,0:T(8,128)(2,1)S(1)}, u32[]{:S(2)}, u32[]{:S(2)}) collective-permute-start(bf16[64,128]{1,0:T(8,128)(2,1)S(1)} %multiply_convert_fusion), channel_id=1, source_target_pairs={{0,16},{1,17},{2,18},{3,19},{4,20},{5,21},{6,22},{7,23},{8,24},{9,... | collective-permute-start | bytes 49160 | tf_op jit(solution)/shard_map/ppermute | solution.py:358
  97.2 2.3 %collective-permute-done.13 = bf16[64,128]{1,0:T(8,128)(2,1)S(1)} collective-permute-done((bf16[64,128]{1,0:T(8,128)(2,1)S(1)}, bf16[64,128]{1,0:T(8,128)(2,1)S(1)}, u32[]{:S(2)}, u32[]{:S(2)}) %collective-permute-start.13) | collective-permute-done | bytes 16416 | tf_op jit(solution)/shard_map/ppermute | solution.py:358
  99.5 0.9 collective-permute-start.14
  100.4 1.9 %collective-permute-done.14 = bf16[128,128]{1,0:T(8,128)(2,1)S(1)} collective-permute-done((bf16[128,128]{1,0:T(8,128)(2,1)S(1)}, bf16[128,128]{1,0:T(8,128)(2,1)S(1)}, u32[]{:S(2)}, u32[]{:S(2)}) %collective-permute-start.14) | collective-permute-done | bytes 32800 | tf_op jit(solution)/shard_map/ppermute | solution.py:358
  102.4 1.1 collective-permute-start.15
  103.4 2.1 %collective-permute-done.15 = bf16[256,128]{1,0:T(8,128)(2,1)S(1)} collective-permute-done((bf16[256,128]{1,0:T(8,128)(2,1)S(1)}, bf16[256,128]{1,0:T(8,128)(2,1)S(1)}, u32[]{:S(2)}, u32[]{:S(2)}) %collective-permute-start.15) | collective-permute-done | bytes 65568 | tf_op jit(solution)/shard_map/ppermute | solution.py:358
  105.6 0.1 collective-permute-start.16
  105.7 0.9 collective-permute-start.4
  106.6 2.8 %collective-permute-start.5 = (bf16[3,96,128]{2,1,0:T(8,128)(2,1)S(1)}, bf16[3,96,128]{2,1,0:T(8,128)(2,1)S(1)}, u32[]{:S(2)}, u32[]{:S(2)}) collective-permute-start(bf16[3,96,128]{2,1,0:T(8,128)(2,1)S(1)} %copy-done.10), channel_id=1, source_target_pairs={{8,0},{16,8},{24,16},{0,24},{9,1},{17,9},{25,17},{1,25},{10,2},{18... | collective-permute-start | bytes 221192 | tf_op jit(solution)/shard_map/ppermute | solution.py:23
  109.4 0.3 copy.15
  109.8 0.3 copy.22
  110.1 1.6 reshape.54.matrix
  111.7 0.0 collective-permute-done.4.below.below_x
  111.7 0.0 collective-permute-done.5.above.above_x
  111.7 0.6 copy-done.3
  112.3 0.0 copy-done.4
  112.4 3.0 %shard_map.89 = (bf16[4,96,128]{2,1,0:T(8,128)(2,1)}, bf16[4,96,128]{2,1,0:T(8,128)(2,1)}) custom-call(s32[36]{0:T(128)} %bitcast.27, bf16[8,8,96,128]{3,2,1,0:T(8,128)(2,1)} %get-tuple-element.21.field, bf16[3,96,128]{2,1,0:T(8,128)(2,1)} %copy-done.3, bf16[3,96,128]{2,1,0:T(8,128)(2,1)} %copy-done.4), custom_call_target="tpu_custom_call" | custom-call | bytes 4194304 | tf_op jit(solution)/shard_map/pallas_call | solution.py:432
  115.4 11.3 %collective-permute-start.6 = (bf16[4,96,128]{2,1,0:T(8,128)(2,1)}, bf16[4,96,128]{2,1,0:T(8,128)(2,1)S(1)}, u32[]{:S(2)}, u32[]{:S(2)}) collective-permute-start(bf16[4,96,128]{2,1,0:T(8,128)(2,1)} %get-tuple-element.24), channel_id=1, source_target_pairs={{0,1},{1,2},{2,3},{3,4},{4,5},{5,6},{6,7},{8,9},{9,10},{10,11},{11... | collective-permute-start | bytes 294920 | tf_op jit(solution)/shard_map/ppermute | solution.py:29
  126.7 1.9 %collective-permute-start.7 = (bf16[4,96,128]{2,1,0:T(8,128)(2,1)}, bf16[4,96,128]{2,1,0:T(8,128)(2,1)S(1)}, u32[]{:S(2)}, u32[]{:S(2)}) collective-permute-start(bf16[4,96,128]{2,1,0:T(8,128)(2,1)} %get-tuple-element.25), channel_id=1, source_target_pairs={{1,0},{2,1},{3,2},{4,3},{5,4},{6,5},{7,6},{9,8},{10,9},{11,10},{12... | collective-permute-start | bytes 294920 | tf_op jit(solution)/shard_map/ppermute | solution.py:29
  128.6 0.0 collective-permute-done.16
  128.6 0.1 maximum_select_fusion.1
  128.7 0.1 collective-permute-start.17
  128.8 0.0 collective-permute-done.6.below_y
  128.8 4.0 %collective-permute-done.7.above_y = bf16[4,96,128]{2,1,0:T(8,128)(2,1)S(1)} collective-permute-done((bf16[4,96,128]{2,1,0:T(8,128)(2,1)}, bf16[4,96,128]{2,1,0:T(8,128)(2,1)S(1)}, u32[]{:S(2)}, u32[]{:S(2)}) %collective-permute-start.7) | collective-permute-done | bytes 98336 | tf_op jit(solution)/shard_map/ppermute | solution.py:29
  132.8 0.6 copy-done.9
  133.5 24.2 %shard_map.90 = bf16[96,16,512]{2,1,0:T(8,128)(2,1)} custom-call(s32[128]{0:T(128)} %reshape.43.links, s32[1]{0:T(128)} %bitcast.17.counts, bf16[8,8,96,128]{3,2,1,0:T(8,128)(2,1)} %get-tuple-element.21.field, bf16[3,96,128]{2,1,0:T(8,128)(2,1)} %copy-done.3, bf16[3,96,128]{2,1,0:T(8,128)(2,1)} %copy-done.4, bf16[4,96,128]{2,1,0:T(8,128)(2,1)} %copy-done.8, ...), custom_call_target="tpu_custom_call" | custom-call | flops 4076863488 | bytes 4194304 | tf_op jit(solution)/shard_map/pallas_call | solution.py:435
  157.7 0.0 collective-permute-done.17
  157.7 0.9 maximum_select_fusion.source
  158.6 2.2 %shard_map.91 = f32[96,2592]{1,0:T(8,128)} custom-call(bf16[2048,128]{1,0:T(8,128)(2,1)} %maximum_select_fusion.source), custom_call_target="tpu_custom_call" | custom-call | bytes 4194304 | tf_op jit(solution)/shard_map/pallas_call | solution.py:446
  (26 shorter events, 0.3 us)
Async XLA Ops:
  0.6 21.7 %copy-start.5 = (s32[1,16,8]{1,2,0:T(8,128)S(1)}, s32[1,16,8]{1,2,0:T(8,128)}, u32[]{:S(2)}) copy-start(s32[1,16,8]{1,2,0:T(8,128)} %param.10) | copy-start | bytes 1540
  5.2 6.2 %collective-permute-start = (bf16[3,96,128]{2,1,0:T(8,128)(2,1)}, bf16[3,96,128]{2,1,0:T(8,128)(2,1)S(1)}, u32[]{:S(2)}, u32[]{:S(2)}) collective-permute-start(bf16[3,96,128]{2,1,0:T(8,128)(2,1)} %get-tuple-element.16), channel_id=1, source_target_pairs={{24,0},{0,8},{8,16},{16,24},{25,1},{1,9},{9,17},{17,25},{26,2},{2,... | collective-permute-start | bytes 221192 | tf_op jit(solution)/shard_map/ppermute | solution.py:23
  7.3 5.3 %collective-permute-start.1 = (bf16[3,96,128]{2,1,0:T(8,128)(2,1)}, bf16[3,96,128]{2,1,0:T(8,128)(2,1)S(1)}, u32[]{:S(2)}, u32[]{:S(2)}) collective-permute-start(bf16[3,96,128]{2,1,0:T(8,128)(2,1)} %get-tuple-element.17), channel_id=1, source_target_pairs={{8,0},{16,8},{24,16},{0,24},{9,1},{17,9},{25,17},{1,25},{10,2},{18... | collective-permute-start | bytes 221192 | tf_op jit(solution)/shard_map/ppermute | solution.py:23
  11.4 1.3 copy-start.1
  12.7 0.6 copy-start.2
  16.3 13.2 %collective-permute-start.2 = (bf16[4,96,128]{2,1,0:T(8,128)(2,1)}, bf16[4,96,128]{2,1,0:T(8,128)(2,1)S(1)}, u32[]{:S(2)}, u32[]{:S(2)}) collective-permute-start(bf16[4,96,128]{2,1,0:T(8,128)(2,1)} %get-tuple-element.18), channel_id=1, source_target_pairs={{0,1},{1,2},{2,3},{3,4},{4,5},{5,6},{6,7},{8,9},{9,10},{10,11},{11... | collective-permute-start | bytes 294920 | tf_op jit(solution)/shard_map/ppermute | solution.py:29
  20.4 9.1 %collective-permute-start.3 = (bf16[4,96,128]{2,1,0:T(8,128)(2,1)}, bf16[4,96,128]{2,1,0:T(8,128)(2,1)S(1)}, u32[]{:S(2)}, u32[]{:S(2)}) collective-permute-start(bf16[4,96,128]{2,1,0:T(8,128)(2,1)} %get-tuple-element.19), channel_id=1, source_target_pairs={{1,0},{2,1},{3,2},{4,3},{5,4},{6,5},{7,6},{9,8},{10,9},{11,10},{12... | collective-permute-start | bytes 294920 | tf_op jit(solution)/shard_map/ppermute | solution.py:29
  23.8 4.5 %copy-start = (bf16[96,2592]{1,0:T(8,128)(2,1)S(1)}, bf16[96,2592]{1,0:T(8,128)(2,1)}, u32[]{:S(2)}) copy-start(bf16[96,2592]{1,0:T(8,128)(2,1)} %param.8) | copy-start | bytes 1492996
  29.5 0.6 copy-start.6
  29.5 0.7 copy-start.7
  72.9 2.0 %collective-permute-start.8 = (f32[1024,128]{1,0:T(8,128)S(1)}, f32[1024,128]{1,0:T(8,128)S(1)}, u32[]{:S(2)}, u32[]{:S(2)}) collective-permute-start(f32[1024,128]{1,0:T(8,128)S(1)} %constant_dynamic-slice_fusion.4), channel_id=1, source_target_pairs={{0,1},{1,0},{2,3},{3,2},{4,5},{5,4},{6,7},{7,6},{8,9},{9,8},{10,11... | collective-permute-start | bytes 1572872 | tf_op jit(solution)/shard_map/ppermute | solution.py:358
  76.0 29.8 %copy-start.11 = (bf16[3,96,128]{2,1,0:T(8,128)(2,1)S(1)}, bf16[3,96,128]{2,1,0:T(8,128)(2,1)}, u32[]{:S(2)}) copy-start(bf16[3,96,128]{2,1,0:T(8,128)(2,1)} %get-tuple-element.22) | copy-start | bytes 221188
  76.0 30.6 %copy-start.10 = (bf16[3,96,128]{2,1,0:T(8,128)(2,1)S(1)}, bf16[3,96,128]{2,1,0:T(8,128)(2,1)}, u32[]{:S(2)}) copy-start(bf16[3,96,128]{2,1,0:T(8,128)(2,1)} %get-tuple-element.23) | copy-start | bytes 221188
  76.0 7.9 %collective-permute-start.9 = (f32[512,128]{1,0:T(8,128)S(1)}, f32[512,128]{1,0:T(8,128)S(1)}, u32[]{:S(2)}, u32[]{:S(2)}) collective-permute-start(f32[512,128]{1,0:T(8,128)S(1)} %constant_dynamic-slice_fusion.3), channel_id=1, source_target_pairs={{0,2},{1,3},{2,0},{3,1},{4,6},{5,7},{6,4},{7,5},{8,10},{9,11},{10,... | collective-permute-start | bytes 786440 | tf_op jit(solution)/shard_map/ppermute | solution.py:358
  83.9 4.6 %collective-permute-start.10 = (f32[256,128]{1,0:T(8,128)S(1)}, f32[256,128]{1,0:T(8,128)S(1)}, u32[]{:S(2)}, u32[]{:S(2)}) collective-permute-start(f32[256,128]{1,0:T(8,128)S(1)} %constant_dynamic-slice_fusion.2), channel_id=1, source_target_pairs={{0,4},{1,5},{2,6},{3,7},{4,0},{5,1},{6,2},{7,3},{8,12},{9,13},{10,... | collective-permute-start | bytes 393224 | tf_op jit(solution)/shard_map/ppermute | solution.py:358
  88.5 3.2 %collective-permute-start.11 = (f32[128,128]{1,0:T(8,128)S(1)}, f32[128,128]{1,0:T(8,128)S(1)}, u32[]{:S(2)}, u32[]{:S(2)}) collective-permute-start(f32[128,128]{1,0:T(8,128)S(1)} %constant_dynamic-slice_fusion.1), channel_id=1, source_target_pairs={{0,8},{1,9},{2,10},{3,11},{4,12},{5,13},{6,14},{7,15},{8,0},{9,1},... | collective-permute-start | bytes 196616 | tf_op jit(solution)/shard_map/ppermute | solution.py:358
  91.7 3.7 %collective-permute-start.12 = (f32[64,128]{1,0:T(8,128)S(1)}, f32[64,128]{1,0:T(8,128)S(1)}, u32[]{:S(2)}, u32[]{:S(2)}) collective-permute-start(f32[64,128]{1,0:T(8,128)S(1)} %constant_dynamic-slice_fusion), channel_id=1, source_target_pairs={{0,16},{1,17},{2,18},{3,19},{4,20},{5,21},{6,22},{7,23},{8,24},{9,... | collective-permute-start | bytes 98312 | tf_op jit(solution)/shard_map/ppermute | solution.py:358
  95.5 4.0 %collective-permute-start.13 = (bf16[64,128]{1,0:T(8,128)(2,1)S(1)}, bf16[64,128]{1,0:T(8,128)(2,1)S(1)}, u32[]{:S(2)}, u32[]{:S(2)}) collective-permute-start(bf16[64,128]{1,0:T(8,128)(2,1)S(1)} %multiply_convert_fusion), channel_id=1, source_target_pairs={{0,16},{1,17},{2,18},{3,19},{4,20},{5,21},{6,22},{7,23},{8,24},{9,... | collective-permute-start | bytes 49160 | tf_op jit(solution)/shard_map/ppermute | solution.py:358
  99.5 2.8 %collective-permute-start.14 = (bf16[128,128]{1,0:T(8,128)(2,1)S(1)}, bf16[128,128]{1,0:T(8,128)(2,1)S(1)}, u32[]{:S(2)}, u32[]{:S(2)}) collective-permute-start(bf16[128,128]{1,0:T(8,128)(2,1)S(1)} %maximum_select_fusion.4), channel_id=1, source_target_pairs={{0,8},{1,9},{2,10},{3,11},{4,12},{5,13},{6,14},{7,15},{8,0},{9,1},... | collective-permute-start | bytes 98312 | tf_op jit(solution)/shard_map/ppermute | solution.py:358
  102.4 3.2 %collective-permute-start.15 = (bf16[256,128]{1,0:T(8,128)(2,1)S(1)}, bf16[256,128]{1,0:T(8,128)(2,1)S(1)}, u32[]{:S(2)}, u32[]{:S(2)}) collective-permute-start(bf16[256,128]{1,0:T(8,128)(2,1)S(1)} %maximum_select_fusion.3), channel_id=1, source_target_pairs={{0,4},{1,5},{2,6},{3,7},{4,0},{5,1},{6,2},{7,3},{8,12},{9,13},{10,... | collective-permute-start | bytes 196616 | tf_op jit(solution)/shard_map/ppermute | solution.py:358
  105.6 23.0 %collective-permute-start.16 = (bf16[512,128]{1,0:T(8,128)(2,1)S(1)}, bf16[512,128]{1,0:T(8,128)(2,1)S(1)}, u32[]{:S(2)}, u32[]{:S(2)}) collective-permute-start(bf16[512,128]{1,0:T(8,128)(2,1)S(1)} %maximum_select_fusion.2), channel_id=1, source_target_pairs={{0,2},{1,3},{2,0},{3,1},{4,6},{5,7},{6,4},{7,5},{8,10},{9,11},{10,... | collective-permute-start | bytes 393224 | tf_op jit(solution)/shard_map/ppermute | solution.py:358
  105.7 6.0 %collective-permute-start.4 = (bf16[3,96,128]{2,1,0:T(8,128)(2,1)S(1)}, bf16[3,96,128]{2,1,0:T(8,128)(2,1)S(1)}, u32[]{:S(2)}, u32[]{:S(2)}) collective-permute-start(bf16[3,96,128]{2,1,0:T(8,128)(2,1)S(1)} %copy-done.11), channel_id=1, source_target_pairs={{24,0},{0,8},{8,16},{16,24},{25,1},{1,9},{9,17},{17,25},{26,2},{2,... | collective-permute-start | bytes 221192 | tf_op jit(solution)/shard_map/ppermute | solution.py:23
  106.6 5.1 %collective-permute-start.5 = (bf16[3,96,128]{2,1,0:T(8,128)(2,1)S(1)}, bf16[3,96,128]{2,1,0:T(8,128)(2,1)S(1)}, u32[]{:S(2)}, u32[]{:S(2)}) collective-permute-start(bf16[3,96,128]{2,1,0:T(8,128)(2,1)S(1)} %copy-done.10), channel_id=1, source_target_pairs={{8,0},{16,8},{24,16},{0,24},{9,1},{17,9},{25,17},{1,25},{10,2},{18... | collective-permute-start | bytes 221192 | tf_op jit(solution)/shard_map/ppermute | solution.py:23
  111.7 0.6 copy-start.3
  111.7 0.6 copy-start.4
  115.4 13.4 %collective-permute-start.6 = (bf16[4,96,128]{2,1,0:T(8,128)(2,1)}, bf16[4,96,128]{2,1,0:T(8,128)(2,1)S(1)}, u32[]{:S(2)}, u32[]{:S(2)}) collective-permute-start(bf16[4,96,128]{2,1,0:T(8,128)(2,1)} %get-tuple-element.24), channel_id=1, source_target_pairs={{0,1},{1,2},{2,3},{3,4},{4,5},{5,6},{6,7},{8,9},{9,10},{10,11},{11... | collective-permute-start | bytes 294920 | tf_op jit(solution)/shard_map/ppermute | solution.py:29
  126.7 6.1 %collective-permute-start.7 = (bf16[4,96,128]{2,1,0:T(8,128)(2,1)}, bf16[4,96,128]{2,1,0:T(8,128)(2,1)S(1)}, u32[]{:S(2)}, u32[]{:S(2)}) collective-permute-start(bf16[4,96,128]{2,1,0:T(8,128)(2,1)} %get-tuple-element.25), channel_id=1, source_target_pairs={{1,0},{2,1},{3,2},{4,3},{5,4},{6,5},{7,6},{9,8},{10,9},{11,10},{12... | collective-permute-start | bytes 294920 | tf_op jit(solution)/shard_map/ppermute | solution.py:29
  128.7 29.0 %collective-permute-start.17 = (bf16[1024,128]{1,0:T(8,128)(2,1)S(1)}, bf16[1024,128]{1,0:T(8,128)(2,1)S(1)}, u32[]{:S(2)}, u32[]{:S(2)}) collective-permute-start(bf16[1024,128]{1,0:T(8,128)(2,1)S(1)} %maximum_select_fusion.1), channel_id=1, source_target_pairs={{0,1},{1,0},{2,3},{3,2},{4,5},{5,4},{6,7},{7,6},{8,9},{9,8},{10,11... | collective-permute-start | bytes 786440 | tf_op jit(solution)/shard_map/ppermute | solution.py:358
  128.8 4.0 %copy-start.8 = (bf16[4,96,128]{2,1,0:T(8,128)(2,1)}, bf16[4,96,128]{2,1,0:T(8,128)(2,1)S(1)}, u32[]{:S(2)}) copy-start(bf16[4,96,128]{2,1,0:T(8,128)(2,1)S(1)} %collective-permute-done.6.below_y) | copy-start | bytes 294916
  132.8 0.6 copy-start.9
where the time goes:
time: 162 us; the launch traced here: 161 us
  Pallas kernels  83 us (51%)
  starting transfers between devices  37.4 us (23%)
  waiting for transfers between devices  28.6 us (18%)
  local copies, waits for them, and re-layouts  7.99 us (5%)
  other arithmetic  2.25 us (1%)
    pallas_call x1, Pallas kernels, per_device(): call(functools.partial(forward_kernel, side=side), [native, field, jax.Sh...  41.6 us
    pallas_call x1, Pallas kernels, per_device(): call(functools.partial(backward_kernel, side=side), native, 2, 7, [table,...  24.2 us
    ppermute x10, waiting for transfers between devices, swapped(): return lax.ppermute(block, axes, [(i, i ^ bit) for i in range(devices)])  21.2 us
    ppermute x4, starting transfers between devices, from_behind(): return lax.ppermute(block, axis, route)  19.3 us
    ppermute x10, starting transfers between devices, swapped(): return lax.ppermute(block, axes, [(i, i ^ bit) for i in range(devices)])  10.3 us
    ppermute x4, starting transfers between devices, passed_along(): return lax.ppermute(block, axis, route)  7.84 us
    pallas_call x1, Pallas kernels, per_device(): call(functools.partial(prepare_kernel, side=side), [field, rows, rows], 1...  4.53 us
    pallas_call x1, Pallas kernels, per_device(): call(regroup_kernel, field, 0, 1, [staging])  4.49 us
  transfers between devices with their start and end apart: 18, of which 11 were waited for; matrix products, arithmetic and copies ran while one was open for 3% of the time, Pallas kernels for 20%

commit v1 on v0

--- a/solution.py
+++ b/solution.py
@@ -12,6 +12,7 @@
 F32 = jnp.float32
 VMEM = pl.BlockSpec(memory_space=pltpu.VMEM)
 SMEM = pl.BlockSpec(memory_space=pltpu.SMEM)
+ANY = pl.BlockSpec(memory_space=pl.ANY)
 LANES = 128
 HALF = 64
 ROWS = 2048
@@ -110,15 +111,11 @@
             out[quarter] = total
 
 
-def fill_table(table, field, below_x, above_x, below_y, above_y):
+def fill_table(table, field, below_x, above_x, below_y, above_y, sem):
     pairs, _, channels, _ = field.shape
     low = lane_ids(channels) < HALF
-
-    def body(pair, carry):
-        table[pair] = field[pair]
-        return carry
-
-    lax.fori_loop(0, pairs, body, 0)
+    copy = pltpu.make_async_copy(field, table.at[pl.ds(0, pairs)], sem)
+    copy.start()
     for quarter in range(4):
         below, above = below_y[quarter], above_y[quarter]
         table[pairs, quarter] = jnp.where(low, below, turn(above, HALF))
@@ -128,6 +125,7 @@
         table[pairs + 1 + tile, 7] = below_x[tile]
         table[pairs + 1 + tile, 0] = above_x[tile]
     table[pairs + 1 + tiles] = jnp.zeros(table.shape[1:], BF)
+    copy.wait()
 
 
 def locate(index, pairs, side, column):
@@ -150,7 +148,7 @@
     return tile, lane
 
 
-def build_columns(group, links, table, columns, pairs, side):
+def column_builder(group, links, table, columns, pairs, side):
     channels = table.shape[2]
     lanes = lane_ids(channels)
     low = lanes < HALF
@@ -185,32 +183,38 @@
                 middle = fetch(layer, h, dx, 0)
             before = jnp.where(y_first, fetch(layer, h, dx, -1), turn(middle, 8))
             after = jnp.where(y_last, fetch(layer, h, dx, 1), turn(middle, LANES - 8))
-            at = pl.multiple_of(xp * 2 * LANES + h * LANES, LANES)
+            at = xp * 2 * LANES + h * LANES
             for b, value in enumerate((before, middle, after)):
                 lower = jnp.where(z_first, nothing(value), turn(value, 1))
                 upper = jnp.where(z_last, nothing(value), turn(value, LANES - 1))
                 for c, shifted in enumerate((lower, value, upper)):
                     start = (b * 3 + c) * channels
-                    columns[start : start + channels, pl.ds(at, LANES)] = shifted
-
-    layer_of(0, 7, -1)
-
-    def body(xp, carry):
-        layer_of(xp, xp - 1, 0)
-        return carry
-
-    lax.fori_loop(1, 9, body, 0)
-    layer_of(9, 0, 1)
+                    columns[start : start + channels, at : at + LANES] = shifted
+
+    def build(xp):
+        if xp == 0:
+            layer_of(0, 7, -1)
+        elif xp == 9:
+            layer_of(9, 0, 1)
+        else:
+            layer_of(xp, xp - 1, 0)
+
+    return build
 
 
 def product(left, right, contract):
     return lax.dot_general(left, right, (contract, ((), ())), preferred_element_type=F32)
 
 
-def convolve_group(matrix, columns, carry_ref, finish):
+def convolve_group(matrix, columns, carry_ref, build, finish):
     channels = matrix.shape[0] // 3
     width = 2 * LANES
+    build(0)
+    build(1)
     for step in range(5):
+        if step < 4:
+            build(2 * step + 2)
+            build(2 * step + 3)
         part = product(
             matrix[...], columns[:, step * 2 * width : (step + 1) * 2 * width], ((1,), (0,))
         )
@@ -242,43 +246,49 @@
 
 
 def forward_kernel(
-    cells, links, counts, field, below_x, above_x, below_y, above_y, upstream, matrix,
+    cells, links, counts, below_x, above_x, below_y, above_y, matrix, field, given,
     out, grad, terms, low_out, high_out,
-    table, columns, shifted, carry_ref, total, staging, *, side,
+    table, columns, shifted, carry_ref, total, upstream, sems, *, side,
 ):
     pairs, _, channels, _ = field.shape
     slots = 2 * pairs
-    fill_table(table, field, below_x, above_x, below_y, above_y)
+    copy = pltpu.make_async_copy(given, upstream, sems.at[1])
+    copy.start()
+    fill_table(table, field, below_x, above_x, below_y, above_y, sems.at[0])
     total[...] = jnp.zeros(total.shape, F32)
     shifted[...] = jnp.zeros(shifted.shape, BF)
     upper = (lane_ids(channels) >= HALF).astype(jnp.int32)
+    copy.wait()
 
     def body(group, carry):
-        build_columns(group, links, table, columns, pairs, side)
+        build = column_builder(group, links, table, columns, pairs, side)
 
         def finish(t, left, right):
             for h in range(2):
                 pair = group * 2 + h
                 live = 2 * pair + upper < counts[0]
-                results = []
                 for odd, hidden in ((0, left), (1, right)):
                     x = 2 * t + odd
                     hidden = hidden[:, h * LANES : (h + 1) * LANES]
                     gate = jax.nn.sigmoid(hidden)
-                    inputs = field[pair, x].astype(F32)
+                    inputs = table[pair, x].astype(F32)
                     gradient = upstream[pair, x].astype(F32)
                     result = jnp.where(live, inputs + hidden * gate, 0.0)
-                    results.append(result.astype(BF))
+                    out[pair, x] = result.astype(BF)
                     gradient = gradient * gate * (1.0 + hidden * (1.0 - gate))
                     gradient = jnp.where(live, gradient, 0.0).astype(BF)
                     grad[pair, x] = gradient
                     for a in range(3):
                         at = (x + a) * 2 * LANES + h * LANES
                         shifted[a * channels : (a + 1) * channels, at : at + LANES] = gradient
-                store_slots(staging, t, pair, slots, *results)
-
-        convolve_group(matrix, columns, carry_ref, finish)
-        total[...] += product(shifted[...], columns[...], ((1,), (1,)))
+            gather_terms(t)
+
+        def gather_terms(step):
+            span = slice(step * 4 * LANES, (step + 1) * 4 * LANES)
+            total[...] += product(shifted[:, span], columns[:, span], ((1,), (1,)))
+
+        convolve_group(matrix, columns, carry_ref, build, finish)
+        gather_terms(4)
         return carry
 
     lax.fori_loop(0, pairs // 2, body, 0)
@@ -290,36 +300,44 @@
             :, tile * LANES : end
         ]
     edge_rows(cells, grad, low_out, high_out, slots, side)
-    write_out(staging, out)
 
 
 def backward_kernel(
-    links, counts, field, below_x, above_x, below_y, above_y, upstream, matrix,
-    out, table, columns, carry_ref, staging, *, side,
+    links, counts, below_x, above_x, below_y, above_y, matrix, field, given,
+    out, table, columns, carry_ref, upstream, sems, *, side, group,
 ):
     pairs, _, channels, _ = field.shape
-    slots = 2 * pairs
-    fill_table(table, field, below_x, above_x, below_y, above_y)
+    copy = pltpu.make_async_copy(given.at[pl.ds(2 * group, 2)], upstream, sems.at[1])
+    copy.start()
+    fill_table(table, field, below_x, above_x, below_y, above_y, sems.at[0])
     upper = (lane_ids(channels) >= HALF).astype(jnp.int32)
-
-    def body(group, carry):
-        build_columns(group, links, table, columns, pairs, side)
-
-        def finish(t, left, right):
-            for h in range(2):
-                pair = group * 2 + h
-                live = 2 * pair + upper < counts[0]
-                results = []
-                for odd, back in ((0, left), (1, right)):
-                    gradient = upstream[pair, 2 * t + odd].astype(F32)
-                    gradient = gradient + back[:, h * LANES : (h + 1) * LANES]
-                    results.append(jnp.where(live, gradient, 0.0).astype(BF))
-                store_slots(staging, t, pair, slots, *results)
-
-        convolve_group(matrix, columns, carry_ref, finish)
-        return carry
-
-    lax.fori_loop(0, pairs // 2, body, 0)
+    build = column_builder(group, links, table, columns, pairs, side)
+
+    def finish(t, left, right):
+        for h in range(2):
+            live = 2 * (group * 2 + h) + upper < counts[0]
+            for odd, back in ((0, left), (1, right)):
+                x = 2 * t + odd
+                gradient = upstream[h, x].astype(F32) + back[:, h * LANES : (h + 1) * LANES]
+                out[h, x] = jnp.where(live, gradient, 0.0).astype(BF)
+
+    copy.wait()
+    convolve_group(matrix, columns, carry_ref, build, finish)
+
+
+def native_kernel(*refs):
+    *parts, out, staging = refs
+    slots = out.shape[1]
+    count = parts[0].shape[0]
+    for index, part in enumerate(parts):
+
+        def body(pair, carry, index=index, part=part):
+            for t in range(4):
+                even, odd = part[pair, 2 * t], part[pair, 2 * t + 1]
+                store_slots(staging, t, index * count + pair, slots, even, odd)
+            return carry
+
+        lax.fori_loop(0, count, body, 0)
     write_out(staging, out)
 
 
@@ -335,12 +353,12 @@
     out[...] = jnp.concatenate(blocks, axis=1)
 
 
-def call(kernel, out_shape, n_smem, n_vmem, scratch=(), flops=0, moved=4 << 20):
+def call(kernel, out_shape, n_smem, n_vmem, scratch=(), flops=0, moved=4 << 20, n_any=0):
     single = not isinstance(out_shape, (list, tuple))
     return pl.pallas_call(
         kernel,
         out_shape=out_shape,
-        in_specs=[SMEM] * n_smem + [VMEM] * n_vmem,
+        in_specs=[SMEM] * n_smem + [VMEM] * n_vmem + [ANY] * n_any,
         out_specs=VMEM if single else [VMEM] * len(out_shape),
         scratch_shapes=list(scratch),
         compiler_params=pltpu.CompilerParams(vmem_limit_bytes=56 << 20),
@@ -348,7 +366,11 @@
     )
 
 
-def summed(terms, scale):
+def tied(value, *others):
+    return lax.optimization_barrier((value, *others))[0]
+
+
+def summed(terms, scale, tasks):
     axes = ("gx", "gy")
     devices = lax.axis_size("gx") * lax.axis_size("gy")
     me = lax.axis_index("gx") * lax.axis_size("gy") + lax.axis_index("gy")
@@ -358,21 +380,25 @@
         return lax.ppermute(block, axes, [(i, i ^ bit) for i in range(devices)])
 
     block = terms
-    for bit in bits:
-        half = block.shape[0] // 2
+    for step, bit in enumerate(bits + bits[::-1]):
+        beside = tasks[step](block) if step in tasks else None
         mine = me // bit % 2
-        kept = lax.dynamic_slice_in_dim(block, mine * half, half, 0)
-        sent = lax.dynamic_slice_in_dim(block, (1 - mine) * half, half, 0)
-        block = kept + swapped(sent, bit)
-    block = (block * scale).astype(BF)
-    for bit in bits[::-1]:
-        other = swapped(block, bit)
-        mine = me // bit % 2
-        block = jnp.where(
-            mine == 0,
-            jnp.concatenate([block, other], axis=0),
-            jnp.concatenate([other, block], axis=0),
-        )
+        if step < len(bits):
+            half = block.shape[0] // 2
+            kept = lax.dynamic_slice_in_dim(block, mine * half, half, 0)
+            sent = lax.dynamic_slice_in_dim(block, (1 - mine) * half, half, 0)
+            block = kept + swapped(sent, bit)
+            if step == len(bits) - 1:
+                block = (block * scale).astype(BF)
+        else:
+            other = swapped(block, bit)
+            block = jnp.where(
+                mine == 0,
+                jnp.concatenate([block, other], axis=0),
+                jnp.concatenate([other, block], axis=0),
+            )
+        if beside is not None:
+            block = tied(block, beside)
     return block
 
 
@@ -391,6 +417,7 @@
     table = pltpu.VMEM((pairs + 2 + side // 2, 8, channels, LANES), BF)
     columns = pltpu.VMEM((9 * channels, 20 * LANES), BF)
     carry_ref = pltpu.VMEM((channels, 4 * LANES), F32)
+    sems = pltpu.SemaphoreType.DMA((2,))
     flops = 2 * 27 * channels * channels * slots * voxels
 
     prepared, low_edge, high_edge = call(
@@ -402,7 +429,7 @@
         cotangent.reshape(channels, slots, voxels)
     )
     make_columns = call(functools.partial(column_kernel, side=side), [column, column], 1, 3)
-    low_column, high_column = make_columns(cells, prepared, below_x, above_x)
+    low_column, high_column = make_columns(cells, tied(prepared, upstream), below_x, above_x)
     below_y = from_behind(high_column, "gy", 1)
     above_y = from_behind(low_column, "gy", -1)
 
@@ -413,43 +440,67 @@
 
     output, grad, terms, low_edge, high_edge = call(
         functools.partial(forward_kernel, side=side),
-        [native, field, jax.ShapeDtypeStruct((ROWS, LANES), F32), rows, rows],
+        [field, field, jax.ShapeDtypeStruct((ROWS, LANES), F32), rows, rows],
         3,
-        7,
+        5,
         [
             table,
             columns,
             pltpu.VMEM((3 * channels, 20 * LANES), BF),
             carry_ref,
             pltpu.VMEM((3 * channels, 9 * channels), F32),
-            staging,
+            pltpu.VMEM(field.shape, BF),
+            sems,
         ],
         2 * flops,
-    )(cells, links, count, prepared, below_x, above_x, below_y, above_y, upstream, matrix)
-
-    below_x = passed_along(high_edge, "gx", 1)
-    above_x = passed_along(low_edge, "gx", -1)
-    low_column, high_column = make_columns(cells, grad, below_x, above_x)
-    below_y = from_behind(high_column, "gy", 1)
-    above_y = from_behind(low_column, "gy", -1)
-    grad_feats = call(
-        functools.partial(backward_kernel, side=side),
-        native,
-        2,
-        7,
-        [table, columns, carry_ref, staging],
-        flops,
-    )(links, count, grad, below_x, above_x, below_y, above_y, upstream, flipped)
-
+        n_any=2,
+    )(cells, links, count, below_x, above_x, below_y, above_y, matrix, prepared, upstream)
+
+    halos = [passed_along(high_edge, "gx", 1), passed_along(low_edge, "gx", -1)]
+    parts = []
+    done = {}
+
+    def columns_task(token):
+        low_column, high_column = make_columns(cells, tied(grad, token), *halos)
+        halos.append(from_behind(high_column, "gy", 1))
+        halos.append(from_behind(low_column, "gy", -1))
+        return low_column
+
+    def output_task(token):
+        done["output"] = call(native_kernel, native, 0, 1, [staging])(tied(output, token))
+        return done["output"]
+
+    def backward_task(group, token):
+        part = call(
+            functools.partial(backward_kernel, side=side, group=group),
+            jax.ShapeDtypeStruct((2, 8, channels, LANES), BF),
+            2,
+            5,
+            [table, columns, carry_ref, pltpu.VMEM((2, 8, channels, LANES), BF), sems],
+            4 * flops // pairs,
+            n_any=2,
+        )(links, count, *halos, flipped, tied(grad, token), upstream)
+        parts.append(part)
+        return part
+
+    def gradient_task(token):
+        first = tied(parts[0], token)
+        done["grad"] = call(native_kernel, native, 0, len(parts), [staging])(first, *parts[1:])
+        return done["grad"]
+
+    tasks = [columns_task, output_task]
+    tasks += [functools.partial(backward_task, group) for group in range(pairs // 2)]
+    tasks += [gradient_task]
     device_total = lax.axis_size("gx") * lax.axis_size("gy")
     scale = 1.0 / math.sqrt(voxels * slots * device_total)
+    whole = summed(terms, scale, dict(enumerate(tasks, 1)))
     grad_weight = call(
         functools.partial(unpack_kernel, height=3 * channels, width=9 * channels),
         jax.ShapeDtypeStruct((channels, 27 * channels), F32),
         0,
         1,
-    )(summed(terms, scale))
-    return (output.reshape(feats.shape), grad_feats.reshape(feats.shape), grad_weight)
+    )(whole)
+    return (done["output"].reshape(feats.shape), done["grad"].reshape(feats.shape), grad_weight)
 
 
 def solution(mesh):

time: 162 us -> 133 us (0.82)
  waiting for transfers between devices: 28.6 us -> 9.16 us
  starting transfers between devices: 37.4 us -> 31.9 us
  Pallas kernels: 83 us -> 77.9 us
    ppermute x10, waiting for transfers between devices: 21.2 us -> 5.76 us  [swapped(): return lax.ppermute(block, axes, [(i, i ^ bit) for i in range(devices)])]
    ppermute x4, starting transfers between devices: 19.3 us -> 12.8 us  [from_behind(): return lax.ppermute(block, axis, route)]
    pallas_call x4 -> x9, Pallas kernels: 71.8 us -> 66.8 us  [the longest x1 25.6 us: per_device(): call(functools.partial(forward_kernel, side=side), [field, field, jax.Sha...]
    ppermute x4, waiting for transfers between devices: 4.03 us -> 1.55 us  [from_behind(): return lax.ppermute(block, axis, route)]
    unnamed x26 -> x30, local copies, waits for them, and re-layouts: 2.97 us -> 4.2 us
  transfers between devices with their start and end apart: 18 -> 18, of which waited for: 11 -> 5; matrix products, arithmetic and copies ran while one was open for 3% -> 3% of each run, Pallas kernels for 20% -> 32%
where the time goes in v1:
time: 133 us; the launch traced here: 132 us
  Pallas kernels  77.9 us (59%)
  starting transfers between devices  31.9 us (24%)
  local copies, waits for them, and re-layouts  9.25 us (7%)
  waiting for transfers between devices  9.16 us (7%)
  other arithmetic  2.26 us (2%)
  between operations  1.77 us (1%)
    pallas_call x1, Pallas kernels, per_device(): call(functools.partial(forward_kernel, side=side), [field, field, jax.Sha...  25.6 us
    pallas_call x4, Pallas kernels, backward_task(): call(functools.partial(backward_kernel, side=side, group=group), jax.Shap...  25.2 us
    ppermute x4, starting transfers between devices, from_behind(): return lax.ppermute(block, axis, route)  12.8 us
    ppermute x10, starting transfers between devices, swapped(): return lax.ppermute(block, axes, [(i, i ^ bit) for i in range(devices)])  11.7 us
    ppermute x4, starting transfers between devices, passed_along(): return lax.ppermute(block, axis, route)  7.41 us
    ppermute x10, waiting for transfers between devices, swapped(): return lax.ppermute(block, axes, [(i, i ^ bit) for i in range(devices)])  5.76 us
    pallas_call x1, Pallas kernels, output_task(): call(native_kernel, native, 0, 1, [staging])(tied(output, token))  5.12 us
    pallas_call x1, Pallas kernels, gradient_task(): call(native_kernel, native, 0, len(parts), [staging])(first, *parts[1:])  4.89 us
  transfers between devices with their start and end apart: 18, of which 5 were waited for; matrix products, arithmetic and copies ran while one was open for 3% of the time, Pallas kernels for 32%

profile of v1, /device:TPU:1, one launch (start us, length us, event | category | flops | bytes accessed | tf_op | source)
XLA Modules:
  0.0 132.3 jit_solution(1481519564257823380)
XLA Ops:
  0.6 4.5 %shard_map.85 = (bf16[8,8,96,128]{3,2,1,0:T(8,128)(2,1)}, bf16[3,96,128]{2,1,0:T(8,128)(2,1)}, bf16[3,96,128]{2,1,0:T(8,128)(2,1)}) custom-call(s32[36]{0:T(128)} %bitcast.29, bf16[96,16,512]{2,1,0:T(8,128)(2,1)} %bitcast.24), custom_call_target="tpu_custom_call" | custom-call | bytes 4194304 | tf_op jit(solution)/shard_map/pallas_call | solution.py:423
  5.2 2.1 %collective-permute-start = (bf16[3,96,128]{2,1,0:T(8,128)(2,1)}, bf16[3,96,128]{2,1,0:T(8,128)(2,1)S(1)}, u32[]{:S(2)}, u32[]{:S(2)}) collective-permute-start(bf16[3,96,128]{2,1,0:T(8,128)(2,1)} %get-tuple-element.30), channel_id=1, source_target_pairs={{24,0},{0,8},{8,16},{16,24},{25,1},{1,9},{9,17},{17,25},{26,2},{2,... | collective-permute-start | bytes 221192 | tf_op jit(solution)/shard_map/ppermute | solution.py:24
  7.3 2.0 %collective-permute-start.1 = (bf16[3,96,128]{2,1,0:T(8,128)(2,1)}, bf16[3,96,128]{2,1,0:T(8,128)(2,1)S(1)}, u32[]{:S(2)}, u32[]{:S(2)}) collective-permute-start(bf16[3,96,128]{2,1,0:T(8,128)(2,1)} %get-tuple-element.31), channel_id=1, source_target_pairs={{8,0},{16,8},{24,16},{0,24},{9,1},{17,9},{25,17},{1,25},{10,2},{18... | collective-permute-start | bytes 221192 | tf_op jit(solution)/shard_map/ppermute | solution.py:24
  9.3 4.4 %shard_map.86.given = bf16[8,8,96,128]{3,2,1,0:T(8,128)(2,1)} custom-call(bf16[96,16,512]{2,1,0:T(8,128)(2,1)} %bitcast.25), custom_call_target="tpu_custom_call" | custom-call | bytes 4194304 | tf_op jit(solution)/shard_map/pallas_call | solution.py:428
  13.7 0.0 collective-permute-done.below.below_x
  13.7 0.0 collective-permute-done.1.above.above_x
  13.8 0.6 copy-done.3
  14.4 0.6 copy-done.4
  15.0 3.0 %shard_map.87 = (bf16[4,96,128]{2,1,0:T(8,128)(2,1)}, bf16[4,96,128]{2,1,0:T(8,128)(2,1)}) custom-call(s32[36]{0:T(128)} %bitcast.30, bf16[8,8,96,128]{3,2,1,0:T(8,128)(2,1)} %get-tuple-element.33.field, bf16[3,96,128]{2,1,0:T(8,128)(2,1)} %copy-done.3, bf16[3,96,128]{2,1,0:T(8,128)(2,1)} %copy-done.4), custom_call_target="tpu_custom_call" | custom-call | bytes 4194304 | tf_op jit(solution)/shard_map/pallas_call | solution.py:432
  18.0 4.2 %collective-permute-start.2 = (bf16[4,96,128]{2,1,0:T(8,128)(2,1)}, bf16[4,96,128]{2,1,0:T(8,128)(2,1)S(1)}, u32[]{:S(2)}, u32[]{:S(2)}) collective-permute-start(bf16[4,96,128]{2,1,0:T(8,128)(2,1)} %get-tuple-element.34), channel_id=1, source_target_pairs={{0,1},{1,2},{2,3},{3,4},{4,5},{5,6},{6,7},{8,9},{9,10},{10,11},{11... | collective-permute-start | bytes 294920 | tf_op jit(solution)/shard_map/ppermute | solution.py:30
  22.2 1.9 %collective-permute-start.3 = (bf16[4,96,128]{2,1,0:T(8,128)(2,1)}, bf16[4,96,128]{2,1,0:T(8,128)(2,1)S(1)}, u32[]{:S(2)}, u32[]{:S(2)}) collective-permute-start(bf16[4,96,128]{2,1,0:T(8,128)(2,1)} %get-tuple-element.35), channel_id=1, source_target_pairs={{1,0},{2,1},{3,2},{4,3},{5,4},{6,5},{7,6},{9,8},{10,9},{11,10},{12... | collective-permute-start | bytes 294920 | tf_op jit(solution)/shard_map/ppermute | solution.py:30
  24.1 0.1 copy.13
  24.2 0.7 reshape.43.links
  25.6 0.4 reshape.47
  26.0 0.8 copy.14
  26.8 0.0 collective-permute-done.2.below_y
  26.8 1.5 %collective-permute-done.3.above_y = bf16[4,96,128]{2,1,0:T(8,128)(2,1)S(1)} collective-permute-done((bf16[4,96,128]{2,1,0:T(8,128)(2,1)}, bf16[4,96,128]{2,1,0:T(8,128)(2,1)S(1)}, u32[]{:S(2)}, u32[]{:S(2)}) %collective-permute-start.3) | collective-permute-done | bytes 98336 | tf_op jit(solution)/shard_map/ppermute | solution.py:30
  28.3 0.6 copy-done.11
  29.0 25.6 %shard_map.88 = (bf16[8,8,96,128]{3,2,1,0:T(8,128)(2,1)}, bf16[8,8,96,128]{3,2,1,0:T(8,128)(2,1)}, f32[2048,128]{1,0:T(8,128)}, bf16[3,96,128]{2,1,0:T(8,128)(2,1)}, bf16[3,96,128]{2,1,0:T(8,128)(2,1)}) custom-call(s32[36]{0:T(128)} %bitcast.31, s32[128]{0:T(128)} %reshape.43.links, s32[1]{0:T(128)} %bitcast.16.counts, bf16[3,96,128]{2,1,0:T(8,128)(2,1)} %copy-done.3, ...), custom_call_target="tpu_custom_call" | custom-call | flops 8153726976 | bytes 4194304 | tf_op jit(solution)/shard_map/pallas_call | solution.py:441
  54.6 1.1 constant_dynamic-slice_fusion.4
  55.7 0.1 collective-permute-start.4
  55.8 1.9 %collective-permute-done.4 = f32[1024,128]{1,0:T(8,128)S(1)} collective-permute-done((f32[1024,128]{1,0:T(8,128)S(1)}, f32[1024,128]{1,0:T(8,128)S(1)}, u32[]{:S(2)}, u32[]{:S(2)}) %collective-permute-start.4) | collective-permute-done | bytes 524320 | tf_op jit(solution)/shard_map/ppermute | solution.py:380
  57.7 1.1 dynamic-slice_add_fusion
  58.8 2.2 %collective-permute-start.5 = (f32[512,128]{1,0:T(8,128)S(1)}, f32[512,128]{1,0:T(8,128)S(1)}, u32[]{:S(2)}, u32[]{:S(2)}) collective-permute-start(f32[512,128]{1,0:T(8,128)S(1)} %constant_dynamic-slice_fusion.3), channel_id=1, source_target_pairs={{0,2},{1,3},{2,0},{3,1},{4,6},{5,7},{6,4},{7,5},{8,10},{9,11},{10,... | collective-permute-start | bytes 786440 | tf_op jit(solution)/shard_map/ppermute | solution.py:380
  61.0 3.3 %collective-permute-start.7 = (bf16[3,96,128]{2,1,0:T(8,128)(2,1)S(1)}, bf16[3,96,128]{2,1,0:T(8,128)(2,1)S(1)}, u32[]{:S(2)}, u32[]{:S(2)}) collective-permute-start(bf16[3,96,128]{2,1,0:T(8,128)(2,1)S(1)} %copy-done.12), channel_id=1, source_target_pairs={{8,0},{16,8},{24,16},{0,24},{9,1},{17,9},{25,17},{1,25},{10,2},{18... | collective-permute-start | bytes 221192 | tf_op jit(solution)/shard_map/ppermute | solution.py:24
  64.3 1.8 %collective-permute-done.6.below.below_x = bf16[3,96,128]{2,1,0:T(8,128)(2,1)S(1)} collective-permute-done((bf16[3,96,128]{2,1,0:T(8,128)(2,1)S(1)}, bf16[3,96,128]{2,1,0:T(8,128)(2,1)S(1)}, u32[]{:S(2)}, u32[]{:S(2)}) %collective-permute-start.6) | collective-permute-done | bytes 73760 | tf_op jit(solution)/shard_map/ppermute | solution.py:24
  66.1 0.0 collective-permute-done.7.above.above_x
  66.1 0.6 copy-done.1
  66.7 0.6 copy-done.2
  67.4 3.0 %shard_map.89 = (bf16[4,96,128]{2,1,0:T(8,128)(2,1)}, bf16[4,96,128]{2,1,0:T(8,128)(2,1)}) custom-call(s32[36]{0:T(128)} %bitcast.32, bf16[8,8,96,128]{3,2,1,0:T(8,128)(2,1)} %get-tuple-element.53.field, bf16[3,96,128]{2,1,0:T(8,128)(2,1)} %copy-done.1, bf16[3,96,128]{2,1,0:T(8,128)(2,1)} %copy-done.2), custom_call_target="tpu_custom_call" | custom-call | bytes 4194304 | tf_op jit(solution)/shard_map/pallas_call | solution.py:464
  70.4 0.0 collective-permute-done.5
  70.4 0.1 collective-permute-start.10
  70.5 0.3 copy.15
  71.0 0.0 copy-start.6
  71.0 0.0 copy-start.7
  71.0 0.3 copy.25
  71.3 1.6 %reshape.54.matrix = bf16[288,864]{1,0:T(8,128)(2,1)} reshape(bf16[3,96,9,96]{3,2,1,0:T(8,128)(2,1)S(1)} %copy.25) | data formatting | bytes 995328 | tf_op jit(solution)/shard_map/reshape | solution.py:439
  72.9 4.1 %collective-permute-start.9 = (bf16[4,96,128]{2,1,0:T(8,128)(2,1)S(1)}, bf16[4,96,128]{2,1,0:T(8,128)(2,1)S(1)}, u32[]{:S(2)}, u32[]{:S(2)}) collective-permute-start(bf16[4,96,128]{2,1,0:T(8,128)(2,1)S(1)} %copy-done.6), channel_id=1, source_target_pairs={{1,0},{2,1},{3,2},{4,3},{5,4},{6,5},{7,6},{9,8},{10,9},{11,10},{12... | collective-permute-start | bytes 294920 | tf_op jit(solution)/shard_map/ppermute | solution.py:30
  77.0 2.7 %collective-permute-start.8 = (bf16[4,96,128]{2,1,0:T(8,128)(2,1)S(1)}, bf16[4,96,128]{2,1,0:T(8,128)(2,1)S(1)}, u32[]{:S(2)}, u32[]{:S(2)}) collective-permute-start(bf16[4,96,128]{2,1,0:T(8,128)(2,1)S(1)} %copy-done.7), channel_id=1, source_target_pairs={{0,1},{1,2},{2,3},{3,4},{4,5},{5,6},{6,7},{8,9},{9,10},{10,11},{11... | collective-permute-start | bytes 294920 | tf_op jit(solution)/shard_map/ppermute | solution.py:30
  79.7 5.1 %shard_map.90 = bf16[96,16,512]{2,1,0:T(8,128)(2,1)} custom-call(bf16[8,8,96,128]{3,2,1,0:T(8,128)(2,1)} %get-tuple-element.44.refs_0_), custom_call_target="tpu_custom_call" | custom-call | bytes 4194304 | tf_op jit(solution)/shard_map/pallas_call | solution.py:470
  84.8 0.1 collective-permute-start.11
  84.9 0.0 collective-permute-done.8.below_y
  84.9 0.0 copy-start.10
  84.9 0.0 collective-permute-done.9.above_y
  84.9 0.6 copy-done.10
  85.6 0.0 copy-done.8
  85.6 6.3 %shard_map.91.refs_0_ = bf16[2,8,96,128]{3,2,1,0:T(8,128)(2,1)} custom-call(s32[128]{0:T(128)} %reshape.43.links, s32[1]{0:T(128)} %bitcast.17.counts, bf16[3,96,128]{2,1,0:T(8,128)(2,1)} %copy-done.1, bf16[3,96,128]{2,1,0:T(8,128)(2,1)} %copy-done.2, bf16[4,96,128]{2,1,0:T(8,128)(2,1)} %copy-done.10, bf16[4,96,128]{2,1,0:T(8,128)(2,1)} %copy-done.8, ...), custom_call_target="tpu_custom_call" | custom-call | flops 2038431744 | bytes 4194304 | tf_op jit(solution)/shard_map/pallas_call | solution.py:474
  91.9 2.6 %collective-permute-start.12 = (f32[64,128]{1,0:T(8,128)S(1)}, f32[64,128]{1,0:T(8,128)S(1)}, u32[]{:S(2)}, u32[]{:S(2)}) collective-permute-start(f32[64,128]{1,0:T(8,128)S(1)} %constant_dynamic-slice_fusion), channel_id=1, source_target_pairs={{0,16},{1,17},{2,18},{3,19},{4,20},{5,21},{6,22},{7,23},{8,24},{9,... | collective-permute-start | bytes 98312 | tf_op jit(solution)/shard_map/ppermute | solution.py:380
  94.5 6.3 %shard_map.92.refs_1_ = bf16[2,8,96,128]{3,2,1,0:T(8,128)(2,1)} custom-call(s32[128]{0:T(128)} %reshape.43.links, s32[1]{0:T(128)} %bitcast.18.counts, bf16[3,96,128]{2,1,0:T(8,128)(2,1)} %copy-done.1, bf16[3,96,128]{2,1,0:T(8,128)(2,1)} %copy-done.2, bf16[4,96,128]{2,1,0:T(8,128)(2,1)} %copy-done.10, bf16[4,96,128]{2,1,0:T(8,128)(2,1)} %copy-done.8, ...), custom_call_target="tpu_custom_call" | custom-call | flops 2038431744 | bytes 4194304 | tf_op jit(solution)/shard_map/pallas_call | solution.py:474
  100.8 0.1 collective-permute-start.13
  100.9 6.3 %shard_map.93.refs_2_ = bf16[2,8,96,128]{3,2,1,0:T(8,128)(2,1)} custom-call(s32[128]{0:T(128)} %reshape.43.links, s32[1]{0:T(128)} %bitcast.19.counts, bf16[3,96,128]{2,1,0:T(8,128)(2,1)} %copy-done.1, bf16[3,96,128]{2,1,0:T(8,128)(2,1)} %copy-done.2, bf16[4,96,128]{2,1,0:T(8,128)(2,1)} %copy-done.10, bf16[4,96,128]{2,1,0:T(8,128)(2,1)} %copy-done.8, ...), custom_call_target="tpu_custom_call" | custom-call | flops 2038431744 | bytes 4194304 | tf_op jit(solution)/shard_map/pallas_call | solution.py:474
  107.2 0.0 collective-permute-done.13
  107.3 1.4 %collective-permute-start.14 = (bf16[128,128]{1,0:T(8,128)(2,1)S(1)}, bf16[128,128]{1,0:T(8,128)(2,1)S(1)}, u32[]{:S(2)}, u32[]{:S(2)}) collective-permute-start(bf16[128,128]{1,0:T(8,128)(2,1)S(1)} %maximum_select_fusion.4), channel_id=1, source_target_pairs={{0,8},{1,9},{2,10},{3,11},{4,12},{5,13},{6,14},{7,15},{8,0},{9,1},... | collective-permute-start | bytes 98312 | tf_op jit(solution)/shard_map/ppermute | solution.py:380
  108.6 6.3 %shard_map.94.refs_3_ = bf16[2,8,96,128]{3,2,1,0:T(8,128)(2,1)} custom-call(s32[128]{0:T(128)} %reshape.43.links, s32[1]{0:T(128)} %bitcast.20.counts, bf16[3,96,128]{2,1,0:T(8,128)(2,1)} %copy-done.1, bf16[3,96,128]{2,1,0:T(8,128)(2,1)} %copy-done.2, bf16[4,96,128]{2,1,0:T(8,128)(2,1)} %copy-done.10, bf16[4,96,128]{2,1,0:T(8,128)(2,1)} %copy-done.8, ...), custom_call_target="tpu_custom_call" | custom-call | flops 2038431744 | bytes 4194304 | tf_op jit(solution)/shard_map/pallas_call | solution.py:474
  115.0 1.1 collective-permute-start.15
  116.0 4.9 %shard_map.95 = bf16[96,16,512]{2,1,0:T(8,128)(2,1)} custom-call(bf16[2,8,96,128]{3,2,1,0:T(8,128)(2,1)} %shard_map.91.refs_0_, bf16[2,8,96,128]{3,2,1,0:T(8,128)(2,1)} %shard_map.92.refs_1_, bf16[2,8,96,128]{3,2,1,0:T(8,128)(2,1)} %shard_map.93.refs_2_, bf16[2,8,96,128]{3,2,1,0:T(8,128)(2,1)} %shard_map.94.refs_3_), custom_call_target="tpu_custom_call" | custom-call | bytes 4194304 | tf_op jit(solution)/shard_map/pallas_call | solution.py:488
  120.9 0.0 collective-permute-done.15
  121.0 1.2 collective-permute-start.16
  122.1 2.7 %collective-permute-done.16 = bf16[512,128]{1,0:T(8,128)(2,1)S(1)} collective-permute-done((bf16[512,128]{1,0:T(8,128)(2,1)S(1)}, bf16[512,128]{1,0:T(8,128)(2,1)S(1)}, u32[]{:S(2)}, u32[]{:S(2)}) %collective-permute-start.16) | collective-permute-done | bytes 131104 | tf_op jit(solution)/shard_map/ppermute | solution.py:380
  124.9 0.1 maximum_select_fusion.1
  124.9 3.1 %collective-permute-start.17 = (bf16[1024,128]{1,0:T(8,128)(2,1)S(1)}, bf16[1024,128]{1,0:T(8,128)(2,1)S(1)}, u32[]{:S(2)}, u32[]{:S(2)}) collective-permute-start(bf16[1024,128]{1,0:T(8,128)(2,1)S(1)} %maximum_select_fusion.1), channel_id=1, source_target_pairs={{0,1},{1,0},{2,3},{3,2},{4,5},{5,4},{6,7},{7,6},{8,9},{9,8},{10,11... | collective-permute-start | bytes 786440 | tf_op jit(solution)/shard_map/ppermute | solution.py:380
  128.1 1.2 collective-permute-done.17
  129.2 0.9 maximum_select_fusion.source
  130.1 2.2 %shard_map.96 = f32[96,2592]{1,0:T(8,128)} custom-call(bf16[2048,128]{1,0:T(8,128)(2,1)} %maximum_select_fusion.source), custom_call_target="tpu_custom_call" | custom-call | bytes 4194304 | tf_op jit(solution)/shard_map/pallas_call | solution.py:497
  (35 shorter events, 0.3 us)
Async XLA Ops:
  5.2 8.6 %collective-permute-start = (bf16[3,96,128]{2,1,0:T(8,128)(2,1)}, bf16[3,96,128]{2,1,0:T(8,128)(2,1)S(1)}, u32[]{:S(2)}, u32[]{:S(2)}) collective-permute-start(bf16[3,96,128]{2,1,0:T(8,128)(2,1)} %get-tuple-element.30), channel_id=1, source_target_pairs={{24,0},{0,8},{8,16},{16,24},{25,1},{1,9},{9,17},{17,25},{26,2},{2,... | collective-permute-start | bytes 221192 | tf_op jit(solution)/shard_map/ppermute | solution.py:24
  7.3 6.5 %collective-permute-start.1 = (bf16[3,96,128]{2,1,0:T(8,128)(2,1)}, bf16[3,96,128]{2,1,0:T(8,128)(2,1)S(1)}, u32[]{:S(2)}, u32[]{:S(2)}) collective-permute-start(bf16[3,96,128]{2,1,0:T(8,128)(2,1)} %get-tuple-element.31), channel_id=1, source_target_pairs={{8,0},{16,8},{24,16},{0,24},{9,1},{17,9},{25,17},{1,25},{10,2},{18... | collective-permute-start | bytes 221192 | tf_op jit(solution)/shard_map/ppermute | solution.py:24
  13.7 10.4 %copy-start.5 = (s32[1,16,8]{1,2,0:T(8,128)S(1)}, s32[1,16,8]{1,2,0:T(8,128)}, u32[]{:S(2)}) copy-start(s32[1,16,8]{1,2,0:T(8,128)} %param.10) | copy-start | bytes 1540
  13.7 11.8 %copy-start = (bf16[96,2592]{1,0:T(8,128)(2,1)S(1)}, bf16[96,2592]{1,0:T(8,128)(2,1)}, u32[]{:S(2)}) copy-start(bf16[96,2592]{1,0:T(8,128)(2,1)} %param.8) | copy-start | bytes 1492996
  13.7 0.6 copy-start.3
  14.4 0.6 copy-start.4
  18.0 8.8 %collective-permute-start.2 = (bf16[4,96,128]{2,1,0:T(8,128)(2,1)}, bf16[4,96,128]{2,1,0:T(8,128)(2,1)S(1)}, u32[]{:S(2)}, u32[]{:S(2)}) collective-permute-start(bf16[4,96,128]{2,1,0:T(8,128)(2,1)} %get-tuple-element.34), channel_id=1, source_target_pairs={{0,1},{1,2},{2,3},{3,4},{4,5},{5,6},{6,7},{8,9},{9,10},{10,11},{11... | collective-permute-start | bytes 294920 | tf_op jit(solution)/shard_map/ppermute | solution.py:30
  22.2 6.1 %collective-permute-start.3 = (bf16[4,96,128]{2,1,0:T(8,128)(2,1)}, bf16[4,96,128]{2,1,0:T(8,128)(2,1)S(1)}, u32[]{:S(2)}, u32[]{:S(2)}) collective-permute-start(bf16[4,96,128]{2,1,0:T(8,128)(2,1)} %get-tuple-element.35), channel_id=1, source_target_pairs={{1,0},{2,1},{3,2},{4,3},{5,4},{6,5},{7,6},{9,8},{10,9},{11,10},{12... | collective-permute-start | bytes 294920 | tf_op jit(solution)/shard_map/ppermute | solution.py:30
  26.8 1.5 %copy-start.9 = (bf16[4,96,128]{2,1,0:T(8,128)(2,1)}, bf16[4,96,128]{2,1,0:T(8,128)(2,1)S(1)}, u32[]{:S(2)}) copy-start(bf16[4,96,128]{2,1,0:T(8,128)(2,1)S(1)} %collective-permute-done.2.below_y) | copy-start | bytes 294916
  28.3 0.6 copy-start.11
  54.6 6.4 %copy-start.13 = (bf16[3,96,128]{2,1,0:T(8,128)(2,1)S(1)}, bf16[3,96,128]{2,1,0:T(8,128)(2,1)}, u32[]{:S(2)}) copy-start(bf16[3,96,128]{2,1,0:T(8,128)(2,1)} %get-tuple-element.40) | copy-start | bytes 221188
  54.6 6.4 %copy-start.12 = (bf16[3,96,128]{2,1,0:T(8,128)(2,1)S(1)}, bf16[3,96,128]{2,1,0:T(8,128)(2,1)}, u32[]{:S(2)}) copy-start(bf16[3,96,128]{2,1,0:T(8,128)(2,1)} %get-tuple-element.41) | copy-start | bytes 221188
  55.7 2.0 %collective-permute-start.4 = (f32[1024,128]{1,0:T(8,128)S(1)}, f32[1024,128]{1,0:T(8,128)S(1)}, u32[]{:S(2)}, u32[]{:S(2)}) collective-permute-start(f32[1024,128]{1,0:T(8,128)S(1)} %constant_dynamic-slice_fusion.4), channel_id=1, source_target_pairs={{0,1},{1,0},{2,3},{3,2},{4,5},{5,4},{6,7},{7,6},{8,9},{9,8},{10,11... | collective-permute-start | bytes 1572872 | tf_op jit(solution)/shard_map/ppermute | solution.py:380
  58.8 11.6 %collective-permute-start.5 = (f32[512,128]{1,0:T(8,128)S(1)}, f32[512,128]{1,0:T(8,128)S(1)}, u32[]{:S(2)}, u32[]{:S(2)}) collective-permute-start(f32[512,128]{1,0:T(8,128)S(1)} %constant_dynamic-slice_fusion.3), channel_id=1, source_target_pairs={{0,2},{1,3},{2,0},{3,1},{4,6},{5,7},{6,4},{7,5},{8,10},{9,11},{10,... | collective-permute-start | bytes 786440 | tf_op jit(solution)/shard_map/ppermute | solution.py:380
  61.0 5.1 %collective-permute-start.6 = (bf16[3,96,128]{2,1,0:T(8,128)(2,1)S(1)}, bf16[3,96,128]{2,1,0:T(8,128)(2,1)S(1)}, u32[]{:S(2)}, u32[]{:S(2)}) collective-permute-start(bf16[3,96,128]{2,1,0:T(8,128)(2,1)S(1)} %copy-done.13), channel_id=1, source_target_pairs={{24,0},{0,8},{8,16},{16,24},{25,1},{1,9},{9,17},{17,25},{26,2},{2,... | collective-permute-start | bytes 221192 | tf_op jit(solution)/shard_map/ppermute | solution.py:24
  61.0 5.1 %collective-permute-start.7 = (bf16[3,96,128]{2,1,0:T(8,128)(2,1)S(1)}, bf16[3,96,128]{2,1,0:T(8,128)(2,1)S(1)}, u32[]{:S(2)}, u32[]{:S(2)}) collective-permute-start(bf16[3,96,128]{2,1,0:T(8,128)(2,1)S(1)} %copy-done.12), channel_id=1, source_target_pairs={{8,0},{16,8},{24,16},{0,24},{9,1},{17,9},{25,17},{1,25},{10,2},{18... | collective-permute-start | bytes 221192 | tf_op jit(solution)/shard_map/ppermute | solution.py:24
  66.1 0.6 copy-start.1
  66.7 0.6 copy-start.2
  70.4 14.3 %collective-permute-start.10 = (f32[256,128]{1,0:T(8,128)S(1)}, f32[256,128]{1,0:T(8,128)S(1)}, u32[]{:S(2)}, u32[]{:S(2)}) collective-permute-start(f32[256,128]{1,0:T(8,128)S(1)} %constant_dynamic-slice_fusion.2), channel_id=1, source_target_pairs={{0,4},{1,5},{2,6},{3,7},{4,0},{5,1},{6,2},{7,3},{8,12},{9,13},{10,... | collective-permute-start | bytes 393224 | tf_op jit(solution)/shard_map/ppermute | solution.py:380
  71.0 1.9 %copy-start.6 = (bf16[4,96,128]{2,1,0:T(8,128)(2,1)S(1)}, bf16[4,96,128]{2,1,0:T(8,128)(2,1)}, u32[]{:S(2)}) copy-start(bf16[4,96,128]{2,1,0:T(8,128)(2,1)} %get-tuple-element.42) | copy-start | bytes 294916
  71.0 6.0 %copy-start.7 = (bf16[4,96,128]{2,1,0:T(8,128)(2,1)S(1)}, bf16[4,96,128]{2,1,0:T(8,128)(2,1)}, u32[]{:S(2)}) copy-start(bf16[4,96,128]{2,1,0:T(8,128)(2,1)} %get-tuple-element.45) | copy-start | bytes 294916
  72.9 12.0 %collective-permute-start.9 = (bf16[4,96,128]{2,1,0:T(8,128)(2,1)S(1)}, bf16[4,96,128]{2,1,0:T(8,128)(2,1)S(1)}, u32[]{:S(2)}, u32[]{:S(2)}) collective-permute-start(bf16[4,96,128]{2,1,0:T(8,128)(2,1)S(1)} %copy-done.6), channel_id=1, source_target_pairs={{1,0},{2,1},{3,2},{4,3},{5,4},{6,5},{7,6},{9,8},{10,9},{11,10},{12... | collective-permute-start | bytes 294920 | tf_op jit(solution)/shard_map/ppermute | solution.py:30
  77.0 7.9 %collective-permute-start.8 = (bf16[4,96,128]{2,1,0:T(8,128)(2,1)S(1)}, bf16[4,96,128]{2,1,0:T(8,128)(2,1)S(1)}, u32[]{:S(2)}, u32[]{:S(2)}) collective-permute-start(bf16[4,96,128]{2,1,0:T(8,128)(2,1)S(1)} %copy-done.7), channel_id=1, source_target_pairs={{0,1},{1,2},{2,3},{3,4},{4,5},{5,6},{6,7},{8,9},{9,10},{10,11},{11... | collective-permute-start | bytes 294920 | tf_op jit(solution)/shard_map/ppermute | solution.py:30
  84.8 7.1 %collective-permute-start.11 = (f32[128,128]{1,0:T(8,128)S(1)}, f32[128,128]{1,0:T(8,128)S(1)}, u32[]{:S(2)}, u32[]{:S(2)}) collective-permute-start(f32[128,128]{1,0:T(8,128)S(1)} %constant_dynamic-slice_fusion.1), channel_id=1, source_target_pairs={{0,8},{1,9},{2,10},{3,11},{4,12},{5,13},{6,14},{7,15},{8,0},{9,1},... | collective-permute-start | bytes 196616 | tf_op jit(solution)/shard_map/ppermute | solution.py:380
  84.9 0.6 copy-start.10
  84.9 0.6 copy-start.8
  91.9 8.9 %collective-permute-start.12 = (f32[64,128]{1,0:T(8,128)S(1)}, f32[64,128]{1,0:T(8,128)S(1)}, u32[]{:S(2)}, u32[]{:S(2)}) collective-permute-start(f32[64,128]{1,0:T(8,128)S(1)} %constant_dynamic-slice_fusion), channel_id=1, source_target_pairs={{0,16},{1,17},{2,18},{3,19},{4,20},{5,21},{6,22},{7,23},{8,24},{9,... | collective-permute-start | bytes 98312 | tf_op jit(solution)/shard_map/ppermute | solution.py:380
  100.8 6.4 %collective-permute-start.13 = (bf16[64,128]{1,0:T(8,128)(2,1)S(1)}, bf16[64,128]{1,0:T(8,128)(2,1)S(1)}, u32[]{:S(2)}, u32[]{:S(2)}) collective-permute-start(bf16[64,128]{1,0:T(8,128)(2,1)S(1)} %multiply_convert_fusion), channel_id=1, source_target_pairs={{0,16},{1,17},{2,18},{3,19},{4,20},{5,21},{6,22},{7,23},{8,24},{9,... | collective-permute-start | bytes 49160 | tf_op jit(solution)/shard_map/ppermute | solution.py:380
  107.3 7.7 %collective-permute-start.14 = (bf16[128,128]{1,0:T(8,128)(2,1)S(1)}, bf16[128,128]{1,0:T(8,128)(2,1)S(1)}, u32[]{:S(2)}, u32[]{:S(2)}) collective-permute-start(bf16[128,128]{1,0:T(8,128)(2,1)S(1)} %maximum_select_fusion.4), channel_id=1, source_target_pairs={{0,8},{1,9},{2,10},{3,11},{4,12},{5,13},{6,14},{7,15},{8,0},{9,1},... | collective-permute-start | bytes 98312 | tf_op jit(solution)/shard_map/ppermute | solution.py:380
  115.0 5.9 %collective-permute-start.15 = (bf16[256,128]{1,0:T(8,128)(2,1)S(1)}, bf16[256,128]{1,0:T(8,128)(2,1)S(1)}, u32[]{:S(2)}, u32[]{:S(2)}) collective-permute-start(bf16[256,128]{1,0:T(8,128)(2,1)S(1)} %maximum_select_fusion.3), channel_id=1, source_target_pairs={{0,4},{1,5},{2,6},{3,7},{4,0},{5,1},{6,2},{7,3},{8,12},{9,13},{10,... | collective-permute-start | bytes 196616 | tf_op jit(solution)/shard_map/ppermute | solution.py:380
  121.0 3.9 %collective-permute-start.16 = (bf16[512,128]{1,0:T(8,128)(2,1)S(1)}, bf16[512,128]{1,0:T(8,128)(2,1)S(1)}, u32[]{:S(2)}, u32[]{:S(2)}) collective-permute-start(bf16[512,128]{1,0:T(8,128)(2,1)S(1)} %maximum_select_fusion.2), channel_id=1, source_target_pairs={{0,2},{1,3},{2,0},{3,1},{4,6},{5,7},{6,4},{7,5},{8,10},{9,11},{10,... | collective-permute-start | bytes 393224 | tf_op jit(solution)/shard_map/ppermute | solution.py:380
  124.9 4.3 %collective-permute-start.17 = (bf16[1024,128]{1,0:T(8,128)(2,1)S(1)}, bf16[1024,128]{1,0:T(8,128)(2,1)S(1)}, u32[]{:S(2)}, u32[]{:S(2)}) collective-permute-start(bf16[1024,128]{1,0:T(8,128)(2,1)S(1)} %maximum_select_fusion.1), channel_id=1, source_target_pairs={{0,1},{1,0},{2,3},{3,2},{4,5},{5,4},{6,7},{7,6},{8,9},{9,8},{10,11... | collective-permute-start | bytes 786440 | tf_op jit(solution)/shard_map/ppermute | solution.py:380

commit v2 on v1

--- a/solution.py
+++ b/solution.py
@@ -42,22 +42,15 @@
     return jnp.zeros_like(value)
 
 
-def load_pairs(source, staging, target):
+def load_pairs(source, target):
     channels, slots, _ = source.shape
     low = lane_ids(channels) < HALF
     for tile in range(4):
-        piece = source[:, :, tile * LANES : (tile + 1) * LANES].astype(F32)
-        staging[tile] = piece.reshape(channels * slots, LANES)
-
-    def body(pair, carry):
-        for tile in range(4):
-            first = staging[tile, pl.ds(2 * pair, channels, stride=slots), :].astype(BF)
-            second = staging[tile, pl.ds(2 * pair + 1, channels, stride=slots), :].astype(BF)
+        rows = jnp.swapaxes(source[:, :, tile * LANES : (tile + 1) * LANES], 0, 1)
+        for pair in range(slots // 2):
+            first, second = rows[2 * pair], rows[2 * pair + 1]
             target[pair, 2 * tile] = jnp.where(low, first, turn(second, HALF))
             target[pair, 2 * tile + 1] = jnp.where(low, turn(first, HALF), second)
-        return carry
-
-    lax.fori_loop(0, slots // 2, body, 0)
 
 
 def edge_rows(cells, field, low_out, high_out, slots, side):
@@ -74,13 +67,26 @@
             out[tile] = jnp.where(low, parts[0], parts[1])
 
 
-def prepare_kernel(cells, feats, pairs, low_out, high_out, staging, *, side):
-    load_pairs(feats, staging, pairs)
+def prepare_kernel(cells, feats, pairs, low_out, high_out, *, side):
+    load_pairs(feats, pairs)
     edge_rows(cells, pairs, low_out, high_out, feats.shape[1], side)
 
 
-def regroup_kernel(source, pairs, staging):
-    load_pairs(source, staging, pairs)
+def regroup_kernel(source, pairs):
+    load_pairs(source, pairs)
+
+
+def weights_kernel(weight, matrix, flipped):
+    channels = weight.shape[0]
+    width = 9 * channels
+    for a in range(3):
+        rows = slice(a * channels, (a + 1) * channels)
+        matrix[rows, :] = weight[:, a * width : (a + 1) * width]
+        blocks = []
+        for bc in range(9):
+            tap = 26 - (a * 9 + bc)
+            blocks.append(weight[:, tap * channels : (tap + 1) * channels].T)
+        flipped[rows, :] = jnp.concatenate(blocks, axis=1)
 
 
 def column_kernel(cells, field, below, above, low_out, high_out, *, side):
@@ -165,7 +171,7 @@
             ):
                 column = {-1: 7, 0: None, 1: 0}[dy]
                 goal = part * HALF + (56 if dy == 1 else 0)
-                tile, lane = locate(links[slot * 8 + k], pairs, side, column)
+                tile, lane = locate(links[k, slot], pairs, side, column)
                 spots[h, part, dx, dy] = tile, (goal + LANES - lane) % LANES
 
     def fetch(layer, h, dx, dy):
@@ -228,27 +234,10 @@
             carry_ref[:, width:] = first[:, width:]
 
 
-def store_slots(staging, t, pair, slots, even, odd):
-    channels = even.shape[0]
-    low = lane_ids(channels) < HALF
-    first = jnp.where(low, even, turn(odd, HALF))
-    second = jnp.where(low, turn(even, HALF), odd)
-    staging[t, pl.ds(2 * pair, channels, stride=slots), :] = first.astype(F32)
-    staging[t, pl.ds(2 * pair + 1, channels, stride=slots), :] = second.astype(F32)
-
-
-def write_out(staging, out):
-    channels, slots, _ = out.shape
-    for tile in range(4):
-        out[:, :, tile * LANES : (tile + 1) * LANES] = (
-            staging[tile].reshape(channels, slots, LANES).astype(BF)
-        )
-
-
 def forward_kernel(
-    cells, links, counts, below_x, above_x, below_y, above_y, matrix, field, given,
-    out, grad, terms, low_out, high_out,
-    table, columns, shifted, carry_ref, total, upstream, sems, *, side,
+    cells, links, counts, mine, below_x, above_x, below_y, above_y, matrix, field, given,
+    out, grad, kept, sent, low_out, high_out,
+    table, columns, shifted, carry_ref, total, terms, upstream, sems, *, side,
 ):
     pairs, _, channels, _ = field.shape
     slots = 2 * pairs
@@ -299,6 +288,9 @@
         terms[tile * height : (tile + 1) * height, : end - tile * LANES] = total[
             :, tile * LANES : end
         ]
+    half = kept.shape[0]
+    kept[...] = terms[pl.ds(pl.multiple_of(mine[0] * half, half), half), :]
+    sent[...] = terms[pl.ds(pl.multiple_of((1 - mine[0]) * half, half), half), :]
     edge_rows(cells, grad, low_out, high_out, slots, side)
 
 
@@ -326,80 +318,115 @@
 
 
 def native_kernel(*refs):
-    *parts, out, staging = refs
-    slots = out.shape[1]
-    count = parts[0].shape[0]
-    for index, part in enumerate(parts):
-
-        def body(pair, carry, index=index, part=part):
-            for t in range(4):
+    *parts, out = refs
+    low = lane_ids(out.shape[0]) < HALF
+    for t in range(4):
+        rows = []
+        for part in parts:
+            for pair in range(part.shape[0]):
                 even, odd = part[pair, 2 * t], part[pair, 2 * t + 1]
-                store_slots(staging, t, index * count + pair, slots, even, odd)
-            return carry
-
-        lax.fori_loop(0, count, body, 0)
-    write_out(staging, out)
-
-
-def unpack_kernel(source, out, *, height, width):
+                rows.append(jnp.where(low, even, turn(odd, HALF)))
+                rows.append(jnp.where(low, turn(even, HALF), odd))
+        out[:, :, t * LANES : (t + 1) * LANES] = jnp.swapaxes(jnp.stack(rows), 0, 1)
+
+
+def unpack_kernel(mine, block, received, out, joined, *, height, width):
+    join_kernel(mine, block, received, joined)
     channels = out.shape[0]
     tiles = -(-width // LANES)
     blocks = []
     for a in range(height // channels):
         for tile in range(tiles):
             start = tile * height + a * channels
-            piece = source[start : start + channels, :].astype(F32)
+            piece = joined[start : start + channels, :].astype(F32)
             blocks.append(piece[:, : min(LANES, width - tile * LANES)])
     out[...] = jnp.concatenate(blocks, axis=1)
 
 
-def call(kernel, out_shape, n_smem, n_vmem, scratch=(), flops=0, moved=4 << 20, n_any=0):
-    single = not isinstance(out_shape, (list, tuple))
-    return pl.pallas_call(
-        kernel,
-        out_shape=out_shape,
-        in_specs=[SMEM] * n_smem + [VMEM] * n_vmem + [ANY] * n_any,
-        out_specs=VMEM if single else [VMEM] * len(out_shape),
+def call(kernel, out_shape, n_smem, n_vmem, scratch=(), flops=0, n_any=0, room=10, after=()):
+    inputs, outputs = n_smem + n_vmem + n_any, len(out_shape)
+
+    def body(*refs):
+        refs, marks = refs[:inputs], refs[inputs + len(after) :]
+        kernel(*refs, *marks[:outputs], *marks[outputs + 1 :])
+        marks[outputs][...] = jnp.zeros((8, LANES), F32)
+
+    called = pl.pallas_call(
+        body,
+        out_shape=[*out_shape, jax.ShapeDtypeStruct((8, LANES), F32)],
+        in_specs=[SMEM] * n_smem + [VMEM] * n_vmem + [ANY] * (n_any + len(after)),
+        out_specs=[VMEM] * (outputs + 1),
         scratch_shapes=list(scratch),
-        compiler_params=pltpu.CompilerParams(vmem_limit_bytes=56 << 20),
-        cost_estimate=pl.CostEstimate(flops=flops, bytes_accessed=moved, transcendentals=0),
+        compiler_params=pltpu.CompilerParams(vmem_limit_bytes=room << 20),
+        cost_estimate=pl.CostEstimate(flops=flops, bytes_accessed=4 << 20, transcendentals=0),
     )
-
-
-def tied(value, *others):
-    return lax.optimization_barrier((value, *others))[0]
-
-
-def summed(terms, scale, tasks):
+    return lambda *args: called(*args, *after)
+
+
+def split_kernel(mine, kept, received, kept_out, sent_out):
+    half = kept_out.shape[0]
+    here = pl.multiple_of(mine[0] * half, half)
+    there = pl.multiple_of((1 - mine[0]) * half, half)
+    kept_out[...] = kept[pl.ds(here, half), :] + received[pl.ds(here, half), :]
+    sent_out[...] = kept[pl.ds(there, half), :] + received[pl.ds(there, half), :]
+
+
+def add_kernel(kept, received, out, *, scale):
+    total = kept[...] + received[...]
+    out[...] = total if scale is None else (total * scale).astype(BF)
+
+
+def join_kernel(mine, block, received, out):
+    half = block.shape[0]
+    out[pl.ds(pl.multiple_of(mine[0] * half, half), half), :] = block[...]
+    out[pl.ds(pl.multiple_of((1 - mine[0]) * half, half), half), :] = received[...]
+
+
+def sum_bits():
+    devices = lax.axis_size("gx") * lax.axis_size("gy")
+    bits = [1 << b for b in range(devices.bit_length() - 1)]
+    inner = [bit for bit in bits if bit < lax.axis_size("gy")]
+    return inner, bits[len(inner) :]
+
+
+def bit_of_me(bit):
+    me = lax.axis_index("gx") * lax.axis_size("gy") + lax.axis_index("gy")
+    return (me // bit % 2).reshape(1)
+
+
+def summed(kept, sent, mark, scale, tasks):
     axes = ("gx", "gy")
     devices = lax.axis_size("gx") * lax.axis_size("gy")
-    me = lax.axis_index("gx") * lax.axis_size("gy") + lax.axis_index("gy")
-    bits = [1 << b for b in range(devices.bit_length() - 1)]
+    inner, outer = sum_bits()
 
     def swapped(block, bit):
         return lax.ppermute(block, axes, [(i, i ^ bit) for i in range(devices)])
 
-    block = terms
-    for step, bit in enumerate(bits + bits[::-1]):
-        beside = tasks[step](block) if step in tasks else None
-        mine = me // bit % 2
-        if step < len(bits):
-            half = block.shape[0] // 2
-            kept = lax.dynamic_slice_in_dim(block, mine * half, half, 0)
-            sent = lax.dynamic_slice_in_dim(block, (1 - mine) * half, half, 0)
-            block = kept + swapped(sent, bit)
-            if step == len(bits) - 1:
-                block = (block * scale).astype(BF)
+    def like(block, factor, kind=F32):
+        return jax.ShapeDtypeStruct((int(block.shape[0] * factor), LANES), kind)
+
+    order = inner + outer + inner[::-1]
+    block = kept
+    for step, bit in enumerate(order):
+        received = swapped(sent if step < len(inner) else block, bit)
+        after = [tasks[step](mark)] if step in tasks else []
+        if step + 1 < len(inner):
+            half = like(block, 0.5)
+            block, sent, mark = call(split_kernel, [half, half], 1, 2, after=after)(
+                bit_of_me(order[step + 1]), block, received
+            )
+        elif step < len(inner) + len(outer):
+            last = step + 1 == len(inner) + len(outer)
+            kernel = functools.partial(add_kernel, scale=scale if last else None)
+            block, mark = call(kernel, [like(block, 1, BF if last else F32)], 0, 2, after=after)(
+                block, received
+            )
+        elif step + 1 < len(order):
+            block, mark = call(join_kernel, [like(block, 2, BF)], 1, 2, after=after)(
+                bit_of_me(bit), block, received
+            )
         else:
-            other = swapped(block, bit)
-            block = jnp.where(
-                mine == 0,
-                jnp.concatenate([block, other], axis=0),
-                jnp.concatenate([other, block], axis=0),
-            )
-        if beside is not None:
-            block = tied(block, beside)
-    return block
+            return bit_of_me(bit), block, received, after
 
 
 def per_device(feats, cotangent, weight, cell_slot, neighbours, counts):
@@ -407,41 +434,40 @@
     side = math.isqrt(cell_slot.shape[1])
     pairs = slots // 2
     cells = cell_slot.reshape(side * side)
-    links = neighbours.reshape(slots * 8)
+    links = neighbours.reshape(slots, 8).T
     count = counts.reshape(1)
     native = jax.ShapeDtypeStruct((channels, slots, voxels), BF)
     field = jax.ShapeDtypeStruct((pairs, 8, channels, LANES), BF)
     rows = jax.ShapeDtypeStruct((side // 2, channels, LANES), BF)
     column = jax.ShapeDtypeStruct((4, channels, LANES), BF)
-    staging = pltpu.VMEM((4, channels * slots, LANES), F32)
     table = pltpu.VMEM((pairs + 2 + side // 2, 8, channels, LANES), BF)
     columns = pltpu.VMEM((9 * channels, 20 * LANES), BF)
     carry_ref = pltpu.VMEM((channels, 4 * LANES), F32)
     sems = pltpu.SemaphoreType.DMA((2,))
     flops = 2 * 27 * channels * channels * slots * voxels
 
-    prepared, low_edge, high_edge = call(
-        functools.partial(prepare_kernel, side=side), [field, rows, rows], 1, 1, [staging]
+    prepared, low_edge, high_edge, _ = call(
+        functools.partial(prepare_kernel, side=side), [field, rows, rows], 1, 1
     )(cells, feats.reshape(channels, slots, voxels))
     below_x = passed_along(high_edge, "gx", 1)
     above_x = passed_along(low_edge, "gx", -1)
-    upstream = call(regroup_kernel, field, 0, 1, [staging])(
+    upstream, mark = call(regroup_kernel, [field], 0, 1)(
         cotangent.reshape(channels, slots, voxels)
     )
-    make_columns = call(functools.partial(column_kernel, side=side), [column, column], 1, 3)
-    low_column, high_column = make_columns(cells, tied(prepared, upstream), below_x, above_x)
+    make_columns = functools.partial(column_kernel, side=side)
+    low_column, high_column, mark = call(make_columns, [column, column], 1, 3, after=[mark])(
+        cells, prepared, below_x, above_x
+    )
     below_y = from_behind(high_column, "gy", 1)
     above_y = from_behind(low_column, "gy", -1)
-
-    taps = weight.reshape(channels, 3, 9 * channels)
-    matrix = taps.transpose(1, 0, 2).reshape(3 * channels, 9 * channels)
-    flipped = weight.reshape(channels, 27, channels)[:, ::-1, :].reshape(channels, 3, 9, channels)
-    flipped = flipped.transpose(1, 3, 2, 0).reshape(3 * channels, 9 * channels)
-
-    output, grad, terms, low_edge, high_edge = call(
+    stacked = jax.ShapeDtypeStruct((3 * channels, 9 * channels), BF)
+    matrix, flipped, _ = call(weights_kernel, [stacked, stacked], 0, 1, after=[mark])(weight)
+
+    half = jax.ShapeDtypeStruct((ROWS // 2, LANES), F32)
+    output, grad, kept, sent, low_edge, high_edge, mark = call(
         functools.partial(forward_kernel, side=side),
-        [field, field, jax.ShapeDtypeStruct((ROWS, LANES), F32), rows, rows],
-        3,
+        [field, field, half, half, rows, rows],
+        4,
         5,
         [
             table,
@@ -449,57 +475,67 @@
             pltpu.VMEM((3 * channels, 20 * LANES), BF),
             carry_ref,
             pltpu.VMEM((3 * channels, 9 * channels), F32),
+            pltpu.VMEM((ROWS, LANES), F32),
             pltpu.VMEM(field.shape, BF),
             sems,
         ],
         2 * flops,
         n_any=2,
-    )(cells, links, count, below_x, above_x, below_y, above_y, matrix, prepared, upstream)
+        room=20,
+    )(
+        cells, links, count, bit_of_me(sum_bits()[0][0]),
+        below_x, above_x, below_y, above_y, matrix, prepared, upstream,
+    )
 
     halos = [passed_along(high_edge, "gx", 1), passed_along(low_edge, "gx", -1)]
     parts = []
     done = {}
 
-    def columns_task(token):
-        low_column, high_column = make_columns(cells, tied(grad, token), *halos)
+    def columns_task(mark):
+        low_column, high_column, mark = call(
+            make_columns, [column, column], 1, 3, after=[mark]
+        )(cells, grad, *halos)
         halos.append(from_behind(high_column, "gy", 1))
         halos.append(from_behind(low_column, "gy", -1))
-        return low_column
-
-    def output_task(token):
-        done["output"] = call(native_kernel, native, 0, 1, [staging])(tied(output, token))
-        return done["output"]
-
-    def backward_task(group, token):
-        part = call(
+        return mark
+
+    def output_task(mark):
+        done["output"], mark = call(native_kernel, [native], 0, 1, after=[mark])(output)
+        return mark
+
+    def backward_task(group, mark):
+        part, mark = call(
             functools.partial(backward_kernel, side=side, group=group),
-            jax.ShapeDtypeStruct((2, 8, channels, LANES), BF),
+            [jax.ShapeDtypeStruct((2, 8, channels, LANES), BF)],
             2,
             5,
             [table, columns, carry_ref, pltpu.VMEM((2, 8, channels, LANES), BF), sems],
             4 * flops // pairs,
             n_any=2,
-        )(links, count, *halos, flipped, tied(grad, token), upstream)
+            room=12,
+            after=[mark],
+        )(links, count, *halos, flipped, grad, upstream)
         parts.append(part)
-        return part
-
-    def gradient_task(token):
-        first = tied(parts[0], token)
-        done["grad"] = call(native_kernel, native, 0, len(parts), [staging])(first, *parts[1:])
-        return done["grad"]
+        return mark
+
+    def gradient_task(mark):
+        done["grad"], mark = call(native_kernel, [native], 0, len(parts), after=[mark])(*parts)
+        return mark
 
     tasks = [columns_task, output_task]
     tasks += [functools.partial(backward_task, group) for group in range(pairs // 2)]
     tasks += [gradient_task]
     device_total = lax.axis_size("gx") * lax.axis_size("gy")
     scale = 1.0 / math.sqrt(voxels * slots * device_total)
-    whole = summed(terms, scale, dict(enumerate(tasks, 1)))
-    grad_weight = call(
+    mine, block, received, after = summed(kept, sent, mark, scale, dict(enumerate(tasks, 1)))
+    grad_weight, _ = call(
         functools.partial(unpack_kernel, height=3 * channels, width=9 * channels),
-        jax.ShapeDtypeStruct((channels, 27 * channels), F32),
-        0,
+        [jax.ShapeDtypeStruct((channels, 27 * channels), F32)],
         1,
-    )(whole)
+        2,
+        [pltpu.VMEM((ROWS, LANES), BF)],
+        after=after,
+    )(mine, block, received)
     return (done["output"].reshape(feats.shape), done["grad"].reshape(feats.shape), grad_weight)
 
 

time: 133 us -> 108 us (0.81)
  Pallas kernels: 77.9 us -> 55.6 us
  local copies, waits for them, and re-layouts: 9.25 us -> 11.9 us
  starting transfers between devices: 31.9 us -> 29.5 us
  other arithmetic: 2.26 us -> 0 us
    pallas_call x12 -> x20, Pallas kernels: 77.9 us -> 55.6 us  [call(): return lambda *args: called(*args, *after)]
    unnamed x30 -> x42, local copies, waits for them, and re-layouts: 4.2 us -> 11.9 us
    ppermute x10 -> x8, starting transfers between devices: 11.7 us -> 8.71 us  [swapped(): return lax.ppermute(block, axes, [(i, i ^ bit) for i in range(devices)])]
    reshape x4 -> x0, local copies, waits for them, and re-layouts: 2.98 us -> none  [the longest x2 1.91 us: per_device(): flipped = flipped.transpose(1, 3, 2, 0).reshape(3 * channels, 9 * channels)]
    ppermute x10 -> x8, waiting for transfers between devices: 5.76 us -> 3.48 us  [swapped(): return lax.ppermute(block, axes, [(i, i ^ bit) for i in range(devices)])]
  transfers between devices with their start and end apart: 18 -> 16, of which waited for: 5 -> 6; matrix products, arithmetic and copies ran while one was open for 3% -> 0% of each run, Pallas kernels for 32% -> 24%
where the time goes in v2:
time: 108 us; the launch traced here: 107 us
  Pallas kernels  55.6 us (51%)
  starting transfers between devices  29.5 us (27%)
  local copies, waits for them, and re-layouts  11.9 us (11%)
  waiting for transfers between devices  8.8 us (8%)
  between operations  1.56 us (1%)
    pallas_call x20, Pallas kernels, call(): return lambda *args: called(*args, *after)  55.6 us
    ppermute x4, starting transfers between devices, from_behind(): return lax.ppermute(block, axis, route)  13.4 us
    unnamed x42, local copies, waits for them, and re-layouts  11.9 us
    ppermute x8, starting transfers between devices, swapped(): return lax.ppermute(block, axes, [(i, i ^ bit) for i in range(devices)])  8.71 us
    ppermute x4, starting transfers between devices, passed_along(): return lax.ppermute(block, axis, route)  7.42 us
    ppermute x8, waiting for transfers between devices, swapped(): return lax.ppermute(block, axes, [(i, i ^ bit) for i in range(devices)])  3.48 us
    ppermute x4, waiting for transfers between devices, passed_along(): return lax.ppermute(block, axis, route)  3.09 us
    ppermute x4, waiting for transfers between devices, from_behind(): return lax.ppermute(block, axis, route)  2.23 us
  transfers between devices with their start and end apart: 16, of which 6 were waited for; matrix products, arithmetic and copies ran while one was open for 0% of the time, Pallas kernels for 24%

profile of v2, /device:TPU:1, one launch (start us, length us, event | category | flops | bytes accessed | tf_op | source)
XLA Modules:
  0.0 107.4 jit_solution(6575135740901303424)
XLA Ops:
  0.6 1.4 %copy-done = bf16[96,1,16,512]{3,2,1,0:T(8,128)(2,1)S(1)} copy-done((bf16[96,1,16,512]{3,2,1,0:T(8,128)(2,1)S(1)}, bf16[96,1,16,512]{3,2,1,0:T(8,128)(2,1)}, u32[]{:S(2)}) %copy-start) | copy-done | bytes 1572888
  2.0 0.7 copy-done.7
  2.7 2.1 %shard_map.85 = (bf16[8,8,96,128]{3,2,1,0:T(8,128)(2,1)S(1)}, bf16[3,96,128]{2,1,0:T(8,128)(2,1)S(1)}, bf16[3,96,128]{2,1,0:T(8,128)(2,1)S(1)}, f32[8,128]{1,0:T(8,128)}) custom-call(s32[36]{0:T(128)S(1)} %bitcast.23, bf16[96,16,512]{2,1,0:T(8,128)(2,1)S(1)} %bitcast.21), custom_call_target="tpu_custom_call" | custom-call | bytes 4194304 | tf_op jit(solution)/shard_map/pallas_call | solution.py:363
  4.8 2.1 %collective-permute-start = (bf16[3,96,128]{2,1,0:T(8,128)(2,1)S(1)}, bf16[3,96,128]{2,1,0:T(8,128)(2,1)S(1)}, u32[]{:S(2)}, u32[]{:S(2)}) collective-permute-start(bf16[3,96,128]{2,1,0:T(8,128)(2,1)S(1)} %get-tuple-element.51), channel_id=1, source_target_pairs={{24,0},{0,8},{8,16},{16,24},{25,1},{1,9},{9,17},{17,25},{26,2},{2,... | collective-permute-start | bytes 221192 | tf_op jit(solution)/shard_map/ppermute | solution.py:24
  7.0 2.0 %collective-permute-start.1 = (bf16[3,96,128]{2,1,0:T(8,128)(2,1)S(1)}, bf16[3,96,128]{2,1,0:T(8,128)(2,1)S(1)}, u32[]{:S(2)}, u32[]{:S(2)}) collective-permute-start(bf16[3,96,128]{2,1,0:T(8,128)(2,1)S(1)} %get-tuple-element.52), channel_id=1, source_target_pairs={{8,0},{16,8},{24,16},{0,24},{9,1},{17,9},{25,17},{1,25},{10,2},{18... | collective-permute-start | bytes 221192 | tf_op jit(solution)/shard_map/ppermute | solution.py:24
  9.0 0.9 shard_map.86
  10.0 1.2 %copy-done.12 = bf16[8,8,96,128]{3,2,1,0:T(8,128)(2,1)} copy-done((bf16[8,8,96,128]{3,2,1,0:T(8,128)(2,1)}, bf16[8,8,96,128]{3,2,1,0:T(8,128)(2,1)S(1)}, u32[]{:S(2)}) %copy-start.12) | copy-done | bytes 1572888
  11.2 0.0 collective-permute-done.refs_2_.refs_4_
  11.2 1.0 collective-permute-done.1.refs_3_.refs_5_
  12.1 1.4 %shard_map.87 = (bf16[4,96,128]{2,1,0:T(8,128)(2,1)S(1)}, bf16[4,96,128]{2,1,0:T(8,128)(2,1)S(1)}, f32[8,128]{1,0:T(8,128)S(1)}) custom-call(s32[36]{0:T(128)S(1)} %bitcast.24, bf16[8,8,96,128]{3,2,1,0:T(8,128)(2,1)S(1)} %get-tuple-element.53.refs_1_.refs_9_, bf16[3,96,128]{2,1,0:T(8,128)(2,1)S(1)} %collective-permute-done.refs_2_.refs_4_, ...), custom_call_target="tpu_custom_call" | custom-call | bytes 4194304 | tf_op jit(solution)/shard_map/pallas_call | solution.py:363
  13.6 4.1 %collective-permute-start.2 = (bf16[4,96,128]{2,1,0:T(8,128)(2,1)S(1)}, bf16[4,96,128]{2,1,0:T(8,128)(2,1)S(1)}, u32[]{:S(2)}, u32[]{:S(2)}) collective-permute-start(bf16[4,96,128]{2,1,0:T(8,128)(2,1)S(1)} %get-tuple-element.55), channel_id=1, source_target_pairs={{0,1},{1,2},{2,3},{3,4},{4,5},{5,6},{6,7},{8,9},{9,10},{10,11},{11... | collective-permute-start | bytes 294920 | tf_op jit(solution)/shard_map/ppermute | solution.py:30
  17.7 1.9 %collective-permute-start.3 = (bf16[4,96,128]{2,1,0:T(8,128)(2,1)S(1)}, bf16[4,96,128]{2,1,0:T(8,128)(2,1)S(1)}, u32[]{:S(2)}, u32[]{:S(2)}) collective-permute-start(bf16[4,96,128]{2,1,0:T(8,128)(2,1)S(1)} %get-tuple-element.56), channel_id=1, source_target_pairs={{1,0},{2,1},{3,2},{4,3},{5,4},{6,5},{7,6},{9,8},{10,9},{11,10},{12... | collective-permute-start | bytes 294920 | tf_op jit(solution)/shard_map/ppermute | solution.py:30
  20.3 1.6 %shard_map.88 = (bf16[288,864]{1,0:T(8,128)(2,1)S(1)}, bf16[288,864]{1,0:T(8,128)(2,1)S(1)}, f32[8,128]{1,0:T(8,128)}) custom-call(bf16[96,2592]{1,0:T(8,128)(2,1)S(1)} %copy-done.6, f32[8,128]{1,0:T(8,128)S(1)} %get-tuple-element.57.refs_1_), custom_call_target="tpu_custom_call" | custom-call | bytes 4194304 | tf_op jit(solution)/shard_map/pallas_call | solution.py:363
  22.0 0.8 copy-done.15
  22.7 0.0 collective-permute-done.2.refs_6_
  22.8 0.9 collective-permute-done.3.refs_7_
  23.6 0.0 copy-done.19
  23.7 1.4 %copy-done.3 = bf16[8,8,96,128]{3,2,1,0:T(8,128)(2,1)S(1)} copy-done((bf16[8,8,96,128]{3,2,1,0:T(8,128)(2,1)S(1)}, bf16[8,8,96,128]{3,2,1,0:T(8,128)(2,1)}, u32[]{:S(2)}) %copy-start.3) | copy-done | bytes 1572888
  25.1 1.4 %copy-done.13 = bf16[8,8,96,128]{3,2,1,0:T(8,128)(2,1)S(1)} copy-done((bf16[8,8,96,128]{3,2,1,0:T(8,128)(2,1)S(1)}, bf16[8,8,96,128]{3,2,1,0:T(8,128)(2,1)}, u32[]{:S(2)}) %copy-start.13) | copy-done | bytes 1572888
  26.5 22.3 %shard_map.89 = (bf16[8,8,96,128]{3,2,1,0:T(8,128)(2,1)S(1)}, bf16[8,8,96,128]{3,2,1,0:T(8,128)(2,1)S(1)}, f32[1024,128]{1,0:T(8,128)S(1)}, f32[1024,128]{1,0:T(...) custom-call(s32[36]{0:T(128)S(1)} %bitcast.25, s32[8,16]{1,0:T(8,128)S(1)} %bitcast.27, ...), custom_call_target="tpu_custom_call" | custom-call | flops 8153726976 | bytes 4194304 | tf_op jit(solution)/shard_map/pallas_call | solution.py:363
  48.8 0.0 copy-start.4
  48.8 0.8 copy-done.4
  49.6 0.6 copy-done.17
  50.3 0.6 copy-done.18
  50.9 0.0 collective-permute-start.4
  50.9 2.2 %collective-permute-done.4.refs_2_ = f32[1024,128]{1,0:T(8,128)} collective-permute-done((f32[1024,128]{1,0:T(8,128)}, f32[1024,128]{1,0:T(8,128)}, u32[]{:S(2)}, u32[]{:S(2)}) %collective-permute-start.4) | collective-permute-done | bytes 524320 | tf_op jit(solution)/shard_map/ppermute | solution.py:403
  53.1 1.0 copy-done.5
  54.2 1.8 %shard_map.90 = (f32[512,128]{1,0:T(8,128)S(1)}, f32[512,128]{1,0:T(8,128)}, f32[8,128]{1,0:T(8,128)S(1)}) custom-call(s32[1]{0:T(128)} %bitcast.8.refs_0_, f32[1024,128]{1,0:T(8,128)S(1)} %copy-done.5, f32[1024,128]{1,0:T(8,128)} %collective-permute-done.4.refs_2_), custom_call_target="tpu_custom_call" | custom-call | bytes 4194304 | tf_op jit(solution)/shard_map/pallas_call | solution.py:363
  56.0 0.6 copy-done.10
  56.6 2.1 %collective-permute-start.5 = (f32[512,128]{1,0:T(8,128)}, f32[512,128]{1,0:T(8,128)}, u32[]{:S(2)}, u32[]{:S(2)}) collective-permute-start(f32[512,128]{1,0:T(8,128)} %get-tuple-element.64), channel_id=1, source_target_pairs={{0,2},{1,3},{2,0},{3,1},{4,6},{5,7},{6,4},{7,5},{8,10},{9,11},{10,... | collective-permute-start | bytes 786440 | tf_op jit(solution)/shard_map/ppermute | solution.py:403
  58.7 0.8 collective-permute-start.6
  59.5 2.4 %collective-permute-start.7 = (bf16[3,96,128]{2,1,0:T(8,128)(2,1)}, bf16[3,96,128]{2,1,0:T(8,128)(2,1)S(1)}, u32[]{:S(2)}, u32[]{:S(2)}) collective-permute-start(bf16[3,96,128]{2,1,0:T(8,128)(2,1)} %copy-done.17), channel_id=1, source_target_pairs={{8,0},{16,8},{24,16},{0,24},{9,1},{17,9},{25,17},{1,25},{10,2},{18... | collective-permute-start | bytes 221192 | tf_op jit(solution)/shard_map/ppermute | solution.py:24
  61.9 2.1 %collective-permute-done.6.refs_2_ = bf16[3,96,128]{2,1,0:T(8,128)(2,1)S(1)} collective-permute-done((bf16[3,96,128]{2,1,0:T(8,128)(2,1)}, bf16[3,96,128]{2,1,0:T(8,128)(2,1)S(1)}, u32[]{:S(2)}, u32[]{:S(2)}) %collective-permute-start.6) | collective-permute-done | bytes 73760 | tf_op jit(solution)/shard_map/ppermute | solution.py:24
  64.1 0.0 collective-permute-done.7.refs_3_
  64.1 0.7 copy-done.9
  64.7 0.7 copy-done.11
  65.4 1.4 %shard_map.91 = (bf16[4,96,128]{2,1,0:T(8,128)(2,1)S(1)}, bf16[4,96,128]{2,1,0:T(8,128)(2,1)S(1)}, f32[8,128]{1,0:T(8,128)S(1)}) custom-call(s32[36]{0:T(128)S(1)} %bitcast.26, bf16[8,8,96,128]{3,2,1,0:T(8,128)(2,1)S(1)} %get-tuple-element.65.refs_1_.refs_7_, bf16[3,96,128]{2,1,0:T(8,128)(2,1)S(1)} %collective-permute-done.6.refs_2_, ...), custom_call_target="tpu_custom_call" | custom-call | bytes 4194304 | tf_op jit(solution)/shard_map/pallas_call | solution.py:363
  66.9 0.0 copy-start.20
  66.9 0.0 collective-permute-done.5.refs_2_
  66.9 1.1 %shard_map.92 = (f32[256,128]{1,0:T(8,128)S(1)}, f32[256,128]{1,0:T(8,128)S(1)}, f32[8,128]{1,0:T(8,128)S(1)}) custom-call(s32[1]{0:T(128)} %bitcast.7.refs_0_, f32[512,128]{1,0:T(8,128)S(1)} %get-tuple-element.63.refs_1_, f32[512,128]{1,0:T(8,128)} %collective-permute-done.5.refs_2_, f32[8,128]{1,0:T(8,128)S(1)} %get-tuple-element.69.refs_3_), custom_call_target="tpu_custom_call" | custom-call | bytes 4194304 | tf_op jit(solution)/shard_map/pallas_call | solution.py:363
  68.0 0.1 collective-permute-start.10
  68.1 5.3 %collective-permute-start.8 = (bf16[4,96,128]{2,1,0:T(8,128)(2,1)S(1)}, bf16[4,96,128]{2,1,0:T(8,128)(2,1)S(1)}, u32[]{:S(2)}, u32[]{:S(2)}) collective-permute-start(bf16[4,96,128]{2,1,0:T(8,128)(2,1)S(1)} %get-tuple-element.72), channel_id=1, source_target_pairs={{0,1},{1,2},{2,3},{3,4},{4,5},{5,6},{6,7},{8,9},{9,10},{10,11},{11... | collective-permute-start | bytes 294920 | tf_op jit(solution)/shard_map/ppermute | solution.py:30
  73.4 2.1 %collective-permute-start.9 = (bf16[4,96,128]{2,1,0:T(8,128)(2,1)S(1)}, bf16[4,96,128]{2,1,0:T(8,128)(2,1)S(1)}, u32[]{:S(2)}, u32[]{:S(2)}) collective-permute-start(bf16[4,96,128]{2,1,0:T(8,128)(2,1)S(1)} %get-tuple-element.73), channel_id=1, source_target_pairs={{1,0},{2,1},{3,2},{4,3},{5,4},{6,5},{7,6},{9,8},{10,9},{11,10},{12... | collective-permute-start | bytes 294920 | tf_op jit(solution)/shard_map/ppermute | solution.py:30
  75.5 2.0 %shard_map.93 = (bf16[96,16,512]{2,1,0:T(8,128)(2,1)}, f32[8,128]{1,0:T(8,128)S(1)}) custom-call(bf16[8,8,96,128]{3,2,1,0:T(8,128)(2,1)S(1)} %get-tuple-element.60.refs_0_, f32[8,128]{1,0:T(8,128)S(1)} %get-tuple-element.70.refs_1_), custom_call_target="tpu_custom_call" | custom-call | bytes 4194304 | tf_op jit(solution)/shard_map/pallas_call | solution.py:363
  77.5 0.0 collective-permute-done.10.refs_1_
  77.5 0.7 collective-permute-start.11
  78.3 0.0 collective-permute-done.8.refs_4_
  78.3 1.3 %collective-permute-done.9.refs_5_ = bf16[4,96,128]{2,1,0:T(8,128)(2,1)S(1)} collective-permute-done((bf16[4,96,128]{2,1,0:T(8,128)(2,1)S(1)}, bf16[4,96,128]{2,1,0:T(8,128)(2,1)S(1)}, u32[]{:S(2)}, u32[]{:S(2)}) %collective-permute-start.9) | collective-permute-done | bytes 98336 | tf_op jit(solution)/shard_map/ppermute | solution.py:30
  79.6 0.0 copy-done.16
  79.6 4.3 %shard_map.95 = (bf16[2,8,96,128]{3,2,1,0:T(8,128)(2,1)S(1)}, f32[8,128]{1,0:T(8,128)S(1)}) custom-call(s32[8,16]{1,0:T(8,128)S(1)} %bitcast.28, s32[1]{0:T(128)} %bitcast.17.refs_1_, bf16[3,96,128]{2,1,0:T(8,128)(2,1)S(1)} %collective-permute-done.6.refs_2_, bf16[3,96,128]{2,1,0:T(8,128)(2,1)S(1)} %collective-permute-done.7.refs_3_, ...), custom_call_target="tpu_custom_call" | custom-call | flops 2038431744 | bytes 4194304 | tf_op jit(solution)/shard_map/pallas_call | solution.py:363
  83.9 0.0 collective-permute-done.11.refs_1_
  84.0 1.2 %collective-permute-start.12 = (f32[256,128]{1,0:T(8,128)S(1)}, f32[256,128]{1,0:T(8,128)S(1)}, u32[]{:S(2)}, u32[]{:S(2)}) collective-permute-start(f32[256,128]{1,0:T(8,128)S(1)} %get-tuple-element.84.refs_0_), channel_id=1, source_target_pairs={{0,16},{1,17},{2,18},{3,19},{4,20},{5,21},{6,22},{7,23},{8,24},{9,... | collective-permute-start | bytes 393224 | tf_op jit(solution)/shard_map/ppermute | solution.py:403
  85.2 4.3 %shard_map.97 = (bf16[2,8,96,128]{3,2,1,0:T(8,128)(2,1)S(1)}, f32[8,128]{1,0:T(8,128)S(1)}) custom-call(s32[8,16]{1,0:T(8,128)S(1)} %bitcast.29, s32[1]{0:T(128)} %bitcast.18.refs_1_, bf16[3,96,128]{2,1,0:T(8,128)(2,1)S(1)} %collective-permute-done.6.refs_2_, bf16[3,96,128]{2,1,0:T(8,128)(2,1)S(1)} %collective-permute-done.7.refs_3_, ...), custom_call_target="tpu_custom_call" | custom-call | flops 2038431744 | bytes 4194304 | tf_op jit(solution)/shard_map/pallas_call | solution.py:363
  89.5 1.2 %collective-permute-done.12.refs_1_ = f32[256,128]{1,0:T(8,128)S(1)} collective-permute-done((f32[256,128]{1,0:T(8,128)S(1)}, f32[256,128]{1,0:T(8,128)S(1)}, u32[]{:S(2)}, u32[]{:S(2)}) %collective-permute-start.12) | collective-permute-done | bytes 131104 | tf_op jit(solution)/shard_map/ppermute | solution.py:403
  90.7 0.1 collective-permute-start.13
  90.8 4.3 %shard_map.99 = (bf16[2,8,96,128]{3,2,1,0:T(8,128)(2,1)S(1)}, f32[8,128]{1,0:T(8,128)S(1)}) custom-call(s32[8,16]{1,0:T(8,128)S(1)} %bitcast.30, s32[1]{0:T(128)} %bitcast.19.refs_1_, bf16[3,96,128]{2,1,0:T(8,128)(2,1)S(1)} %collective-permute-done.6.refs_2_, bf16[3,96,128]{2,1,0:T(8,128)(2,1)S(1)} %collective-permute-done.7.refs_3_, ...), custom_call_target="tpu_custom_call" | custom-call | flops 2038431744 | bytes 4194304 | tf_op jit(solution)/shard_map/pallas_call | solution.py:363
  95.1 0.0 collective-permute-done.13.refs_2_
  95.1 4.0 %collective-permute-start.14 = (bf16[512,128]{1,0:T(8,128)(2,1)S(1)}, bf16[512,128]{1,0:T(8,128)(2,1)S(1)}, u32[]{:S(2)}, u32[]{:S(2)}) collective-permute-start(bf16[512,128]{1,0:T(8,128)(2,1)S(1)} %get-tuple-element.92.refs_1_), channel_id=1, source_target_pairs={{0,2},{1,3},{2,0},{3,1},{4,6},{5,7},{6,4},{7,5},{8,10},{9,11},{10,... | collective-permute-start | bytes 393224 | tf_op jit(solution)/shard_map/ppermute | solution.py:403
  99.1 4.5 %shard_map.101 = (bf16[2,8,96,128]{3,2,1,0:T(8,128)(2,1)S(1)}, f32[8,128]{1,0:T(8,128)S(1)}) custom-call(s32[8,16]{1,0:T(8,128)S(1)} %bitcast.31, s32[1]{0:T(128)} %bitcast.20.refs_1_, bf16[3,96,128]{2,1,0:T(8,128)(2,1)S(1)} %collective-permute-done.6.refs_2_, bf16[3,96,128]{2,1,0:T(8,128)(2,1)S(1)} %collective-permute-done.7.refs_3_, ...), custom_call_target="tpu_custom_call" | custom-call | flops 2038431744 | bytes 4194304 | tf_op jit(solution)/shard_map/pallas_call | solution.py:363
  103.7 0.0 collective-permute-done.14.refs_2_
  103.7 0.5 collective-permute-start.15
  104.2 2.0 %shard_map.103 = (bf16[96,16,512]{2,1,0:T(8,128)(2,1)}, f32[8,128]{1,0:T(8,128)S(1)}) custom-call(bf16[2,8,96,128]{3,2,1,0:T(8,128)(2,1)S(1)} %get-tuple-element.79.refs_0_, bf16[2,8,96,128]{3,2,1,0:T(8,128)(2,1)S(1)} %get-tuple-element.83.refs_1_, bf16[2,8,96,128]{3,2,1,0:T(8,128)(2,1)S(1)} %get-tuple-element.87.refs_2_, ...), custom_call_target="tpu_custom_call" | custom-call | bytes 4194304 | tf_op jit(solution)/shard_map/pallas_call | solution.py:363
  106.3 0.0 collective-permute-done.15.refs_2_
  106.3 1.2 %shard_map.104 = (f32[96,2592]{1,0:T(8,128)}, f32[8,128]{1,0:T(8,128)}) custom-call(s32[1]{0:T(128)} %bitcast.4.refs_3_.refs_0_, bf16[1024,128]{1,0:T(8,128)(2,1)S(1)} %get-tuple-element.96.refs_1_, bf16[1024,128]{1,0:T(8,128)(2,1)S(1)} %collective-permute-done.15.refs_2_, f32[8,128]{1,0:T(8,128)S(1)} %get-tuple-element.97.refs_3_), custom_call_target="tpu_custom_call" | custom-call | bytes 4194304 | tf_op jit(solution)/shard_map/pallas_call | solution.py:363
  (30 shorter events, 0.1 us)
Async XLA Ops:
  0.6 1.4 %copy-start = (bf16[96,1,16,512]{3,2,1,0:T(8,128)(2,1)S(1)}, bf16[96,1,16,512]{3,2,1,0:T(8,128)(2,1)}, u32[]{:S(2)}) copy-start(bf16[96,1,16,512]{3,2,1,0:T(8,128)(2,1)} %param.6) | copy-start | bytes 4718596
  2.0 0.7 copy-start.7
  2.7 6.3 %copy-start.1 = (bf16[96,1,16,512]{3,2,1,0:T(8,128)(2,1)S(1)}, bf16[96,1,16,512]{3,2,1,0:T(8,128)(2,1)}, u32[]{:S(2)}) copy-start(bf16[96,1,16,512]{3,2,1,0:T(8,128)(2,1)} %param.7) | copy-start | bytes 4718596
  4.8 8.7 %copy-start.2 = (bf16[8,8,96,128]{3,2,1,0:T(8,128)(2,1)}, bf16[8,8,96,128]{3,2,1,0:T(8,128)(2,1)S(1)}, u32[]{:S(2)}) copy-start(bf16[8,8,96,128]{3,2,1,0:T(8,128)(2,1)S(1)} %get-tuple-element.53.refs_1_.refs_9_) | copy-start | bytes 4718596
  4.8 6.3 %collective-permute-start = (bf16[3,96,128]{2,1,0:T(8,128)(2,1)S(1)}, bf16[3,96,128]{2,1,0:T(8,128)(2,1)S(1)}, u32[]{:S(2)}, u32[]{:S(2)}) collective-permute-start(bf16[3,96,128]{2,1,0:T(8,128)(2,1)S(1)} %get-tuple-element.51), channel_id=1, source_target_pairs={{24,0},{0,8},{8,16},{16,24},{25,1},{1,9},{9,17},{17,25},{26,2},{2,... | collective-permute-start | bytes 221192 | tf_op jit(solution)/shard_map/ppermute | solution.py:24
  7.0 5.1 %collective-permute-start.1 = (bf16[3,96,128]{2,1,0:T(8,128)(2,1)S(1)}, bf16[3,96,128]{2,1,0:T(8,128)(2,1)S(1)}, u32[]{:S(2)}, u32[]{:S(2)}) collective-permute-start(bf16[3,96,128]{2,1,0:T(8,128)(2,1)S(1)} %get-tuple-element.52), channel_id=1, source_target_pairs={{8,0},{16,8},{24,16},{0,24},{9,1},{17,9},{25,17},{1,25},{10,2},{18... | collective-permute-start | bytes 221192 | tf_op jit(solution)/shard_map/ppermute | solution.py:24
  9.0 11.3 %copy-start.6 = (bf16[96,2592]{1,0:T(8,128)(2,1)S(1)}, bf16[96,2592]{1,0:T(8,128)(2,1)}, u32[]{:S(2)}) copy-start(bf16[96,2592]{1,0:T(8,128)(2,1)} %refs_0_.1) | copy-start | bytes 1492996
  9.0 14.6 %copy-start.8 = (s32[1,36]{1,0:T(1,128)S(1)}, s32[1,36]{1,0:T(1,128)}, u32[]{:S(2)}) copy-start(s32[1,36]{1,0:T(1,128)} %param.9) | copy-start | bytes 436
  9.0 14.6 %copy-start.19 = (s32[1,16,8]{1,2,0:T(8,128)S(1)}, s32[1,16,8]{1,2,0:T(8,128)}, u32[]{:S(2)}) copy-start(s32[1,16,8]{1,2,0:T(8,128)} %param.10) | copy-start | bytes 1540
  10.0 1.2 %copy-start.12 = (bf16[8,8,96,128]{3,2,1,0:T(8,128)(2,1)}, bf16[8,8,96,128]{3,2,1,0:T(8,128)(2,1)S(1)}, u32[]{:S(2)}) copy-start(bf16[8,8,96,128]{3,2,1,0:T(8,128)(2,1)S(1)} %get-tuple-element.59.refs_10_.refs_8_) | copy-start | bytes 4718596
  13.6 9.2 %collective-permute-start.2 = (bf16[4,96,128]{2,1,0:T(8,128)(2,1)S(1)}, bf16[4,96,128]{2,1,0:T(8,128)(2,1)S(1)}, u32[]{:S(2)}, u32[]{:S(2)}) collective-permute-start(bf16[4,96,128]{2,1,0:T(8,128)(2,1)S(1)} %get-tuple-element.55), channel_id=1, source_target_pairs={{0,1},{1,2},{2,3},{3,4},{4,5},{5,6},{6,7},{8,9},{9,10},{10,11},{11... | collective-permute-start | bytes 294920 | tf_op jit(solution)/shard_map/ppermute | solution.py:30
  17.7 5.9 %collective-permute-start.3 = (bf16[4,96,128]{2,1,0:T(8,128)(2,1)S(1)}, bf16[4,96,128]{2,1,0:T(8,128)(2,1)S(1)}, u32[]{:S(2)}, u32[]{:S(2)}) collective-permute-start(bf16[4,96,128]{2,1,0:T(8,128)(2,1)S(1)} %get-tuple-element.56), channel_id=1, source_target_pairs={{1,0},{2,1},{3,2},{4,3},{5,4},{6,5},{7,6},{9,8},{10,9},{11,10},{12... | collective-permute-start | bytes 294920 | tf_op jit(solution)/shard_map/ppermute | solution.py:30
  22.0 0.8 copy-start.15
  23.7 1.4 %copy-start.3 = (bf16[8,8,96,128]{3,2,1,0:T(8,128)(2,1)S(1)}, bf16[8,8,96,128]{3,2,1,0:T(8,128)(2,1)}, u32[]{:S(2)}) copy-start(bf16[8,8,96,128]{3,2,1,0:T(8,128)(2,1)} %copy-done.2) | copy-start | bytes 4718596
  25.1 1.4 %copy-start.13 = (bf16[8,8,96,128]{3,2,1,0:T(8,128)(2,1)S(1)}, bf16[8,8,96,128]{3,2,1,0:T(8,128)(2,1)}, u32[]{:S(2)}) copy-start(bf16[8,8,96,128]{3,2,1,0:T(8,128)(2,1)} %copy-done.12) | copy-start | bytes 4718596
  48.8 0.8 copy-start.4
  49.6 0.6 copy-start.17
  50.3 0.6 copy-start.18
  50.9 2.3 %collective-permute-start.4 = (f32[1024,128]{1,0:T(8,128)}, f32[1024,128]{1,0:T(8,128)}, u32[]{:S(2)}, u32[]{:S(2)}) collective-permute-start(f32[1024,128]{1,0:T(8,128)} %get-tuple-element.62), channel_id=1, source_target_pairs={{0,1},{1,0},{2,3},{3,2},{4,5},{5,4},{6,7},{7,6},{8,9},{9,8},{10,11... | collective-permute-start | bytes 1572872 | tf_op jit(solution)/shard_map/ppermute | solution.py:403
  53.1 1.0 copy-start.5
  56.0 0.6 copy-start.10
  56.6 10.3 %collective-permute-start.5 = (f32[512,128]{1,0:T(8,128)}, f32[512,128]{1,0:T(8,128)}, u32[]{:S(2)}, u32[]{:S(2)}) collective-permute-start(f32[512,128]{1,0:T(8,128)} %get-tuple-element.64), channel_id=1, source_target_pairs={{0,2},{1,3},{2,0},{3,1},{4,6},{5,7},{6,4},{7,5},{8,10},{9,11},{10,... | collective-permute-start | bytes 786440 | tf_op jit(solution)/shard_map/ppermute | solution.py:403
  58.7 5.4 %collective-permute-start.6 = (bf16[3,96,128]{2,1,0:T(8,128)(2,1)}, bf16[3,96,128]{2,1,0:T(8,128)(2,1)S(1)}, u32[]{:S(2)}, u32[]{:S(2)}) collective-permute-start(bf16[3,96,128]{2,1,0:T(8,128)(2,1)} %copy-done.18), channel_id=1, source_target_pairs={{24,0},{0,8},{8,16},{16,24},{25,1},{1,9},{9,17},{17,25},{26,2},{2,... | collective-permute-start | bytes 221192 | tf_op jit(solution)/shard_map/ppermute | solution.py:24
  59.5 4.5 %collective-permute-start.7 = (bf16[3,96,128]{2,1,0:T(8,128)(2,1)}, bf16[3,96,128]{2,1,0:T(8,128)(2,1)S(1)}, u32[]{:S(2)}, u32[]{:S(2)}) collective-permute-start(bf16[3,96,128]{2,1,0:T(8,128)(2,1)} %copy-done.17), channel_id=1, source_target_pairs={{8,0},{16,8},{24,16},{0,24},{9,1},{17,9},{25,17},{1,25},{10,2},{18... | collective-permute-start | bytes 221192 | tf_op jit(solution)/shard_map/ppermute | solution.py:24
  64.1 0.7 copy-start.9
  64.7 0.7 copy-start.11
  66.9 12.7 %copy-start.14 = (bf16[8,8,96,128]{3,2,1,0:T(8,128)(2,1)S(1)}, bf16[8,8,96,128]{3,2,1,0:T(8,128)(2,1)}, u32[]{:S(2)}) copy-start(bf16[8,8,96,128]{3,2,1,0:T(8,128)(2,1)} %copy-done.12) | copy-start | bytes 4718596
  66.9 12.7 %copy-start.16 = (bf16[288,864]{1,0:T(8,128)(2,1)S(1)}, bf16[288,864]{1,0:T(8,128)(2,1)}, u32[]{:S(2)}) copy-start(bf16[288,864]{1,0:T(8,128)(2,1)} %copy-done.15) | copy-start | bytes 1492996
  66.9 12.7 %copy-start.20 = (s32[1,16,8]{1,2,0:T(8,128)S(1)}, s32[1,16,8]{1,2,0:T(8,128)}, u32[]{:S(2)}) copy-start(s32[1,16,8]{1,2,0:T(8,128)} %param.10) | copy-start | bytes 1540
  68.0 9.5 %collective-permute-start.10 = (f32[256,128]{1,0:T(8,128)S(1)}, f32[256,128]{1,0:T(8,128)S(1)}, u32[]{:S(2)}, u32[]{:S(2)}) collective-permute-start(f32[256,128]{1,0:T(8,128)S(1)} %get-tuple-element.76), channel_id=1, source_target_pairs={{0,4},{1,5},{2,6},{3,7},{4,0},{5,1},{6,2},{7,3},{8,12},{9,13},{10,... | collective-permute-start | bytes 393224 | tf_op jit(solution)/shard_map/ppermute | solution.py:403
  68.1 10.2 %collective-permute-start.8 = (bf16[4,96,128]{2,1,0:T(8,128)(2,1)S(1)}, bf16[4,96,128]{2,1,0:T(8,128)(2,1)S(1)}, u32[]{:S(2)}, u32[]{:S(2)}) collective-permute-start(bf16[4,96,128]{2,1,0:T(8,128)(2,1)S(1)} %get-tuple-element.72), channel_id=1, source_target_pairs={{0,1},{1,2},{2,3},{3,4},{4,5},{5,6},{6,7},{8,9},{9,10},{10,11},{11... | collective-permute-start | bytes 294920 | tf_op jit(solution)/shard_map/ppermute | solution.py:30
  73.4 6.2 %collective-permute-start.9 = (bf16[4,96,128]{2,1,0:T(8,128)(2,1)S(1)}, bf16[4,96,128]{2,1,0:T(8,128)(2,1)S(1)}, u32[]{:S(2)}, u32[]{:S(2)}) collective-permute-start(bf16[4,96,128]{2,1,0:T(8,128)(2,1)S(1)} %get-tuple-element.73), channel_id=1, source_target_pairs={{1,0},{2,1},{3,2},{4,3},{5,4},{6,5},{7,6},{9,8},{10,9},{11,10},{12... | collective-permute-start | bytes 294920 | tf_op jit(solution)/shard_map/ppermute | solution.py:30
  77.5 6.4 %collective-permute-start.11 = (f32[256,128]{1,0:T(8,128)S(1)}, f32[256,128]{1,0:T(8,128)S(1)}, u32[]{:S(2)}, u32[]{:S(2)}) collective-permute-start(f32[256,128]{1,0:T(8,128)S(1)} %get-tuple-element.80.refs_0_), channel_id=1, source_target_pairs={{0,8},{1,9},{2,10},{3,11},{4,12},{5,13},{6,14},{7,15},{8,0},{9,1},... | collective-permute-start | bytes 393224 | tf_op jit(solution)/shard_map/ppermute | solution.py:403
  84.0 6.7 %collective-permute-start.12 = (f32[256,128]{1,0:T(8,128)S(1)}, f32[256,128]{1,0:T(8,128)S(1)}, u32[]{:S(2)}, u32[]{:S(2)}) collective-permute-start(f32[256,128]{1,0:T(8,128)S(1)} %get-tuple-element.84.refs_0_), channel_id=1, source_target_pairs={{0,16},{1,17},{2,18},{3,19},{4,20},{5,21},{6,22},{7,23},{8,24},{9,... | collective-permute-start | bytes 393224 | tf_op jit(solution)/shard_map/ppermute | solution.py:403
  90.7 4.4 %collective-permute-start.13 = (bf16[256,128]{1,0:T(8,128)(2,1)S(1)}, bf16[256,128]{1,0:T(8,128)(2,1)S(1)}, u32[]{:S(2)}, u32[]{:S(2)}) collective-permute-start(bf16[256,128]{1,0:T(8,128)(2,1)S(1)} %get-tuple-element.88.refs_1_), channel_id=1, source_target_pairs={{0,4},{1,5},{2,6},{3,7},{4,0},{5,1},{6,2},{7,3},{8,12},{9,13},{10,... | collective-permute-start | bytes 196616 | tf_op jit(solution)/shard_map/ppermute | solution.py:403
  95.1 8.5 %collective-permute-start.14 = (bf16[512,128]{1,0:T(8,128)(2,1)S(1)}, bf16[512,128]{1,0:T(8,128)(2,1)S(1)}, u32[]{:S(2)}, u32[]{:S(2)}) collective-permute-start(bf16[512,128]{1,0:T(8,128)(2,1)S(1)} %get-tuple-element.92.refs_1_), channel_id=1, source_target_pairs={{0,2},{1,3},{2,0},{3,1},{4,6},{5,7},{6,4},{7,5},{8,10},{9,11},{10,... | collective-permute-start | bytes 393224 | tf_op jit(solution)/shard_map/ppermute | solution.py:403
  103.7 2.6 %collective-permute-start.15 = (bf16[1024,128]{1,0:T(8,128)(2,1)S(1)}, bf16[1024,128]{1,0:T(8,128)(2,1)S(1)}, u32[]{:S(2)}, u32[]{:S(2)}) collective-permute-start(bf16[1024,128]{1,0:T(8,128)(2,1)S(1)} %get-tuple-element.96.refs_1_), channel_id=1, source_target_pairs={{0,1},{1,0},{2,3},{3,2},{4,5},{5,4},{6,7},{7,6},{8,9},{9,8},{10,11... | collective-permute-start | bytes 786440 | tf_op jit(solution)/shard_map/ppermute | solution.py:403

commit v3 on v2

--- a/solution.py
+++ b/solution.py
@@ -16,6 +16,7 @@
 LANES = 128
 HALF = 64
 ROWS = 2048
+GROUPS = 2
 
 
 def passed_along(block, axis, distance):
@@ -24,10 +25,12 @@
     return lax.ppermute(block, axis, route)
 
 
-def from_behind(block, axis, distance):
+def exchanged(first, second, axis):
     devices = range(lax.axis_size(axis))
-    route = [(i - distance, i) for i in devices if i - distance in devices]
-    return lax.ppermute(block, axis, route)
+    inside = [(i, i ^ 1) for i in devices]
+    across = [(i, ((i + 1) ^ 1) - 1) for i in devices]
+    across = [(i, j) for i, j in across if j in devices]
+    return lax.ppermute(first, axis, inside), lax.ppermute(second, axis, across)
 
 
 def lane_ids(channels):
@@ -89,13 +92,14 @@
         flipped[rows, :] = jnp.concatenate(blocks, axis=1)
 
 
-def column_kernel(cells, field, below, above, low_out, high_out, *, side):
+def column_kernel(cells, odd, field, below, above, inside, across, *, side):
     channels = field.shape[2]
     slots = 2 * field.shape[0]
     lanes = lane_ids(channels)
-    for out, line, place in ((low_out, 0, 0), (high_out, side - 1, 56)):
-        corner = line % 2 * HALF + place
-        for quarter in range(4):
+    for quarter in range(4):
+        both = []
+        for line, place in ((0, 0), (side - 1, 56)):
+            corner = line % 2 * HALF + place
             total = jnp.zeros((channels, LANES), BF)
             for half in range(2):
                 layer = quarter + 4 * half
@@ -114,16 +118,19 @@
                     goal = half * HALF + (side + 1) * 8
                     row = turn(above[line // 2], (goal - corner) % LANES)
                     total = jnp.where(lanes // 8 == goal // 8, row, total)
-            out[quarter] = total
-
-
-def fill_table(table, field, below_x, above_x, below_y, above_y, sem):
+            both.append(total)
+        inside[quarter] = jnp.where(odd[0] == 1, both[0], both[1])
+        across[quarter] = jnp.where(odd[0] == 1, both[1], both[0])
+
+
+def fill_table(table, field, below_x, above_x, inside, across, odd, sem):
     pairs, _, channels, _ = field.shape
     low = lane_ids(channels) < HALF
     copy = pltpu.make_async_copy(field, table.at[pl.ds(0, pairs)], sem)
     copy.start()
     for quarter in range(4):
-        below, above = below_y[quarter], above_y[quarter]
+        below = jnp.where(odd[0] == 1, inside[quarter], across[quarter])
+        above = jnp.where(odd[0] == 1, across[quarter], inside[quarter])
         table[pairs, quarter] = jnp.where(low, below, turn(above, HALF))
         table[pairs, quarter + 4] = jnp.where(low, turn(below, HALF), above)
     tiles = below_x.shape[0]
@@ -235,7 +242,7 @@
 
 
 def forward_kernel(
-    cells, links, counts, mine, below_x, above_x, below_y, above_y, matrix, field, given,
+    cells, links, counts, odd, below_x, above_x, inside, across, matrix, field, given,
     out, grad, kept, sent, low_out, high_out,
     table, columns, shifted, carry_ref, total, terms, upstream, sems, *, side,
 ):
@@ -243,7 +250,7 @@
     slots = 2 * pairs
     copy = pltpu.make_async_copy(given, upstream, sems.at[1])
     copy.start()
-    fill_table(table, field, below_x, above_x, below_y, above_y, sems.at[0])
+    fill_table(table, field, below_x, above_x, inside, across, odd, sems.at[0])
     total[...] = jnp.zeros(total.shape, F32)
     shifted[...] = jnp.zeros(shifted.shape, BF)
     upper = (lane_ids(channels) >= HALF).astype(jnp.int32)
@@ -280,7 +287,7 @@
         gather_terms(4)
         return carry
 
-    lax.fori_loop(0, pairs // 2, body, 0)
+    lax.fori_loop(0, pairs // 2, body, 0, unroll=True)
     height, width = total.shape
     terms[...] = jnp.zeros(terms.shape, F32)
     for tile in range(-(-width // LANES)):
@@ -289,32 +296,38 @@
             :, tile * LANES : end
         ]
     half = kept.shape[0]
-    kept[...] = terms[pl.ds(pl.multiple_of(mine[0] * half, half), half), :]
-    sent[...] = terms[pl.ds(pl.multiple_of((1 - mine[0]) * half, half), half), :]
+    kept[...] = terms[pl.ds(pl.multiple_of(odd[0] * half, half), half), :]
+    sent[...] = terms[pl.ds(pl.multiple_of((1 - odd[0]) * half, half), half), :]
     edge_rows(cells, grad, low_out, high_out, slots, side)
 
 
 def backward_kernel(
-    links, counts, below_x, above_x, below_y, above_y, matrix, field, given,
-    out, table, columns, carry_ref, upstream, sems, *, side, group,
+    links, counts, odd, below_x, above_x, inside, across, matrix, field, given,
+    out, table, columns, carry_ref, upstream, sems, *, side, first,
 ):
     pairs, _, channels, _ = field.shape
-    copy = pltpu.make_async_copy(given.at[pl.ds(2 * group, 2)], upstream, sems.at[1])
+    copy = pltpu.make_async_copy(given.at[pl.ds(2 * first, out.shape[0])], upstream, sems.at[1])
     copy.start()
-    fill_table(table, field, below_x, above_x, below_y, above_y, sems.at[0])
+    fill_table(table, field, below_x, above_x, inside, across, odd, sems.at[0])
     upper = (lane_ids(channels) >= HALF).astype(jnp.int32)
-    build = column_builder(group, links, table, columns, pairs, side)
-
-    def finish(t, left, right):
-        for h in range(2):
-            live = 2 * (group * 2 + h) + upper < counts[0]
-            for odd, back in ((0, left), (1, right)):
-                x = 2 * t + odd
-                gradient = upstream[h, x].astype(F32) + back[:, h * LANES : (h + 1) * LANES]
-                out[h, x] = jnp.where(live, gradient, 0.0).astype(BF)
-
     copy.wait()
-    convolve_group(matrix, columns, carry_ref, build, finish)
+
+    def body(index, carry):
+        group = first + index
+        build = column_builder(group, links, table, columns, pairs, side)
+
+        def finish(t, left, right):
+            for h in range(2):
+                pair = 2 * index + h
+                live = 2 * (group * 2 + h) + upper < counts[0]
+                for x, back in ((2 * t, left), (2 * t + 1, right)):
+                    gradient = upstream[pair, x].astype(F32) + back[:, h * LANES : (h + 1) * LANES]
+                    out[pair, x] = jnp.where(live, gradient, 0.0).astype(BF)
+
+        convolve_group(matrix, columns, carry_ref, build, finish)
+        return carry
+
+    lax.fori_loop(0, out.shape[0] // 2, body, 0, unroll=True)
 
 
 def native_kernel(*refs):
@@ -412,9 +425,10 @@
         after = [tasks[step](mark)] if step in tasks else []
         if step + 1 < len(inner):
             half = like(block, 0.5)
-            block, sent, mark = call(split_kernel, [half, half], 1, 2, after=after)(
+            block, sent, _ = call(split_kernel, [half, half], 1, 2, after=after)(
                 bit_of_me(order[step + 1]), block, received
             )
+            mark = sent
         elif step < len(inner) + len(outer):
             last = step + 1 == len(inner) + len(outer)
             kernel = functools.partial(add_kernel, scale=scale if last else None)
@@ -455,11 +469,11 @@
         cotangent.reshape(channels, slots, voxels)
     )
     make_columns = functools.partial(column_kernel, side=side)
-    low_column, high_column, mark = call(make_columns, [column, column], 1, 3, after=[mark])(
-        cells, prepared, below_x, above_x
+    odd = (lax.axis_index("gy") % 2).reshape(1)
+    *both, mark = call(make_columns, [column, column], 2, 3, after=[mark])(
+        cells, odd, prepared, below_x, above_x
     )
-    below_y = from_behind(high_column, "gy", 1)
-    above_y = from_behind(low_column, "gy", -1)
+    inside, across = exchanged(*both, "gy")
     stacked = jax.ShapeDtypeStruct((3 * channels, 9 * channels), BF)
     matrix, flipped, _ = call(weights_kernel, [stacked, stacked], 0, 1, after=[mark])(weight)
 
@@ -483,8 +497,7 @@
         n_any=2,
         room=20,
     )(
-        cells, links, count, bit_of_me(sum_bits()[0][0]),
-        below_x, above_x, below_y, above_y, matrix, prepared, upstream,
+        cells, links, count, odd, below_x, above_x, inside, across, matrix, prepared, upstream,
     )
 
     halos = [passed_along(high_edge, "gx", 1), passed_along(low_edge, "gx", -1)]
@@ -492,29 +505,28 @@
     done = {}
 
     def columns_task(mark):
-        low_column, high_column, mark = call(
-            make_columns, [column, column], 1, 3, after=[mark]
-        )(cells, grad, *halos)
-        halos.append(from_behind(high_column, "gy", 1))
-        halos.append(from_behind(low_column, "gy", -1))
+        *both, mark = call(make_columns, [column, column], 2, 3, after=[mark])(
+            cells, odd, grad, *halos
+        )
+        halos.extend(exchanged(*both, "gy"))
         return mark
 
     def output_task(mark):
         done["output"], mark = call(native_kernel, [native], 0, 1, after=[mark])(output)
         return mark
 
-    def backward_task(group, mark):
+    def backward_task(first, mark):
         part, mark = call(
-            functools.partial(backward_kernel, side=side, group=group),
-            [jax.ShapeDtypeStruct((2, 8, channels, LANES), BF)],
-            2,
+            functools.partial(backward_kernel, side=side, first=first),
+            [jax.ShapeDtypeStruct((2 * GROUPS, 8, channels, LANES), BF)],
+            3,
             5,
-            [table, columns, carry_ref, pltpu.VMEM((2, 8, channels, LANES), BF), sems],
-            4 * flops // pairs,
+            [table, columns, carry_ref, pltpu.VMEM((2 * GROUPS, 8, channels, LANES), BF), sems],
+            2 * GROUPS * flops // pairs,
             n_any=2,
             room=12,
             after=[mark],
-        )(links, count, *halos, flipped, grad, upstream)
+        )(links, count, odd, *halos, flipped, grad, upstream)
         parts.append(part)
         return mark
 
@@ -523,7 +535,7 @@
         return mark
 
     tasks = [columns_task, output_task]
-    tasks += [functools.partial(backward_task, group) for group in range(pairs // 2)]
+    tasks += [functools.partial(backward_task, group) for group in range(0, pairs // 2, GROUPS)]
     tasks += [gradient_task]
     device_total = lax.axis_size("gx") * lax.axis_size("gy")
     scale = 1.0 / math.sqrt(voxels * slots * device_total)

time: 108 us -> 97.9 us (0.906)
  Pallas kernels: 55.6 us -> 46.5 us
  starting transfers between devices: 29.5 us -> 25.8 us
  waiting for transfers between devices: 8.8 us -> 12 us
    pallas_call x20 -> x18, Pallas kernels: 55.6 us -> 46.5 us  [call(): return lambda *args: called(*args, *after)]
    ppermute x8, waiting for transfers between devices: 3.48 us -> 7.46 us  [swapped(): return lax.ppermute(block, axes, [(i, i ^ bit) for i in range(devices)])]
    ppermute x4, starting transfers between devices: 13.4 us -> 9.87 us  [the longest x2 6.09 us: exchanged(): lax.ppermute(second, axis, across)]
    unnamed x42 -> x46, local copies, waits for them, and re-layouts: 11.9 us -> 11.5 us
  transfers between devices with their start and end apart: 16 -> 16, of which waited for: 6 -> 9; matrix products, arithmetic and copies ran while one was open for 0% -> 0% of each run, Pallas kernels for 24% -> 22%
where the time goes in v3:
time: 97.9 us; the launch traced here: 97.3 us
  Pallas kernels  46.5 us (47%)
  starting transfers between devices  25.8 us (26%)
  waiting for transfers between devices  12 us (12%)
  local copies, waits for them, and re-layouts  11.5 us (12%)
  between operations  1.48 us (2%)
    pallas_call x18, Pallas kernels, call(): return lambda *args: called(*args, *after)  46.5 us
    unnamed x46, local copies, waits for them, and re-layouts  11.5 us
    ppermute x8, starting transfers between devices, swapped(): return lax.ppermute(block, axes, [(i, i ^ bit) for i in range(devices)])  8.52 us
    ppermute x8, waiting for transfers between devices, swapped(): return lax.ppermute(block, axes, [(i, i ^ bit) for i in range(devices)])  7.46 us
    ppermute x4, starting transfers between devices, passed_along(): return lax.ppermute(block, axis, route)  7.42 us
    ppermute x2, starting transfers between devices, exchanged(): lax.ppermute(second, axis, across)  6.09 us
    ppermute x2, starting transfers between devices, exchanged(): lax.ppermute(first, axis, inside)  3.78 us
    ppermute x4, waiting for transfers between devices, passed_along(): return lax.ppermute(block, axis, route)  3.13 us
  transfers between devices with their start and end apart: 16, of which 9 were waited for; matrix products, arithmetic and copies ran while one was open for 0% of the time, Pallas kernels for 22%

profile of v3, /device:TPU:1, one launch (start us, length us, event | category | flops | bytes accessed | tf_op | source)
XLA Modules:
  0.0 97.3 jit_solution(1959661949382199416)
XLA Ops:
  0.6 1.4 %copy-done = bf16[96,1,16,512]{3,2,1,0:T(8,128)(2,1)S(1)} copy-done((bf16[96,1,16,512]{3,2,1,0:T(8,128)(2,1)S(1)}, bf16[96,1,16,512]{3,2,1,0:T(8,128)(2,1)}, u32[]{:S(2)}) %copy-start) | copy-done | bytes 1572888
  2.0 0.7 copy-done.11
  2.7 2.1 %shard_map.85 = (bf16[8,8,96,128]{3,2,1,0:T(8,128)(2,1)S(1)}, bf16[3,96,128]{2,1,0:T(8,128)(2,1)S(1)}, bf16[3,96,128]{2,1,0:T(8,128)(2,1)S(1)}, f32[8,128]{1,0:T(8,128)}) custom-call(s32[36]{0:T(128)S(1)} %bitcast.22, bf16[96,16,512]{2,1,0:T(8,128)(2,1)S(1)} %bitcast.20), custom_call_target="tpu_custom_call" | custom-call | bytes 4194304 | tf_op jit(solution)/shard_map/pallas_call | solution.py:376
  4.8 2.1 %collective-permute-start = (bf16[3,96,128]{2,1,0:T(8,128)(2,1)S(1)}, bf16[3,96,128]{2,1,0:T(8,128)(2,1)S(1)}, u32[]{:S(2)}, u32[]{:S(2)}) collective-permute-start(bf16[3,96,128]{2,1,0:T(8,128)(2,1)S(1)} %get-tuple-element.43), channel_id=1, source_target_pairs={{24,0},{0,8},{8,16},{16,24},{25,1},{1,9},{9,17},{17,25},{26,2},{2,... | collective-permute-start | bytes 221192 | tf_op jit(solution)/shard_map/ppermute | solution.py:25
  7.0 2.0 %collective-permute-start.1 = (bf16[3,96,128]{2,1,0:T(8,128)(2,1)S(1)}, bf16[3,96,128]{2,1,0:T(8,128)(2,1)S(1)}, u32[]{:S(2)}, u32[]{:S(2)}) collective-permute-start(bf16[3,96,128]{2,1,0:T(8,128)(2,1)S(1)} %get-tuple-element.44), channel_id=1, source_target_pairs={{8,0},{16,8},{24,16},{0,24},{9,1},{17,9},{25,17},{1,25},{10,2},{18... | collective-permute-start | bytes 221192 | tf_op jit(solution)/shard_map/ppermute | solution.py:25
  9.0 0.9 shard_map.86
  10.0 0.0 copy-start.14
  10.0 1.1 %copy-done.14 = bf16[8,8,96,128]{3,2,1,0:T(8,128)(2,1)} copy-done((bf16[8,8,96,128]{3,2,1,0:T(8,128)(2,1)}, bf16[8,8,96,128]{3,2,1,0:T(8,128)(2,1)S(1)}, u32[]{:S(2)}) %copy-start.14) | copy-done | bytes 1572888
  11.1 0.0 collective-permute-done.refs_3_.refs_4_
  11.1 1.0 %collective-permute-done.1.refs_4_.refs_5_ = bf16[3,96,128]{2,1,0:T(8,128)(2,1)S(1)} collective-permute-done((bf16[3,96,128]{2,1,0:T(8,128)(2,1)S(1)}, bf16[3,96,128]{2,1,0:T(8,128)(2,1)S(1)}, u32[]{:S(2)}, u32[]{:S(2)}) %collective-permute-start.1) | collective-permute-done | bytes 73760 | tf_op jit(solution)/shard_map/ppermute | solution.py:25
  12.1 1.4 %shard_map.87 = (bf16[4,96,128]{2,1,0:T(8,128)(2,1)S(1)}, bf16[4,96,128]{2,1,0:T(8,128)(2,1)S(1)}, f32[8,128]{1,0:T(8,128)S(1)}) custom-call(s32[36]{0:T(128)S(1)} %bitcast.23, s32[1]{0:T(128)} %bitcast.4.refs_1_.refs_3_.refs_2_, bf16[8,8,96,128]{3,2,1,0:T(8,128)(2,1)S(1)} %get-tuple-element.45.refs_2_.refs_9_, ...), custom_call_target="tpu_custom_call" | custom-call | bytes 4194304 | tf_op jit(solution)/shard_map/pallas_call | solution.py:376
  13.6 1.2 %collective-permute-start.2 = (bf16[4,96,128]{2,1,0:T(8,128)(2,1)S(1)}, bf16[4,96,128]{2,1,0:T(8,128)(2,1)S(1)}, u32[]{:S(2)}, u32[]{:S(2)}) collective-permute-start(bf16[4,96,128]{2,1,0:T(8,128)(2,1)S(1)} %get-tuple-element.47), channel_id=1, source_target_pairs={{0,1},{1,0},{2,3},{3,2},{4,5},{5,4},{6,7},{7,6},{8,9},{9,8},{10,11... | collective-permute-start | bytes 294920 | tf_op jit(solution)/shard_map/ppermute | solution.py:33
  14.8 3.0 %collective-permute-start.3 = (bf16[4,96,128]{2,1,0:T(8,128)(2,1)S(1)}, bf16[4,96,128]{2,1,0:T(8,128)(2,1)S(1)}, u32[]{:S(2)}, u32[]{:S(2)}) collective-permute-start(bf16[4,96,128]{2,1,0:T(8,128)(2,1)S(1)} %get-tuple-element.48), channel_id=1, source_target_pairs={{1,2},{2,1},{3,4},{4,3},{5,6},{6,5},{9,10},{10,9},{11,12},{12,11},... | collective-permute-start | bytes 294920 | tf_op jit(solution)/shard_map/ppermute | solution.py:33
  18.4 1.6 %shard_map.88 = (bf16[288,864]{1,0:T(8,128)(2,1)S(1)}, bf16[288,864]{1,0:T(8,128)(2,1)S(1)}, f32[8,128]{1,0:T(8,128)}) custom-call(bf16[96,2592]{1,0:T(8,128)(2,1)S(1)} %copy-done.8, f32[8,128]{1,0:T(8,128)S(1)} %get-tuple-element.49.refs_1_), custom_call_target="tpu_custom_call" | custom-call | bytes 4194304 | tf_op jit(solution)/shard_map/pallas_call | solution.py:376
  20.1 0.8 copy-done.17
  20.9 0.0 collective-permute-done.2.refs_6_
  20.9 0.6 collective-permute-done.3.refs_7_
  21.4 17.1 %shard_map.89 = (bf16[8,8,96,128]{3,2,1,0:T(8,128)(2,1)S(1)}, bf16[8,8,96,128]{3,2,1,0:T(8,128)(2,1)S(1)}, f32[1024,128]{1,0:T(8,128)S(1)}, f32[1024,128]{1,0:T(...) custom-call(s32[36]{0:T(128)S(1)} %bitcast.24, s32[8,16]{1,0:T(8,128)S(1)} %bitcast.26, ...), custom_call_target="tpu_custom_call" | custom-call | flops 8153726976 | bytes 4194304 | tf_op jit(solution)/shard_map/pallas_call | solution.py:376
  38.5 0.0 copy-start.2
  38.6 1.1 %copy-done.2 = bf16[8,8,96,128]{3,2,1,0:T(8,128)(2,1)} copy-done((bf16[8,8,96,128]{3,2,1,0:T(8,128)(2,1)}, bf16[8,8,96,128]{3,2,1,0:T(8,128)(2,1)S(1)}, u32[]{:S(2)}) %copy-start.2) | copy-done | bytes 1572888
  39.7 0.8 copy-done.4
  40.5 0.6 copy-done.19
  41.1 0.6 copy-done.20
  41.8 0.0 collective-permute-start.4
  41.8 2.1 %collective-permute-done.4.refs_2_ = f32[1024,128]{1,0:T(8,128)S(1)} collective-permute-done((f32[1024,128]{1,0:T(8,128)}, f32[1024,128]{1,0:T(8,128)S(1)}, u32[]{:S(2)}, u32[]{:S(2)}) %collective-permute-start.4) | collective-permute-done | bytes 524320 | tf_op jit(solution)/shard_map/ppermute | solution.py:416
  43.9 0.8 copy-done.6
  44.7 1.0 %copy-done.5 = f32[1024,128]{1,0:T(8,128)S(1)} copy-done((f32[1024,128]{1,0:T(8,128)S(1)}, f32[1024,128]{1,0:T(8,128)}, u32[]{:S(2)}) %copy-start.5) | copy-done | bytes 524312
  45.7 1.0 %copy-done.7 = f32[1024,128]{1,0:T(8,128)S(1)} copy-done((f32[1024,128]{1,0:T(8,128)S(1)}, f32[1024,128]{1,0:T(8,128)}, u32[]{:S(2)}) %copy-start.7) | copy-done | bytes 524312
  46.8 0.6 shard_map.90
  47.4 0.7 copy-done.9
  48.1 1.8 %collective-permute-start.5 = (f32[512,128]{1,0:T(8,128)S(1)}, f32[512,128]{1,0:T(8,128)}, u32[]{:S(2)}, u32[]{:S(2)}) collective-permute-start(f32[512,128]{1,0:T(8,128)S(1)} %get-tuple-element.56.refs_5_), channel_id=1, source_target_pairs={{0,2},{1,3},{2,0},{3,1},{4,6},{5,7},{6,4},{7,5},{8,10},{9,11},{10,... | collective-permute-start | bytes 786440 | tf_op jit(solution)/shard_map/ppermute | solution.py:416
  49.9 0.8 collective-permute-start.6
  50.7 2.4 %collective-permute-start.7 = (bf16[3,96,128]{2,1,0:T(8,128)(2,1)}, bf16[3,96,128]{2,1,0:T(8,128)(2,1)S(1)}, u32[]{:S(2)}, u32[]{:S(2)}) collective-permute-start(bf16[3,96,128]{2,1,0:T(8,128)(2,1)} %copy-done.19), channel_id=1, source_target_pairs={{8,0},{16,8},{24,16},{0,24},{9,1},{17,9},{25,17},{1,25},{10,2},{18... | collective-permute-start | bytes 221192 | tf_op jit(solution)/shard_map/ppermute | solution.py:25
  53.1 2.1 %collective-permute-done.6.refs_3_ = bf16[3,96,128]{2,1,0:T(8,128)(2,1)S(1)} collective-permute-done((bf16[3,96,128]{2,1,0:T(8,128)(2,1)}, bf16[3,96,128]{2,1,0:T(8,128)(2,1)S(1)}, u32[]{:S(2)}, u32[]{:S(2)}) %collective-permute-start.6) | collective-permute-done | bytes 73760 | tf_op jit(solution)/shard_map/ppermute | solution.py:25
  55.2 0.0 collective-permute-done.7.refs_4_
  55.2 0.7 copy-done.13
  55.9 1.4 %shard_map.91 = (bf16[4,96,128]{2,1,0:T(8,128)(2,1)S(1)}, bf16[4,96,128]{2,1,0:T(8,128)(2,1)S(1)}, f32[8,128]{1,0:T(8,128)S(1)}) custom-call(s32[36]{0:T(128)S(1)} %bitcast.25, s32[1]{0:T(128)} %bitcast.4.refs_1_.refs_3_.refs_2_, bf16[8,8,96,128]{3,2,1,0:T(8,128)(2,1)S(1)} %get-tuple-element.57.refs_2_.refs_8_, ...), custom_call_target="tpu_custom_call" | custom-call | bytes 4194304 | tf_op jit(solution)/shard_map/pallas_call | solution.py:376
  57.4 0.0 copy-start.16
  57.4 0.0 copy-start.22
  57.4 0.0 collective-permute-done.5.refs_2_
  57.4 1.7 %shard_map.92 = (f32[256,128]{1,0:T(8,128)S(1)}, f32[256,128]{1,0:T(8,128)S(1)}, f32[8,128]{1,0:T(8,128)}) custom-call(s32[1]{0:T(128)} %bitcast.7.refs_0_, f32[512,128]{1,0:T(8,128)S(1)} %copy-done.10, f32[512,128]{1,0:T(8,128)} %collective-permute-done.5.refs_2_, f32[8,128]{1,0:T(8,128)S(1)} %get-tuple-element.60.refs_3_), custom_call_target="tpu_custom_call" | custom-call | bytes 4194304 | tf_op jit(solution)/shard_map/pallas_call | solution.py:376
  59.1 0.1 collective-permute-start.10
  59.1 2.6 %collective-permute-start.8 = (bf16[4,96,128]{2,1,0:T(8,128)(2,1)S(1)}, bf16[4,96,128]{2,1,0:T(8,128)(2,1)S(1)}, u32[]{:S(2)}, u32[]{:S(2)}) collective-permute-start(bf16[4,96,128]{2,1,0:T(8,128)(2,1)S(1)} %get-tuple-element.63), channel_id=1, source_target_pairs={{0,1},{1,0},{2,3},{3,2},{4,5},{5,4},{6,7},{7,6},{8,9},{9,8},{10,11... | collective-permute-start | bytes 294920 | tf_op jit(solution)/shard_map/ppermute | solution.py:33
  61.7 3.1 %collective-permute-start.9 = (bf16[4,96,128]{2,1,0:T(8,128)(2,1)S(1)}, bf16[4,96,128]{2,1,0:T(8,128)(2,1)S(1)}, u32[]{:S(2)}, u32[]{:S(2)}) collective-permute-start(bf16[4,96,128]{2,1,0:T(8,128)(2,1)S(1)} %get-tuple-element.64), channel_id=1, source_target_pairs={{1,2},{2,1},{3,4},{4,3},{5,6},{6,5},{9,10},{10,9},{11,12},{12,11},... | collective-permute-start | bytes 294920 | tf_op jit(solution)/shard_map/ppermute | solution.py:33
  64.8 2.0 %shard_map.93 = (bf16[96,16,512]{2,1,0:T(8,128)(2,1)}, f32[8,128]{1,0:T(8,128)S(1)}) custom-call(bf16[8,8,96,128]{3,2,1,0:T(8,128)(2,1)S(1)} %copy-done.3, f32[256,128]{1,0:T(8,128)S(1)} %get-tuple-element.61.refs_1_), custom_call_target="tpu_custom_call" | custom-call | bytes 4194304 | tf_op jit(solution)/shard_map/pallas_call | solution.py:376
  66.9 0.0 collective-permute-done.10.refs_1_
  66.9 0.7 collective-permute-start.11
  67.5 0.0 collective-permute-done.8.refs_5_
  67.5 0.9 collective-permute-done.9.refs_6_
  68.4 6.5 %shard_map.95 = (bf16[4,8,96,128]{3,2,1,0:T(8,128)(2,1)S(1)}, f32[8,128]{1,0:T(8,128)S(1)}) custom-call(s32[8,16]{1,0:T(8,128)S(1)} %bitcast.27, s32[1]{0:T(128)} %bitcast.18.refs_1_, s32[1]{0:T(128)} %bitcast.4.refs_1_.refs_3_.refs_2_, bf16[3,96,128]{2,1,0:T(8,128)(2,1)S(1)} %collective-permute-done.6.refs_3_, ...), custom_call_target="tpu_custom_call" | custom-call | flops 2038431744 | bytes 4194304 | tf_op jit(solution)/shard_map/pallas_call | solution.py:376
  74.9 0.0 collective-permute-done.11.refs_1_
  75.0 1.9 %collective-permute-start.12 = (f32[256,128]{1,0:T(8,128)S(1)}, f32[256,128]{1,0:T(8,128)S(1)}, u32[]{:S(2)}, u32[]{:S(2)}) collective-permute-start(f32[256,128]{1,0:T(8,128)S(1)} %get-tuple-element.74.refs_0_), channel_id=1, source_target_pairs={{0,16},{1,17},{2,18},{3,19},{4,20},{5,21},{6,22},{7,23},{8,24},{9,... | collective-permute-start | bytes 393224 | tf_op jit(solution)/shard_map/ppermute | solution.py:416
  76.9 6.5 %shard_map.97 = (bf16[4,8,96,128]{3,2,1,0:T(8,128)(2,1)S(1)}, f32[8,128]{1,0:T(8,128)S(1)}) custom-call(s32[8,16]{1,0:T(8,128)S(1)} %bitcast.28, s32[1]{0:T(128)} %bitcast.19.refs_1_, s32[1]{0:T(128)} %bitcast.4.refs_1_.refs_3_.refs_2_, bf16[3,96,128]{2,1,0:T(8,128)(2,1)S(1)} %collective-permute-done.6.refs_3_, ...), custom_call_target="tpu_custom_call" | custom-call | flops 2038431744 | bytes 4194304 | tf_op jit(solution)/shard_map/pallas_call | solution.py:376
  83.4 0.6 collective-permute-done.12.refs_1_
  84.1 0.5 collective-permute-start.13
  84.5 2.0 %shard_map.99 = (bf16[96,16,512]{2,1,0:T(8,128)(2,1)}, f32[8,128]{1,0:T(8,128)S(1)}) custom-call(bf16[4,8,96,128]{3,2,1,0:T(8,128)(2,1)S(1)} %get-tuple-element.69.refs_0_, bf16[4,8,96,128]{3,2,1,0:T(8,128)(2,1)S(1)} %get-tuple-element.73.refs_1_, f32[8,128]{1,0:T(8,128)S(1)} %get-tuple-element.76.refs_2_), custom_call_target="tpu_custom_call" | custom-call | bytes 4194304 | tf_op jit(solution)/shard_map/pallas_call | solution.py:376
  86.6 0.7 collective-permute-done.13.refs_2_
  87.2 0.6 shard_map.100
  87.9 1.0 collective-permute-start.14
  88.8 2.9 %collective-permute-done.14.refs_2_ = bf16[512,128]{1,0:T(8,128)(2,1)S(1)} collective-permute-done((bf16[512,128]{1,0:T(8,128)(2,1)S(1)}, bf16[512,128]{1,0:T(8,128)(2,1)S(1)}, u32[]{:S(2)}, u32[]{:S(2)}) %collective-permute-start.14) | collective-permute-done | bytes 131104 | tf_op jit(solution)/shard_map/ppermute | solution.py:416
  91.7 0.6 shard_map.101
  92.3 2.7 %collective-permute-start.15 = (bf16[1024,128]{1,0:T(8,128)(2,1)S(1)}, bf16[1024,128]{1,0:T(8,128)(2,1)S(1)}, u32[]{:S(2)}, u32[]{:S(2)}) collective-permute-start(bf16[1024,128]{1,0:T(8,128)(2,1)S(1)} %get-tuple-element.81.refs_1_), channel_id=1, source_target_pairs={{0,1},{1,0},{2,3},{3,2},{4,5},{5,4},{6,7},{7,6},{8,9},{9,8},{10,11... | collective-permute-start | bytes 786440 | tf_op jit(solution)/shard_map/ppermute | solution.py:416
  95.0 1.2 %collective-permute-done.15.refs_2_ = bf16[1024,128]{1,0:T(8,128)(2,1)S(1)} collective-permute-done((bf16[1024,128]{1,0:T(8,128)(2,1)S(1)}, bf16[1024,128]{1,0:T(8,128)(2,1)S(1)}, u32[]{:S(2)}, u32[]{:S(2)}) %collective-permute-start.15) | collective-permute-done | bytes 262176 | tf_op jit(solution)/shard_map/ppermute | solution.py:416
  96.1 1.2 %shard_map.102 = (f32[96,2592]{1,0:T(8,128)}, f32[8,128]{1,0:T(8,128)}) custom-call(s32[1]{0:T(128)} %bitcast.14.refs_0_, bf16[1024,128]{1,0:T(8,128)(2,1)S(1)} %get-tuple-element.81.refs_1_, bf16[1024,128]{1,0:T(8,128)(2,1)S(1)} %collective-permute-done.15.refs_2_), custom_call_target="tpu_custom_call" | custom-call | bytes 4194304 | tf_op jit(solution)/shard_map/pallas_call | solution.py:376
  (32 shorter events, 0.1 us)
Async XLA Ops:
  0.6 1.4 %copy-start = (bf16[96,1,16,512]{3,2,1,0:T(8,128)(2,1)S(1)}, bf16[96,1,16,512]{3,2,1,0:T(8,128)(2,1)}, u32[]{:S(2)}) copy-start(bf16[96,1,16,512]{3,2,1,0:T(8,128)(2,1)} %param.6) | copy-start | bytes 4718596
  2.0 0.7 copy-start.11
  2.7 6.3 %copy-start.1 = (bf16[96,1,16,512]{3,2,1,0:T(8,128)(2,1)S(1)}, bf16[96,1,16,512]{3,2,1,0:T(8,128)(2,1)}, u32[]{:S(2)}) copy-start(bf16[96,1,16,512]{3,2,1,0:T(8,128)(2,1)} %param.7) | copy-start | bytes 4718596
  2.7 9.4 %copy-start.12 = (s32[1,36]{1,0:T(1,128)S(1)}, s32[1,36]{1,0:T(1,128)}, u32[]{:S(2)}) copy-start(s32[1,36]{1,0:T(1,128)} %param.9) | copy-start | bytes 436
  4.8 6.3 %collective-permute-start = (bf16[3,96,128]{2,1,0:T(8,128)(2,1)S(1)}, bf16[3,96,128]{2,1,0:T(8,128)(2,1)S(1)}, u32[]{:S(2)}, u32[]{:S(2)}) collective-permute-start(bf16[3,96,128]{2,1,0:T(8,128)(2,1)S(1)} %get-tuple-element.43), channel_id=1, source_target_pairs={{24,0},{0,8},{8,16},{16,24},{25,1},{1,9},{9,17},{17,25},{26,2},{2,... | collective-permute-start | bytes 221192 | tf_op jit(solution)/shard_map/ppermute | solution.py:25
  7.0 5.1 %collective-permute-start.1 = (bf16[3,96,128]{2,1,0:T(8,128)(2,1)S(1)}, bf16[3,96,128]{2,1,0:T(8,128)(2,1)S(1)}, u32[]{:S(2)}, u32[]{:S(2)}) collective-permute-start(bf16[3,96,128]{2,1,0:T(8,128)(2,1)S(1)} %get-tuple-element.44), channel_id=1, source_target_pairs={{8,0},{16,8},{24,16},{0,24},{9,1},{17,9},{25,17},{1,25},{10,2},{18... | collective-permute-start | bytes 221192 | tf_op jit(solution)/shard_map/ppermute | solution.py:25
  9.0 12.4 %copy-start.21 = (s32[1,16,8]{1,2,0:T(8,128)S(1)}, s32[1,16,8]{1,2,0:T(8,128)}, u32[]{:S(2)}) copy-start(s32[1,16,8]{1,2,0:T(8,128)} %param.10) | copy-start | bytes 1540
  10.0 1.1 %copy-start.14 = (bf16[8,8,96,128]{3,2,1,0:T(8,128)(2,1)}, bf16[8,8,96,128]{3,2,1,0:T(8,128)(2,1)S(1)}, u32[]{:S(2)}) copy-start(bf16[8,8,96,128]{3,2,1,0:T(8,128)(2,1)S(1)} %get-tuple-element.51.refs_10_.refs_9_) | copy-start | bytes 4718596
  11.1 7.3 %copy-start.8 = (bf16[96,2592]{1,0:T(8,128)(2,1)S(1)}, bf16[96,2592]{1,0:T(8,128)(2,1)}, u32[]{:S(2)}) copy-start(bf16[96,2592]{1,0:T(8,128)(2,1)} %refs_0_.1) | copy-start | bytes 1492996
  11.1 10.3 %copy-start.15 = (bf16[8,8,96,128]{3,2,1,0:T(8,128)(2,1)S(1)}, bf16[8,8,96,128]{3,2,1,0:T(8,128)(2,1)}, u32[]{:S(2)}) copy-start(bf16[8,8,96,128]{3,2,1,0:T(8,128)(2,1)} %copy-done.14) | copy-start | bytes 4718596
  13.6 7.3 %collective-permute-start.2 = (bf16[4,96,128]{2,1,0:T(8,128)(2,1)S(1)}, bf16[4,96,128]{2,1,0:T(8,128)(2,1)S(1)}, u32[]{:S(2)}, u32[]{:S(2)}) collective-permute-start(bf16[4,96,128]{2,1,0:T(8,128)(2,1)S(1)} %get-tuple-element.47), channel_id=1, source_target_pairs={{0,1},{1,0},{2,3},{3,2},{4,5},{5,4},{6,7},{7,6},{8,9},{9,8},{10,11... | collective-permute-start | bytes 294920 | tf_op jit(solution)/shard_map/ppermute | solution.py:33
  14.8 6.7 %collective-permute-start.3 = (bf16[4,96,128]{2,1,0:T(8,128)(2,1)S(1)}, bf16[4,96,128]{2,1,0:T(8,128)(2,1)S(1)}, u32[]{:S(2)}, u32[]{:S(2)}) collective-permute-start(bf16[4,96,128]{2,1,0:T(8,128)(2,1)S(1)} %get-tuple-element.48), channel_id=1, source_target_pairs={{1,2},{2,1},{3,4},{4,3},{5,6},{6,5},{9,10},{10,9},{11,12},{12,11},... | collective-permute-start | bytes 294920 | tf_op jit(solution)/shard_map/ppermute | solution.py:33
  20.1 0.8 copy-start.17
  38.5 1.1 %copy-start.2 = (bf16[8,8,96,128]{3,2,1,0:T(8,128)(2,1)}, bf16[8,8,96,128]{3,2,1,0:T(8,128)(2,1)S(1)}, u32[]{:S(2)}) copy-start(bf16[8,8,96,128]{3,2,1,0:T(8,128)(2,1)S(1)} %get-tuple-element.52.refs_0_) | copy-start | bytes 4718596
  39.7 0.8 copy-start.4
  40.5 0.6 copy-start.19
  41.1 0.6 copy-start.20
  41.8 2.1 %collective-permute-start.4 = (f32[1024,128]{1,0:T(8,128)}, f32[1024,128]{1,0:T(8,128)S(1)}, u32[]{:S(2)}, u32[]{:S(2)}) collective-permute-start(f32[1024,128]{1,0:T(8,128)} %get-tuple-element.54), channel_id=1, source_target_pairs={{0,1},{1,0},{2,3},{3,2},{4,5},{5,4},{6,7},{7,6},{8,9},{9,8},{10,11... | collective-permute-start | bytes 1572872 | tf_op jit(solution)/shard_map/ppermute | solution.py:416
  43.9 0.8 copy-start.6
  44.7 1.0 %copy-start.5 = (f32[1024,128]{1,0:T(8,128)S(1)}, f32[1024,128]{1,0:T(8,128)}, u32[]{:S(2)}) copy-start(f32[1024,128]{1,0:T(8,128)} %copy-done.4) | copy-start | bytes 1572868
  45.7 1.0 %copy-start.7 = (f32[1024,128]{1,0:T(8,128)S(1)}, f32[1024,128]{1,0:T(8,128)}, u32[]{:S(2)}) copy-start(f32[1024,128]{1,0:T(8,128)} %copy-done.6) | copy-start | bytes 1572868
  46.8 18.1 %copy-start.3 = (bf16[8,8,96,128]{3,2,1,0:T(8,128)(2,1)S(1)}, bf16[8,8,96,128]{3,2,1,0:T(8,128)(2,1)}, u32[]{:S(2)}) copy-start(bf16[8,8,96,128]{3,2,1,0:T(8,128)(2,1)} %copy-done.2) | copy-start | bytes 4718596
  47.3 0.7 copy-start.9
  48.1 9.3 %collective-permute-start.5 = (f32[512,128]{1,0:T(8,128)S(1)}, f32[512,128]{1,0:T(8,128)}, u32[]{:S(2)}, u32[]{:S(2)}) collective-permute-start(f32[512,128]{1,0:T(8,128)S(1)} %get-tuple-element.56.refs_5_), channel_id=1, source_target_pairs={{0,2},{1,3},{2,0},{3,1},{4,6},{5,7},{6,4},{7,5},{8,10},{9,11},{10,... | collective-permute-start | bytes 786440 | tf_op jit(solution)/shard_map/ppermute | solution.py:416
  49.9 5.4 %collective-permute-start.6 = (bf16[3,96,128]{2,1,0:T(8,128)(2,1)}, bf16[3,96,128]{2,1,0:T(8,128)(2,1)S(1)}, u32[]{:S(2)}, u32[]{:S(2)}) collective-permute-start(bf16[3,96,128]{2,1,0:T(8,128)(2,1)} %copy-done.20), channel_id=1, source_target_pairs={{24,0},{0,8},{8,16},{16,24},{25,1},{1,9},{9,17},{17,25},{26,2},{2,... | collective-permute-start | bytes 221192 | tf_op jit(solution)/shard_map/ppermute | solution.py:25
  50.7 4.5 %collective-permute-start.7 = (bf16[3,96,128]{2,1,0:T(8,128)(2,1)}, bf16[3,96,128]{2,1,0:T(8,128)(2,1)S(1)}, u32[]{:S(2)}, u32[]{:S(2)}) collective-permute-start(bf16[3,96,128]{2,1,0:T(8,128)(2,1)} %copy-done.19), channel_id=1, source_target_pairs={{8,0},{16,8},{24,16},{0,24},{9,1},{17,9},{25,17},{1,25},{10,2},{18... | collective-permute-start | bytes 221192 | tf_op jit(solution)/shard_map/ppermute | solution.py:25
  53.1 4.3 %copy-start.10 = (f32[512,128]{1,0:T(8,128)S(1)}, f32[512,128]{1,0:T(8,128)}, u32[]{:S(2)}) copy-start(f32[512,128]{1,0:T(8,128)} %copy-done.9) | copy-start | bytes 786436
  55.2 0.7 copy-start.13
  57.4 11.0 %copy-start.16 = (bf16[8,8,96,128]{3,2,1,0:T(8,128)(2,1)S(1)}, bf16[8,8,96,128]{3,2,1,0:T(8,128)(2,1)}, u32[]{:S(2)}) copy-start(bf16[8,8,96,128]{3,2,1,0:T(8,128)(2,1)} %copy-done.14) | copy-start | bytes 4718596
  57.4 11.0 %copy-start.18 = (bf16[288,864]{1,0:T(8,128)(2,1)S(1)}, bf16[288,864]{1,0:T(8,128)(2,1)}, u32[]{:S(2)}) copy-start(bf16[288,864]{1,0:T(8,128)(2,1)} %copy-done.17) | copy-start | bytes 1492996
  57.4 11.0 %copy-start.22 = (s32[1,16,8]{1,2,0:T(8,128)S(1)}, s32[1,16,8]{1,2,0:T(8,128)}, u32[]{:S(2)}) copy-start(s32[1,16,8]{1,2,0:T(8,128)} %param.10) | copy-start | bytes 1540
  59.1 7.8 %collective-permute-start.10 = (f32[256,128]{1,0:T(8,128)S(1)}, f32[256,128]{1,0:T(8,128)S(1)}, u32[]{:S(2)}, u32[]{:S(2)}) collective-permute-start(f32[256,128]{1,0:T(8,128)S(1)} %get-tuple-element.61.refs_1_), channel_id=1, source_target_pairs={{0,4},{1,5},{2,6},{3,7},{4,0},{5,1},{6,2},{7,3},{8,12},{9,13},{10,... | collective-permute-start | bytes 393224 | tf_op jit(solution)/shard_map/ppermute | solution.py:416
  59.1 8.4 %collective-permute-start.8 = (bf16[4,96,128]{2,1,0:T(8,128)(2,1)S(1)}, bf16[4,96,128]{2,1,0:T(8,128)(2,1)S(1)}, u32[]{:S(2)}, u32[]{:S(2)}) collective-permute-start(bf16[4,96,128]{2,1,0:T(8,128)(2,1)S(1)} %get-tuple-element.63), channel_id=1, source_target_pairs={{0,1},{1,0},{2,3},{3,2},{4,5},{5,4},{6,7},{7,6},{8,9},{9,8},{10,11... | collective-permute-start | bytes 294920 | tf_op jit(solution)/shard_map/ppermute | solution.py:33
  61.7 6.7 %collective-permute-start.9 = (bf16[4,96,128]{2,1,0:T(8,128)(2,1)S(1)}, bf16[4,96,128]{2,1,0:T(8,128)(2,1)S(1)}, u32[]{:S(2)}, u32[]{:S(2)}) collective-permute-start(bf16[4,96,128]{2,1,0:T(8,128)(2,1)S(1)} %get-tuple-element.64), channel_id=1, source_target_pairs={{1,2},{2,1},{3,4},{4,3},{5,6},{6,5},{9,10},{10,9},{11,12},{12,11},... | collective-permute-start | bytes 294920 | tf_op jit(solution)/shard_map/ppermute | solution.py:33
  66.9 8.1 %collective-permute-start.11 = (f32[256,128]{1,0:T(8,128)S(1)}, f32[256,128]{1,0:T(8,128)S(1)}, u32[]{:S(2)}, u32[]{:S(2)}) collective-permute-start(f32[256,128]{1,0:T(8,128)S(1)} %get-tuple-element.70.refs_0_), channel_id=1, source_target_pairs={{0,8},{1,9},{2,10},{3,11},{4,12},{5,13},{6,14},{7,15},{8,0},{9,1},... | collective-permute-start | bytes 393224 | tf_op jit(solution)/shard_map/ppermute | solution.py:416
  75.0 9.1 %collective-permute-start.12 = (f32[256,128]{1,0:T(8,128)S(1)}, f32[256,128]{1,0:T(8,128)S(1)}, u32[]{:S(2)}, u32[]{:S(2)}) collective-permute-start(f32[256,128]{1,0:T(8,128)S(1)} %get-tuple-element.74.refs_0_), channel_id=1, source_target_pairs={{0,16},{1,17},{2,18},{3,19},{4,20},{5,21},{6,22},{7,23},{8,24},{9,... | collective-permute-start | bytes 393224 | tf_op jit(solution)/shard_map/ppermute | solution.py:416
  84.1 3.2 %collective-permute-start.13 = (bf16[256,128]{1,0:T(8,128)(2,1)S(1)}, bf16[256,128]{1,0:T(8,128)(2,1)S(1)}, u32[]{:S(2)}, u32[]{:S(2)}) collective-permute-start(bf16[256,128]{1,0:T(8,128)(2,1)S(1)} %get-tuple-element.78.refs_1_), channel_id=1, source_target_pairs={{0,4},{1,5},{2,6},{3,7},{4,0},{5,1},{6,2},{7,3},{8,12},{9,13},{10,... | collective-permute-start | bytes 196616 | tf_op jit(solution)/shard_map/ppermute | solution.py:416
  87.9 3.8 %collective-permute-start.14 = (bf16[512,128]{1,0:T(8,128)(2,1)S(1)}, bf16[512,128]{1,0:T(8,128)(2,1)S(1)}, u32[]{:S(2)}, u32[]{:S(2)}) collective-permute-start(bf16[512,128]{1,0:T(8,128)(2,1)S(1)} %get-tuple-element.80.refs_1_), channel_id=1, source_target_pairs={{0,2},{1,3},{2,0},{3,1},{4,6},{5,7},{6,4},{7,5},{8,10},{9,11},{10,... | collective-permute-start | bytes 393224 | tf_op jit(solution)/shard_map/ppermute | solution.py:416
  92.3 3.9 %collective-permute-start.15 = (bf16[1024,128]{1,0:T(8,128)(2,1)S(1)}, bf16[1024,128]{1,0:T(8,128)(2,1)S(1)}, u32[]{:S(2)}, u32[]{:S(2)}) collective-permute-start(bf16[1024,128]{1,0:T(8,128)(2,1)S(1)} %get-tuple-element.81.refs_1_), channel_id=1, source_target_pairs={{0,1},{1,0},{2,3},{3,2},{4,5},{5,4},{6,7},{7,6},{8,9},{9,8},{10,11... | collective-permute-start | bytes 786440 | tf_op jit(solution)/shard_map/ppermute | solution.py:416

commit v4 on v3

--- a/solution.py
+++ b/solution.py
@@ -534,9 +534,9 @@
         done["grad"], mark = call(native_kernel, [native], 0, len(parts), after=[mark])(*parts)
         return mark
 
-    tasks = [columns_task, output_task]
+    tasks = [columns_task, lambda mark: mark]
     tasks += [functools.partial(backward_task, group) for group in range(0, pairs // 2, GROUPS)]
-    tasks += [gradient_task]
+    tasks += [gradient_task, output_task]
     device_total = lax.axis_size("gx") * lax.axis_size("gy")
     scale = 1.0 / math.sqrt(voxels * slots * device_total)
     mine, block, received, after = summed(kept, sent, mark, scale, dict(enumerate(tasks, 1)))

time: 97.9 us -> 96.9 us (0.990)
  local copies, waits for them, and re-layouts: 11.5 us -> 9.87 us
    unnamed x46 -> x42, local copies, waits for them, and re-layouts: 11.5 us -> 9.87 us
    ppermute x2, waiting for transfers between devices: 1.43 us -> 2.89 us  [exchanged(): lax.ppermute(second, axis, across)]
    ppermute x8, waiting for transfers between devices: 7.46 us -> 6.37 us  [swapped(): return lax.ppermute(block, axes, [(i, i ^ bit) for i in range(devices)])]
where the time goes in v4:
time: 96.9 us; the launch traced here: 96.2 us
  Pallas kernels  46.8 us (48%)
  starting transfers between devices  25.6 us (26%)
  waiting for transfers between devices  12.4 us (13%)
  local copies, waits for them, and re-layouts  9.87 us (10%)
  between operations  1.47 us (2%)
    pallas_call x18, Pallas kernels, call(): return lambda *args: called(*args, *after)  46.8 us
    unnamed x42, local copies, waits for them, and re-layouts  9.87 us
    ppermute x8, starting transfers between devices, swapped(): return lax.ppermute(block, axes, [(i, i ^ bit) for i in range(devices)])  8.39 us
    ppermute x4, starting transfers between devices, passed_along(): return lax.ppermute(block, axis, route)  7.42 us
    ppermute x8, waiting for transfers between devices, swapped(): return lax.ppermute(block, axes, [(i, i ^ bit) for i in range(devices)])  6.37 us
    ppermute x2, starting transfers between devices, exchanged(): lax.ppermute(second, axis, across)  6.08 us
    ppermute x2, starting transfers between devices, exchanged(): lax.ppermute(first, axis, inside)  3.75 us
    ppermute x4, waiting for transfers between devices, passed_along(): return lax.ppermute(block, axis, route)  3.13 us
  transfers between devices with their start and end apart: 16, of which 9 were waited for; matrix products, arithmetic and copies ran while one was open for 0% of the time, Pallas kernels for 22%

profile of v4, /device:TPU:1, one launch (start us, length us, event | category | flops | bytes accessed | tf_op | source)
XLA Modules:
  0.0 96.2 jit_solution(4784088414059210979)
XLA Ops:
  0.6 0.0 copy-start
  0.6 1.4 %copy-done = bf16[96,1,16,512]{3,2,1,0:T(8,128)(2,1)S(1)} copy-done((bf16[96,1,16,512]{3,2,1,0:T(8,128)(2,1)S(1)}, bf16[96,1,16,512]{3,2,1,0:T(8,128)(2,1)}, u32[]{:S(2)}) %copy-start) | copy-done | bytes 1572888
  2.0 0.7 copy-done.9
  2.7 2.1 %shard_map.85 = (bf16[8,8,96,128]{3,2,1,0:T(8,128)(2,1)S(1)}, bf16[3,96,128]{2,1,0:T(8,128)(2,1)S(1)}, bf16[3,96,128]{2,1,0:T(8,128)(2,1)S(1)}, f32[8,128]{1,0:T(8,128)}) custom-call(s32[36]{0:T(128)S(1)} %bitcast.22, bf16[96,16,512]{2,1,0:T(8,128)(2,1)S(1)} %bitcast.20), custom_call_target="tpu_custom_call" | custom-call | bytes 4194304 | tf_op jit(solution)/shard_map/pallas_call | solution.py:376
  4.9 2.1 %collective-permute-start = (bf16[3,96,128]{2,1,0:T(8,128)(2,1)S(1)}, bf16[3,96,128]{2,1,0:T(8,128)(2,1)S(1)}, u32[]{:S(2)}, u32[]{:S(2)}) collective-permute-start(bf16[3,96,128]{2,1,0:T(8,128)(2,1)S(1)} %get-tuple-element.44), channel_id=1, source_target_pairs={{24,0},{0,8},{8,16},{16,24},{25,1},{1,9},{9,17},{17,25},{26,2},{2,... | collective-permute-start | bytes 221192 | tf_op jit(solution)/shard_map/ppermute | solution.py:25
  7.0 2.0 %collective-permute-start.1 = (bf16[3,96,128]{2,1,0:T(8,128)(2,1)S(1)}, bf16[3,96,128]{2,1,0:T(8,128)(2,1)S(1)}, u32[]{:S(2)}, u32[]{:S(2)}) collective-permute-start(bf16[3,96,128]{2,1,0:T(8,128)(2,1)S(1)} %get-tuple-element.45), channel_id=1, source_target_pairs={{8,0},{16,8},{24,16},{0,24},{9,1},{17,9},{25,17},{1,25},{10,2},{18... | collective-permute-start | bytes 221192 | tf_op jit(solution)/shard_map/ppermute | solution.py:25
  9.0 0.0 copy-done.1
  9.0 0.9 shard_map.86
  10.0 0.0 copy-start.12
  10.0 1.1 %copy-done.12 = bf16[8,8,96,128]{3,2,1,0:T(8,128)(2,1)} copy-done((bf16[8,8,96,128]{3,2,1,0:T(8,128)(2,1)}, bf16[8,8,96,128]{3,2,1,0:T(8,128)(2,1)S(1)}, u32[]{:S(2)}) %copy-start.12) | copy-done | bytes 1572888
  11.1 0.0 collective-permute-done.refs_3_.refs_4_
  11.1 1.0 %collective-permute-done.1.refs_4_.refs_5_ = bf16[3,96,128]{2,1,0:T(8,128)(2,1)S(1)} collective-permute-done((bf16[3,96,128]{2,1,0:T(8,128)(2,1)S(1)}, bf16[3,96,128]{2,1,0:T(8,128)(2,1)S(1)}, u32[]{:S(2)}, u32[]{:S(2)}) %collective-permute-start.1) | collective-permute-done | bytes 73760 | tf_op jit(solution)/shard_map/ppermute | solution.py:25
  12.1 0.0 copy-done.10
  12.1 1.4 %shard_map.87 = (bf16[4,96,128]{2,1,0:T(8,128)(2,1)S(1)}, bf16[4,96,128]{2,1,0:T(8,128)(2,1)S(1)}, f32[8,128]{1,0:T(8,128)S(1)}) custom-call(s32[36]{0:T(128)S(1)} %bitcast.23, s32[1]{0:T(128)} %bitcast.4.refs_1_.refs_3_.refs_2_, bf16[8,8,96,128]{3,2,1,0:T(8,128)(2,1)S(1)} %get-tuple-element.46.refs_2_.refs_9_, ...), custom_call_target="tpu_custom_call" | custom-call | bytes 4194304 | tf_op jit(solution)/shard_map/pallas_call | solution.py:376
  13.6 0.0 copy-done.2
  13.6 1.2 %collective-permute-start.2 = (bf16[4,96,128]{2,1,0:T(8,128)(2,1)S(1)}, bf16[4,96,128]{2,1,0:T(8,128)(2,1)S(1)}, u32[]{:S(2)}, u32[]{:S(2)}) collective-permute-start(bf16[4,96,128]{2,1,0:T(8,128)(2,1)S(1)} %get-tuple-element.48), channel_id=1, source_target_pairs={{0,1},{1,0},{2,3},{3,2},{4,5},{5,4},{6,7},{7,6},{8,9},{9,8},{10,11... | collective-permute-start | bytes 294920 | tf_op jit(solution)/shard_map/ppermute | solution.py:33
  14.8 3.0 %collective-permute-start.3 = (bf16[4,96,128]{2,1,0:T(8,128)(2,1)S(1)}, bf16[4,96,128]{2,1,0:T(8,128)(2,1)S(1)}, u32[]{:S(2)}, u32[]{:S(2)}) collective-permute-start(bf16[4,96,128]{2,1,0:T(8,128)(2,1)S(1)} %get-tuple-element.49), channel_id=1, source_target_pairs={{1,2},{2,1},{3,4},{4,3},{5,6},{6,5},{9,10},{10,9},{11,12},{12,11},... | collective-permute-start | bytes 294920 | tf_op jit(solution)/shard_map/ppermute | solution.py:33
  18.5 1.6 %shard_map.88 = (bf16[288,864]{1,0:T(8,128)(2,1)S(1)}, bf16[288,864]{1,0:T(8,128)(2,1)S(1)}, f32[8,128]{1,0:T(8,128)}) custom-call(bf16[96,2592]{1,0:T(8,128)(2,1)S(1)} %copy-done.6, f32[8,128]{1,0:T(8,128)S(1)} %get-tuple-element.50.refs_1_), custom_call_target="tpu_custom_call" | custom-call | bytes 4194304 | tf_op jit(solution)/shard_map/pallas_call | solution.py:376
  20.1 0.8 copy-done.15
  20.9 0.0 collective-permute-done.2.refs_6_
  20.9 0.6 collective-permute-done.3.refs_7_
  21.5 1.4 %copy-done.3 = bf16[8,8,96,128]{3,2,1,0:T(8,128)(2,1)S(1)} copy-done((bf16[8,8,96,128]{3,2,1,0:T(8,128)(2,1)S(1)}, bf16[8,8,96,128]{3,2,1,0:T(8,128)(2,1)}, u32[]{:S(2)}) %copy-start.3) | copy-done | bytes 1572888
  22.9 17.1 %shard_map.89 = (bf16[8,8,96,128]{3,2,1,0:T(8,128)(2,1)S(1)}, bf16[8,8,96,128]{3,2,1,0:T(8,128)(2,1)S(1)}, f32[1024,128]{1,0:T(8,128)S(1)}, f32[1024,128]{1,0:T(...) custom-call(s32[36]{0:T(128)S(1)} %bitcast.24, s32[8,16]{1,0:T(8,128)S(1)} %bitcast.26, ...), custom_call_target="tpu_custom_call" | custom-call | flops 8153726976 | bytes 4194304 | tf_op jit(solution)/shard_map/pallas_call | solution.py:376
  40.0 0.0 copy-start.4
  40.0 0.8 copy-done.4
  40.8 0.6 copy-done.17
  41.4 0.6 copy-done.18
  42.0 0.0 collective-permute-start.4
  42.0 2.2 %collective-permute-done.4.refs_2_ = f32[1024,128]{1,0:T(8,128)} collective-permute-done((f32[1024,128]{1,0:T(8,128)}, f32[1024,128]{1,0:T(8,128)}, u32[]{:S(2)}, u32[]{:S(2)}) %collective-permute-start.4) | collective-permute-done | bytes 524320 | tf_op jit(solution)/shard_map/ppermute | solution.py:416
  44.3 1.0 %copy-done.5 = f32[1024,128]{1,0:T(8,128)S(1)} copy-done((f32[1024,128]{1,0:T(8,128)S(1)}, f32[1024,128]{1,0:T(8,128)}, u32[]{:S(2)}) %copy-start.5) | copy-done | bytes 524312
  45.3 1.6 %shard_map.90 = (f32[512,128]{1,0:T(8,128)S(1)}, f32[512,128]{1,0:T(8,128)S(1)}, f32[8,128]{1,0:T(8,128)}) custom-call(s32[1]{0:T(128)} %bitcast.8.refs_0_, f32[1024,128]{1,0:T(8,128)S(1)} %copy-done.5, f32[1024,128]{1,0:T(8,128)} %collective-permute-done.4.refs_2_), custom_call_target="tpu_custom_call" | custom-call | bytes 4194304 | tf_op jit(solution)/shard_map/pallas_call | solution.py:376
  46.9 0.7 copy-done.7
  47.6 1.8 %collective-permute-start.5 = (f32[512,128]{1,0:T(8,128)S(1)}, f32[512,128]{1,0:T(8,128)}, u32[]{:S(2)}, u32[]{:S(2)}) collective-permute-start(f32[512,128]{1,0:T(8,128)S(1)} %get-tuple-element.57.refs_5_), channel_id=1, source_target_pairs={{0,2},{1,3},{2,0},{3,1},{4,6},{5,7},{6,4},{7,5},{8,10},{9,11},{10,... | collective-permute-start | bytes 786440 | tf_op jit(solution)/shard_map/ppermute | solution.py:416
  49.4 0.8 collective-permute-start.6
  50.3 2.4 %collective-permute-start.7 = (bf16[3,96,128]{2,1,0:T(8,128)(2,1)}, bf16[3,96,128]{2,1,0:T(8,128)(2,1)S(1)}, u32[]{:S(2)}, u32[]{:S(2)}) collective-permute-start(bf16[3,96,128]{2,1,0:T(8,128)(2,1)} %copy-done.17), channel_id=1, source_target_pairs={{8,0},{16,8},{24,16},{0,24},{9,1},{17,9},{25,17},{1,25},{10,2},{18... | collective-permute-start | bytes 221192 | tf_op jit(solution)/shard_map/ppermute | solution.py:25
  52.7 2.1 %collective-permute-done.6.refs_3_ = bf16[3,96,128]{2,1,0:T(8,128)(2,1)S(1)} collective-permute-done((bf16[3,96,128]{2,1,0:T(8,128)(2,1)}, bf16[3,96,128]{2,1,0:T(8,128)(2,1)S(1)}, u32[]{:S(2)}, u32[]{:S(2)}) %collective-permute-start.6) | collective-permute-done | bytes 73760 | tf_op jit(solution)/shard_map/ppermute | solution.py:25
  54.8 0.0 collective-permute-done.7.refs_4_
  54.8 0.7 copy-done.11
  55.5 1.4 %shard_map.91 = (bf16[4,96,128]{2,1,0:T(8,128)(2,1)S(1)}, bf16[4,96,128]{2,1,0:T(8,128)(2,1)S(1)}, f32[8,128]{1,0:T(8,128)S(1)}) custom-call(s32[36]{0:T(128)S(1)} %bitcast.25, s32[1]{0:T(128)} %bitcast.4.refs_1_.refs_3_.refs_2_, bf16[8,8,96,128]{3,2,1,0:T(8,128)(2,1)S(1)} %get-tuple-element.58.refs_2_.refs_8_, ...), custom_call_target="tpu_custom_call" | custom-call | bytes 4194304 | tf_op jit(solution)/shard_map/pallas_call | solution.py:376
  56.9 0.0 collective-permute-done.5.refs_2_
  57.0 1.5 %shard_map.92 = (f32[256,128]{1,0:T(8,128)S(1)}, f32[256,128]{1,0:T(8,128)S(1)}, f32[8,128]{1,0:T(8,128)}) custom-call(s32[1]{0:T(128)} %bitcast.7.refs_0_, f32[512,128]{1,0:T(8,128)S(1)} %copy-done.8, f32[512,128]{1,0:T(8,128)} %collective-permute-done.5.refs_2_, f32[8,128]{1,0:T(8,128)S(1)} %get-tuple-element.61.refs_3_), custom_call_target="tpu_custom_call" | custom-call | bytes 4194304 | tf_op jit(solution)/shard_map/pallas_call | solution.py:376
  58.5 0.1 collective-permute-start.8
  58.6 2.6 %collective-permute-start.10 = (bf16[4,96,128]{2,1,0:T(8,128)(2,1)S(1)}, bf16[4,96,128]{2,1,0:T(8,128)(2,1)S(1)}, u32[]{:S(2)}, u32[]{:S(2)}) collective-permute-start(bf16[4,96,128]{2,1,0:T(8,128)(2,1)S(1)} %get-tuple-element.65), channel_id=1, source_target_pairs={{0,1},{1,0},{2,3},{3,2},{4,5},{5,4},{6,7},{7,6},{8,9},{9,8},{10,11... | collective-permute-start | bytes 294920 | tf_op jit(solution)/shard_map/ppermute | solution.py:33
  61.2 3.1 %collective-permute-start.11 = (bf16[4,96,128]{2,1,0:T(8,128)(2,1)S(1)}, bf16[4,96,128]{2,1,0:T(8,128)(2,1)S(1)}, u32[]{:S(2)}, u32[]{:S(2)}) collective-permute-start(bf16[4,96,128]{2,1,0:T(8,128)(2,1)S(1)} %get-tuple-element.66), channel_id=1, source_target_pairs={{1,2},{2,1},{3,4},{4,3},{5,6},{6,5},{9,10},{10,9},{11,12},{12,11},... | collective-permute-start | bytes 294920 | tf_op jit(solution)/shard_map/ppermute | solution.py:33
  64.2 0.0 collective-permute-done.8.refs_1_
  64.3 1.2 %collective-permute-start.9 = (f32[256,128]{1,0:T(8,128)S(1)}, f32[256,128]{1,0:T(8,128)S(1)}, u32[]{:S(2)}, u32[]{:S(2)}) collective-permute-start(f32[256,128]{1,0:T(8,128)S(1)} %get-tuple-element.64.refs_0_), channel_id=1, source_target_pairs={{0,8},{1,9},{2,10},{3,11},{4,12},{5,13},{6,14},{7,15},{8,0},{9,1},... | collective-permute-start | bytes 393224 | tf_op jit(solution)/shard_map/ppermute | solution.py:416
  65.5 0.0 collective-permute-done.10.refs_5_
  65.5 2.3 %collective-permute-done.11.refs_6_ = bf16[4,96,128]{2,1,0:T(8,128)(2,1)S(1)} collective-permute-done((bf16[4,96,128]{2,1,0:T(8,128)(2,1)S(1)}, bf16[4,96,128]{2,1,0:T(8,128)(2,1)S(1)}, u32[]{:S(2)}, u32[]{:S(2)}) %collective-permute-start.11) | collective-permute-done | bytes 98336 | tf_op jit(solution)/shard_map/ppermute | solution.py:33
  67.8 0.0 copy-done.16
  67.8 6.5 %shard_map.94 = (bf16[4,8,96,128]{3,2,1,0:T(8,128)(2,1)S(1)}, f32[8,128]{1,0:T(8,128)S(1)}) custom-call(s32[8,16]{1,0:T(8,128)S(1)} %bitcast.27, s32[1]{0:T(128)} %bitcast.18.refs_1_, s32[1]{0:T(128)} %bitcast.4.refs_1_.refs_3_.refs_2_, bf16[3,96,128]{2,1,0:T(8,128)(2,1)S(1)} %collective-permute-done.6.refs_3_, ...), custom_call_target="tpu_custom_call" | custom-call | flops 2038431744 | bytes 4194304 | tf_op jit(solution)/shard_map/pallas_call | solution.py:376
  74.4 0.0 collective-permute-done.9.refs_1_
  74.4 1.1 %collective-permute-start.12 = (f32[256,128]{1,0:T(8,128)S(1)}, f32[256,128]{1,0:T(8,128)S(1)}, u32[]{:S(2)}, u32[]{:S(2)}) collective-permute-start(f32[256,128]{1,0:T(8,128)S(1)} %get-tuple-element.70.refs_0_), channel_id=1, source_target_pairs={{0,16},{1,17},{2,18},{3,19},{4,20},{5,21},{6,22},{7,23},{8,24},{9,... | collective-permute-start | bytes 393224 | tf_op jit(solution)/shard_map/ppermute | solution.py:416
  75.5 6.5 %shard_map.96 = (bf16[4,8,96,128]{3,2,1,0:T(8,128)(2,1)S(1)}, f32[8,128]{1,0:T(8,128)S(1)}) custom-call(s32[8,16]{1,0:T(8,128)S(1)} %bitcast.28, s32[1]{0:T(128)} %bitcast.19.refs_1_, s32[1]{0:T(128)} %bitcast.4.refs_1_.refs_3_.refs_2_, bf16[3,96,128]{2,1,0:T(8,128)(2,1)S(1)} %collective-permute-done.6.refs_3_, ...), custom_call_target="tpu_custom_call" | custom-call | flops 2038431744 | bytes 4194304 | tf_op jit(solution)/shard_map/pallas_call | solution.py:376
  82.1 1.4 %collective-permute-done.12.refs_1_ = f32[256,128]{1,0:T(8,128)S(1)} collective-permute-done((f32[256,128]{1,0:T(8,128)S(1)}, f32[256,128]{1,0:T(8,128)S(1)}, u32[]{:S(2)}, u32[]{:S(2)}) %collective-permute-start.12) | collective-permute-done | bytes 131104 | tf_op jit(solution)/shard_map/ppermute | solution.py:416
  83.5 0.5 collective-permute-start.13
  83.9 2.0 %shard_map.98 = (bf16[96,16,512]{2,1,0:T(8,128)(2,1)}, f32[8,128]{1,0:T(8,128)S(1)}) custom-call(bf16[4,8,96,128]{3,2,1,0:T(8,128)(2,1)S(1)} %get-tuple-element.74.refs_0_, bf16[4,8,96,128]{3,2,1,0:T(8,128)(2,1)S(1)} %get-tuple-element.75.refs_1_, f32[8,128]{1,0:T(8,128)S(1)} %get-tuple-element.76.refs_2_), custom_call_target="tpu_custom_call" | custom-call | bytes 4194304 | tf_op jit(solution)/shard_map/pallas_call | solution.py:376
  86.0 0.7 collective-permute-done.13.refs_2_
  86.7 1.0 %collective-permute-start.14 = (bf16[512,128]{1,0:T(8,128)(2,1)S(1)}, bf16[512,128]{1,0:T(8,128)(2,1)S(1)}, u32[]{:S(2)}, u32[]{:S(2)}) collective-permute-start(bf16[512,128]{1,0:T(8,128)(2,1)S(1)} %get-tuple-element.81.refs_1_), channel_id=1, source_target_pairs={{0,2},{1,3},{2,0},{3,1},{4,6},{5,7},{6,4},{7,5},{8,10},{9,11},{10,... | collective-permute-start | bytes 393224 | tf_op jit(solution)/shard_map/ppermute | solution.py:416
  87.7 2.0 %shard_map.100 = (bf16[96,16,512]{2,1,0:T(8,128)(2,1)}, f32[8,128]{1,0:T(8,128)S(1)}) custom-call(bf16[8,8,96,128]{3,2,1,0:T(8,128)(2,1)S(1)} %get-tuple-element.53.refs_0_, f32[8,128]{1,0:T(8,128)S(1)} %get-tuple-element.78.refs_1_), custom_call_target="tpu_custom_call" | custom-call | bytes 4194304 | tf_op jit(solution)/shard_map/pallas_call | solution.py:376
  89.7 0.9 collective-permute-done.14.refs_2_
  90.6 0.6 shard_map.101
  91.2 2.7 %collective-permute-start.15 = (bf16[1024,128]{1,0:T(8,128)(2,1)S(1)}, bf16[1024,128]{1,0:T(8,128)(2,1)S(1)}, u32[]{:S(2)}, u32[]{:S(2)}) collective-permute-start(bf16[1024,128]{1,0:T(8,128)(2,1)S(1)} %get-tuple-element.83.refs_1_), channel_id=1, source_target_pairs={{0,1},{1,0},{2,3},{3,2},{4,5},{5,4},{6,7},{7,6},{8,9},{9,8},{10,11... | collective-permute-start | bytes 786440 | tf_op jit(solution)/shard_map/ppermute | solution.py:416
  93.9 1.2 %collective-permute-done.15.refs_2_ = bf16[1024,128]{1,0:T(8,128)(2,1)S(1)} collective-permute-done((bf16[1024,128]{1,0:T(8,128)(2,1)S(1)}, bf16[1024,128]{1,0:T(8,128)(2,1)S(1)}, u32[]{:S(2)}, u32[]{:S(2)}) %collective-permute-start.15) | collective-permute-done | bytes 262176 | tf_op jit(solution)/shard_map/ppermute | solution.py:416
  95.0 1.2 %shard_map.102 = (f32[96,2592]{1,0:T(8,128)}, f32[8,128]{1,0:T(8,128)}) custom-call(s32[1]{0:T(128)} %bitcast.14.refs_0_, bf16[1024,128]{1,0:T(8,128)(2,1)S(1)} %get-tuple-element.83.refs_1_, bf16[1024,128]{1,0:T(8,128)(2,1)S(1)} %collective-permute-done.15.refs_2_), custom_call_target="tpu_custom_call" | custom-call | bytes 4194304 | tf_op jit(solution)/shard_map/pallas_call | solution.py:376
  (28 shorter events, 0.1 us)
Async XLA Ops:
  0.6 1.4 %copy-start = (bf16[96,1,16,512]{3,2,1,0:T(8,128)(2,1)S(1)}, bf16[96,1,16,512]{3,2,1,0:T(8,128)(2,1)}, u32[]{:S(2)}) copy-start(bf16[96,1,16,512]{3,2,1,0:T(8,128)(2,1)} %param.6) | copy-start | bytes 4718596
  2.0 0.7 copy-start.9
  2.7 6.3 %copy-start.1 = (bf16[96,1,16,512]{3,2,1,0:T(8,128)(2,1)S(1)}, bf16[96,1,16,512]{3,2,1,0:T(8,128)(2,1)}, u32[]{:S(2)}) copy-start(bf16[96,1,16,512]{3,2,1,0:T(8,128)(2,1)} %param.7) | copy-start | bytes 4718596
  2.7 9.4 %copy-start.10 = (s32[1,36]{1,0:T(1,128)S(1)}, s32[1,36]{1,0:T(1,128)}, u32[]{:S(2)}) copy-start(s32[1,36]{1,0:T(1,128)} %param.9) | copy-start | bytes 436
  4.8 8.7 %copy-start.2 = (bf16[8,8,96,128]{3,2,1,0:T(8,128)(2,1)}, bf16[8,8,96,128]{3,2,1,0:T(8,128)(2,1)S(1)}, u32[]{:S(2)}) copy-start(bf16[8,8,96,128]{3,2,1,0:T(8,128)(2,1)S(1)} %get-tuple-element.46.refs_2_.refs_9_) | copy-start | bytes 4718596
  4.9 6.3 %collective-permute-start = (bf16[3,96,128]{2,1,0:T(8,128)(2,1)S(1)}, bf16[3,96,128]{2,1,0:T(8,128)(2,1)S(1)}, u32[]{:S(2)}, u32[]{:S(2)}) collective-permute-start(bf16[3,96,128]{2,1,0:T(8,128)(2,1)S(1)} %get-tuple-element.44), channel_id=1, source_target_pairs={{24,0},{0,8},{8,16},{16,24},{25,1},{1,9},{9,17},{17,25},{26,2},{2,... | collective-permute-start | bytes 221192 | tf_op jit(solution)/shard_map/ppermute | solution.py:25
  7.0 5.1 %collective-permute-start.1 = (bf16[3,96,128]{2,1,0:T(8,128)(2,1)S(1)}, bf16[3,96,128]{2,1,0:T(8,128)(2,1)S(1)}, u32[]{:S(2)}, u32[]{:S(2)}) collective-permute-start(bf16[3,96,128]{2,1,0:T(8,128)(2,1)S(1)} %get-tuple-element.45), channel_id=1, source_target_pairs={{8,0},{16,8},{24,16},{0,24},{9,1},{17,9},{25,17},{1,25},{10,2},{18... | collective-permute-start | bytes 221192 | tf_op jit(solution)/shard_map/ppermute | solution.py:25
  9.0 12.4 %copy-start.19 = (s32[1,16,8]{1,2,0:T(8,128)S(1)}, s32[1,16,8]{1,2,0:T(8,128)}, u32[]{:S(2)}) copy-start(s32[1,16,8]{1,2,0:T(8,128)} %param.10) | copy-start | bytes 1540
  10.0 1.1 %copy-start.12 = (bf16[8,8,96,128]{3,2,1,0:T(8,128)(2,1)}, bf16[8,8,96,128]{3,2,1,0:T(8,128)(2,1)S(1)}, u32[]{:S(2)}) copy-start(bf16[8,8,96,128]{3,2,1,0:T(8,128)(2,1)S(1)} %get-tuple-element.52.refs_10_.refs_9_) | copy-start | bytes 4718596
  11.1 7.3 %copy-start.6 = (bf16[96,2592]{1,0:T(8,128)(2,1)S(1)}, bf16[96,2592]{1,0:T(8,128)(2,1)}, u32[]{:S(2)}) copy-start(bf16[96,2592]{1,0:T(8,128)(2,1)} %refs_0_.1) | copy-start | bytes 1492996
  11.1 10.4 %copy-start.13 = (bf16[8,8,96,128]{3,2,1,0:T(8,128)(2,1)S(1)}, bf16[8,8,96,128]{3,2,1,0:T(8,128)(2,1)}, u32[]{:S(2)}) copy-start(bf16[8,8,96,128]{3,2,1,0:T(8,128)(2,1)} %copy-done.12) | copy-start | bytes 4718596
  13.6 7.3 %collective-permute-start.2 = (bf16[4,96,128]{2,1,0:T(8,128)(2,1)S(1)}, bf16[4,96,128]{2,1,0:T(8,128)(2,1)S(1)}, u32[]{:S(2)}, u32[]{:S(2)}) collective-permute-start(bf16[4,96,128]{2,1,0:T(8,128)(2,1)S(1)} %get-tuple-element.48), channel_id=1, source_target_pairs={{0,1},{1,0},{2,3},{3,2},{4,5},{5,4},{6,7},{7,6},{8,9},{9,8},{10,11... | collective-permute-start | bytes 294920 | tf_op jit(solution)/shard_map/ppermute | solution.py:33
  14.8 6.7 %collective-permute-start.3 = (bf16[4,96,128]{2,1,0:T(8,128)(2,1)S(1)}, bf16[4,96,128]{2,1,0:T(8,128)(2,1)S(1)}, u32[]{:S(2)}, u32[]{:S(2)}) collective-permute-start(bf16[4,96,128]{2,1,0:T(8,128)(2,1)S(1)} %get-tuple-element.49), channel_id=1, source_target_pairs={{1,2},{2,1},{3,4},{4,3},{5,6},{6,5},{9,10},{10,9},{11,12},{12,11},... | collective-permute-start | bytes 294920 | tf_op jit(solution)/shard_map/ppermute | solution.py:33
  20.1 0.8 copy-start.15
  21.5 1.4 %copy-start.3 = (bf16[8,8,96,128]{3,2,1,0:T(8,128)(2,1)S(1)}, bf16[8,8,96,128]{3,2,1,0:T(8,128)(2,1)}, u32[]{:S(2)}) copy-start(bf16[8,8,96,128]{3,2,1,0:T(8,128)(2,1)} %copy-done.2) | copy-start | bytes 4718596
  40.0 0.8 copy-start.4
  40.8 0.6 copy-start.17
  41.4 0.6 copy-start.18
  42.0 2.3 %collective-permute-start.4 = (f32[1024,128]{1,0:T(8,128)}, f32[1024,128]{1,0:T(8,128)}, u32[]{:S(2)}, u32[]{:S(2)}) collective-permute-start(f32[1024,128]{1,0:T(8,128)} %get-tuple-element.55), channel_id=1, source_target_pairs={{0,1},{1,0},{2,3},{3,2},{4,5},{5,4},{6,7},{7,6},{8,9},{9,8},{10,11... | collective-permute-start | bytes 1572872 | tf_op jit(solution)/shard_map/ppermute | solution.py:416
  44.3 1.0 %copy-start.5 = (f32[1024,128]{1,0:T(8,128)S(1)}, f32[1024,128]{1,0:T(8,128)}, u32[]{:S(2)}) copy-start(f32[1024,128]{1,0:T(8,128)} %copy-done.4) | copy-start | bytes 1572868
  46.9 0.7 copy-start.7
  47.6 9.3 %collective-permute-start.5 = (f32[512,128]{1,0:T(8,128)S(1)}, f32[512,128]{1,0:T(8,128)}, u32[]{:S(2)}, u32[]{:S(2)}) collective-permute-start(f32[512,128]{1,0:T(8,128)S(1)} %get-tuple-element.57.refs_5_), channel_id=1, source_target_pairs={{0,2},{1,3},{2,0},{3,1},{4,6},{5,7},{6,4},{7,5},{8,10},{9,11},{10,... | collective-permute-start | bytes 786440 | tf_op jit(solution)/shard_map/ppermute | solution.py:416
  49.4 5.4 %collective-permute-start.6 = (bf16[3,96,128]{2,1,0:T(8,128)(2,1)}, bf16[3,96,128]{2,1,0:T(8,128)(2,1)S(1)}, u32[]{:S(2)}, u32[]{:S(2)}) collective-permute-start(bf16[3,96,128]{2,1,0:T(8,128)(2,1)} %copy-done.18), channel_id=1, source_target_pairs={{24,0},{0,8},{8,16},{16,24},{25,1},{1,9},{9,17},{17,25},{26,2},{2,... | collective-permute-start | bytes 221192 | tf_op jit(solution)/shard_map/ppermute | solution.py:25
  50.3 4.5 %collective-permute-start.7 = (bf16[3,96,128]{2,1,0:T(8,128)(2,1)}, bf16[3,96,128]{2,1,0:T(8,128)(2,1)S(1)}, u32[]{:S(2)}, u32[]{:S(2)}) collective-permute-start(bf16[3,96,128]{2,1,0:T(8,128)(2,1)} %copy-done.17), channel_id=1, source_target_pairs={{8,0},{16,8},{24,16},{0,24},{9,1},{17,9},{25,17},{1,25},{10,2},{18... | collective-permute-start | bytes 221192 | tf_op jit(solution)/shard_map/ppermute | solution.py:25
  52.7 4.2 %copy-start.8 = (f32[512,128]{1,0:T(8,128)S(1)}, f32[512,128]{1,0:T(8,128)}, u32[]{:S(2)}) copy-start(f32[512,128]{1,0:T(8,128)} %copy-done.7) | copy-start | bytes 786436
  54.8 0.7 copy-start.11
  55.5 12.3 %copy-start.14 = (bf16[8,8,96,128]{3,2,1,0:T(8,128)(2,1)S(1)}, bf16[8,8,96,128]{3,2,1,0:T(8,128)(2,1)}, u32[]{:S(2)}) copy-start(bf16[8,8,96,128]{3,2,1,0:T(8,128)(2,1)} %copy-done.12) | copy-start | bytes 4718596
  55.5 12.3 %copy-start.16 = (bf16[288,864]{1,0:T(8,128)(2,1)S(1)}, bf16[288,864]{1,0:T(8,128)(2,1)}, u32[]{:S(2)}) copy-start(bf16[288,864]{1,0:T(8,128)(2,1)} %copy-done.15) | copy-start | bytes 1492996
  55.5 12.3 %copy-start.20 = (s32[1,16,8]{1,2,0:T(8,128)S(1)}, s32[1,16,8]{1,2,0:T(8,128)}, u32[]{:S(2)}) copy-start(s32[1,16,8]{1,2,0:T(8,128)} %param.10) | copy-start | bytes 1540
  58.5 5.7 %collective-permute-start.8 = (f32[256,128]{1,0:T(8,128)S(1)}, f32[256,128]{1,0:T(8,128)S(1)}, u32[]{:S(2)}, u32[]{:S(2)}) collective-permute-start(f32[256,128]{1,0:T(8,128)S(1)} %get-tuple-element.63.refs_2_), channel_id=1, source_target_pairs={{0,4},{1,5},{2,6},{3,7},{4,0},{5,1},{6,2},{7,3},{8,12},{9,13},{10,... | collective-permute-start | bytes 393224 | tf_op jit(solution)/shard_map/ppermute | solution.py:416
  58.6 6.9 %collective-permute-start.10 = (bf16[4,96,128]{2,1,0:T(8,128)(2,1)S(1)}, bf16[4,96,128]{2,1,0:T(8,128)(2,1)S(1)}, u32[]{:S(2)}, u32[]{:S(2)}) collective-permute-start(bf16[4,96,128]{2,1,0:T(8,128)(2,1)S(1)} %get-tuple-element.65), channel_id=1, source_target_pairs={{0,1},{1,0},{2,3},{3,2},{4,5},{5,4},{6,7},{7,6},{8,9},{9,8},{10,11... | collective-permute-start | bytes 294920 | tf_op jit(solution)/shard_map/ppermute | solution.py:33
  61.2 6.7 %collective-permute-start.11 = (bf16[4,96,128]{2,1,0:T(8,128)(2,1)S(1)}, bf16[4,96,128]{2,1,0:T(8,128)(2,1)S(1)}, u32[]{:S(2)}, u32[]{:S(2)}) collective-permute-start(bf16[4,96,128]{2,1,0:T(8,128)(2,1)S(1)} %get-tuple-element.66), channel_id=1, source_target_pairs={{1,2},{2,1},{3,4},{4,3},{5,6},{6,5},{9,10},{10,9},{11,12},{12,11},... | collective-permute-start | bytes 294920 | tf_op jit(solution)/shard_map/ppermute | solution.py:33
  64.3 10.1 %collective-permute-start.9 = (f32[256,128]{1,0:T(8,128)S(1)}, f32[256,128]{1,0:T(8,128)S(1)}, u32[]{:S(2)}, u32[]{:S(2)}) collective-permute-start(f32[256,128]{1,0:T(8,128)S(1)} %get-tuple-element.64.refs_0_), channel_id=1, source_target_pairs={{0,8},{1,9},{2,10},{3,11},{4,12},{5,13},{6,14},{7,15},{8,0},{9,1},... | collective-permute-start | bytes 393224 | tf_op jit(solution)/shard_map/ppermute | solution.py:416
  74.4 9.0 %collective-permute-start.12 = (f32[256,128]{1,0:T(8,128)S(1)}, f32[256,128]{1,0:T(8,128)S(1)}, u32[]{:S(2)}, u32[]{:S(2)}) collective-permute-start(f32[256,128]{1,0:T(8,128)S(1)} %get-tuple-element.70.refs_0_), channel_id=1, source_target_pairs={{0,16},{1,17},{2,18},{3,19},{4,20},{5,21},{6,22},{7,23},{8,24},{9,... | collective-permute-start | bytes 393224 | tf_op jit(solution)/shard_map/ppermute | solution.py:416
  83.5 3.2 %collective-permute-start.13 = (bf16[256,128]{1,0:T(8,128)(2,1)S(1)}, bf16[256,128]{1,0:T(8,128)(2,1)S(1)}, u32[]{:S(2)}, u32[]{:S(2)}) collective-permute-start(bf16[256,128]{1,0:T(8,128)(2,1)S(1)} %get-tuple-element.73.refs_1_), channel_id=1, source_target_pairs={{0,4},{1,5},{2,6},{3,7},{4,0},{5,1},{6,2},{7,3},{8,12},{9,13},{10,... | collective-permute-start | bytes 196616 | tf_op jit(solution)/shard_map/ppermute | solution.py:416
  86.7 3.9 %collective-permute-start.14 = (bf16[512,128]{1,0:T(8,128)(2,1)S(1)}, bf16[512,128]{1,0:T(8,128)(2,1)S(1)}, u32[]{:S(2)}, u32[]{:S(2)}) collective-permute-start(bf16[512,128]{1,0:T(8,128)(2,1)S(1)} %get-tuple-element.81.refs_1_), channel_id=1, source_target_pairs={{0,2},{1,3},{2,0},{3,1},{4,6},{5,7},{6,4},{7,5},{8,10},{9,11},{10,... | collective-permute-start | bytes 393224 | tf_op jit(solution)/shard_map/ppermute | solution.py:416
  91.2 3.9 %collective-permute-start.15 = (bf16[1024,128]{1,0:T(8,128)(2,1)S(1)}, bf16[1024,128]{1,0:T(8,128)(2,1)S(1)}, u32[]{:S(2)}, u32[]{:S(2)}) collective-permute-start(bf16[1024,128]{1,0:T(8,128)(2,1)S(1)} %get-tuple-element.83.refs_1_), channel_id=1, source_target_pairs={{0,1},{1,0},{2,3},{3,2},{4,5},{5,4},{6,7},{7,6},{8,9},{9,8},{10,11... | collective-permute-start | bytes 786440 | tf_op jit(solution)/shard_map/ppermute | solution.py:416
